TPU v7x, 512 devices: a whole 4x8x8 slice. The times are simulated.
512 devices in a mesh: seq: 64 (over y, z), chan: 8 (over x, core).
Axes of the slice: x: 4, y: 8, z: 8, core: 2. Of those that a mesh axis runs over, the one named last changes fastest.
Arguments:
- qkv: bfloat16 [3, 24576, 8192], P(None, 'seq', 'chan'), may hold values from -6 to 6
- feat_taps: float32 [3, 7, 8192], P(None, None, 'chan'), may hold values from -2.5 to 2.5
- long_filter: bfloat16 [128, 512], P(None, 'chan'), may hold values from -0.5 to 0.5
- skip_gain: float32 [8192], P('chan'), may hold values from -6 to 6
- out_weight: bfloat16 [8192, 4096], P('chan', 'seq'), may hold values from -0.1875 to 0.1875
Outputs:
- mixed: bfloat16 [24576, 4096], P('seq', 'chan')
All inputs are finite; a program needn't handle non-finite values.
Results may differ from a plain program's by a relative error of at most 0.017.
Values may be sent and summed in bfloat16 or wider, within the bound.
A program may use at most 64 MiB of HBM per device.

v0:
```python
import jax
import jax.numpy as jnp
from jax import lax
from jax.sharding import PartitionSpec as P

GROUP = 16


def from_behind(array, axis, by):
    length = lax.axis_size(axis)
    pairs = [(i, i + by) for i in range(length) if 0 <= i + by < length]
    return lax.ppermute(array, axis, pairs)


def featurize(extended, taps, rows):
    count = taps.shape[1]
    total = jnp.zeros((3, rows, extended.shape[2]), jnp.float32)
    for j in range(count):
        lower = count - 1 - j
        total = total + taps[:, j, None, :] * extended[:, lower : lower + rows, :].astype(
            jnp.float32
        )
    return total


def toeplitz(long_filter):
    span = long_filter.shape[0]
    groups_here = long_filter.shape[1]
    flipped = long_filter[::-1]
    padded = jnp.concatenate([flipped, jnp.zeros((span, groups_here), long_filter.dtype)], axis=0)
    tiled = jnp.tile(padded, (span, 1))
    return tiled[: span * (2 * span - 1)].reshape(span, 2 * span - 1, groups_here)


def local(qkv, feat_taps, long_filter, skip_gain, out_weight):
    rows = qkv.shape[1]
    width = qkv.shape[2]
    span = long_filter.shape[0]
    ftap_count = feat_taps.shape[1]
    rim = from_behind(qkv[:, rows - (ftap_count - 1) :, :], "seq", 1)
    feats = featurize(jnp.concatenate([rim, qkv], axis=1), feat_taps, rows)
    query_feat = feats[0]
    mixed_in = (feats[1] * feats[2]).astype(jnp.bfloat16)
    tail = from_behind(mixed_in[rows - (span - 1) :], "seq", 1)
    extended_u = jnp.concatenate([tail, mixed_in], axis=0)
    mixed_in = extended_u[span - 1 :]
    matrix = toeplitz(long_filter)
    grouped = extended_u.reshape(rows + span - 1, width // GROUP, GROUP)
    blocks = rows // span
    windows = jnp.stack([grouped[b * span : b * span + 2 * span - 1] for b in range(blocks)])
    conv = jnp.einsum("rsg,bsge->brge", matrix, windows, preferred_element_type=jnp.float32)
    z_field = conv.reshape(rows, width) + skip_gain * mixed_in.astype(jnp.float32)
    y_field = (query_feat * z_field).astype(jnp.bfloat16)
    partial_value = jnp.dot(
        y_field,
        lax.all_gather(out_weight, "seq", axis=1, tiled=True),
        preferred_element_type=jnp.float32,
    )
    summed = lax.psum_scatter(
        partial_value.astype(jnp.bfloat16), "chan", scatter_dimension=1, tiled=True
    )
    return summed


def solution(mesh):
    return jax.shard_map(
        local,
        mesh=mesh,
        in_specs=(
            P(None, "seq", "chan"),
            P(None, None, "chan"),
            P(None, "chan"),
            P("chan"),
            P("chan", "seq"),
        ),
        out_specs=P("seq", "chan"),
        check_vma=False,
    )
```

profile of v0, /device:TPU:8, one launch (start us, length us, event | category | flops | bytes accessed | tf_op | source)
XLA Modules:
  0.0 170.7 jit_solution(15158486921916934913)
XLA Ops:
  6.5 0.7 all-gather.2.cloned.1.call-update
  7.3 0.8 slice.78
  8.1 4.3 %collective-permute-start = (bf16[3,6,1024]{2,1,0:T(8,128)(2,1)S(1)}, bf16[3,6,1024]{2,1,0:T(8,128)(2,1)S(1)}, u32[]{:S(2)}, u32[]{:S(2)}) collective-permute-start(bf16[3,6,1024]{2,1,0:T(8,128)(2,1)S(1)} %slice.78), channel_id=1, source_target_pairs={{0,8},{8,16},{16,24},{24,32},{32,40},{40,48},{48,56},{56,64},{64,7... | collective-permute-start | bytes 110600 | tf_op jit(solution)/shard_map/ppermute | solution.py:12
  12.4 1.5 fusion.25
  14.0 3.0 %copy.13 = bf16[3,384,1024]{1,2,0:T(8,128)(2,1)S(1)} copy(bf16[3,384,1024]{2,1,0:T(8,128)(2,1)} %param.5) | data formatting | bytes 4718592 | tf_op args[0]
  17.0 0.1 rev.3
  17.1 0.3 tile.4
  17.4 2.6 %copy.25 = bf16[8,8,128,256]{3,1,2,0:T(8,128)(2,1)S(1)} copy(bf16[8,8,128,256]{3,2,1,0:T(8,128)(2,1)S(1)} %bitcast.56) | data formatting | bytes 8388608
  20.0 2.2 %slice.115 = bf16[32640,64]{0,1:T(8,128)(2,1)} slice(bf16[32768,64]{0,1:T(8,128)(2,1)S(1)} %bitcast.57), slice={[0:32640], [0:64]} | slice | bytes 8355840 | tf_op jit(solution)/shard_map/slice | solution.py:32
  22.2 15.8 %reshape.27 = bf16[128,255,64,1]{1,0,2,3:T(8,128)(2,1)} reshape(bf16[32640,64]{0,1:T(8,128)(2,1)} %slice.115) | data formatting | bytes 8355840 | tf_op jit(solution)/shard_map/reshape | solution.py:32
  38.1 0.4 copy.14
  38.5 9.6 %multiply_add_fusion = f32[3,384,1024]{1,2,0:T(8,128)S(1)} fusion(bf16[3,384,1024]{1,2,0:T(8,128)(2,1)S(1)} %copy.13, bf16[3,6,1024]{1,2,0:T(8,128)(2,1)S(1)} %copy.14, f32[3,1024]{1,0:T(4,128)S(1)} %get-tuple-element.14, f32[3,1024]{1,0:T(4,128)S(1)} %get-tuple-element.15, f32[3,1024]{1,0:T(4,128)S(1)} %get-tuple-element.16, ...), kind=kLoop, calls=%fused_computation.6 | loop fusion | flops 44826624 | bytes 7200768 | tf_op jit(solution)/shard_map/add | solution.py:20
  48.1 0.1 fusion.9
  48.2 0.1 slice_bitcast_fusion.1
  48.4 4.7 %collective-permute-start.1 = (bf16[127,1024]{0,1:T(8,128)(2,1)S(1)}, bf16[127,1024]{0,1:T(8,128)(2,1)S(1)}, u32[]{:S(2)}, u32[]{:S(2)}) collective-permute-start(bf16[127,1024]{0,1:T(8,128)(2,1)S(1)} %slice_bitcast_fusion.1), channel_id=1, source_target_pairs={{0,8},{8,16},{16,24},{24,32},{32,40},{40,48},{48,56},{56,64},{64,7... | collective-permute-start | bytes 780296 | tf_op jit(solution)/shard_map/ppermute | solution.py:12
  53.1 0.1 fusion.27
  53.3 0.4 fusion.24
  53.7 10.1 %collective-permute-done.1 = bf16[127,1024]{0,1:T(8,128)(2,1)S(1)} collective-permute-done((bf16[127,1024]{0,1:T(8,128)(2,1)S(1)}, bf16[127,1024]{0,1:T(8,128)(2,1)S(1)}, u32[]{:S(2)}, u32[]{:S(2)}) %collective-permute-start.1) | collective-permute-done | bytes 260128 | tf_op jit(solution)/shard_map/ppermute | solution.py:12
  63.8 0.2 pad_maximum_fusion.1
  64.1 1.5 fusion.15
  65.6 0.9 copy.16
  66.5 48.8 %all-gather.2.cloned.1.call-done = bf16[1024,4096]{0,1:T(8,128)(2,1)} async-done(((bf16[1024,64]{0,1:T(8,128)(2,1)}), bf16[1024,4096]{0,1:T(8,128)(2,1)}) %all-gather.2.cloned.1.call-update) | async-done | bytes 8388624 | tf_op jit(solution)/shard_map/all_gather | solution.py:56
  115.3 9.3 %convolution_convert_fusion = bf16[384,4096]{1,0:T(8,128)(2,1)} fusion(bf16[1024,4096]{0,1:T(8,128)(2,1)} %all-gather.2.cloned.1.call-done, f32[128,8,3,128]{3,2,1,0:T(4,128)S(1)} %bitcast.61, f32[3,384,1024]{1,2,0:T(8,128)} %copy-done, f32[1024]{0:T(1024)S(1)} %copy-done.3, bf16[1,384,1024]{1,2,0:T(8,128)(2,1)S(1)} %fusion.9), kind=kOutput, calls=%fused_computation.5 | convolution fusion | flops 3224764416 | bytes 15470592 | tf_op jit(solution)/shard_map/dot_general | solution.py:54
  124.6 39.3 %reduce-scatter.2.cloned.1.call-done = bf16[384,512]{1,0:T(8,128)(2,1)} async-done(((bf16[384,4096]{1,0:T(8,128)(2,1)}), bf16[384,512]{1,0:T(8,128)(2,1)}) %reduce-scatter.2.cloned.1.call-update) | async-done | bytes 393232 | tf_op jit(solution)/shard_map/reduce_scatter | solution.py:59
  (17 shorter events, 0.1 us)
Async XLA Ops:
  6.5 10.5 %copy-start.2 = (bf16[128,64]{0,1:T(8,128)(2,1)S(1)}, bf16[128,64]{0,1:T(8,128)(2,1)}, u32[]{:S(2)}) copy-start(bf16[128,64]{0,1:T(8,128)(2,1)} %param.7) | copy-start | bytes 49156
  6.5 108.8 %all-gather.2.cloned.1.call-start = ((), (), s32[]{:S(2)}) async-start(), calls=%async_computation.1 | async-start | bytes 8519680 | tf_op jit(solution)/shard_map/all_gather | solution.py:56
  7.3 156.6 %reduce-scatter.2.cloned.1.call-start = ((), (), s32[]{:S(2)}) async-start(), calls=%async_computation.2 | async-start | bytes 3538944 | tf_op jit(solution)/shard_map/reduce_scatter | solution.py:59
  8.1 29.9 %collective-permute-start = (bf16[3,6,1024]{2,1,0:T(8,128)(2,1)S(1)}, bf16[3,6,1024]{2,1,0:T(8,128)(2,1)S(1)}, u32[]{:S(2)}, u32[]{:S(2)}) collective-permute-start(bf16[3,6,1024]{2,1,0:T(8,128)(2,1)S(1)} %slice.78), channel_id=1, source_target_pairs={{0,8},{8,16},{16,24},{24,32},{32,40},{40,48},{48,56},{56,64},{64,7... | collective-permute-start | bytes 110600 | tf_op jit(solution)/shard_map/ppermute | solution.py:12
  48.1 5.6 %copy-start = (f32[3,384,1024]{1,2,0:T(8,128)}, f32[3,384,1024]{1,2,0:T(8,128)S(1)}, u32[]{:S(2)}) copy-start(f32[3,384,1024]{1,2,0:T(8,128)S(1)} %multiply_add_fusion) | copy-start | bytes 14155780
  48.2 15.8 %copy-start.1 = (bf16[128,255,64,1]{1,0,2,3:T(8,128)(2,1)S(1)}, bf16[128,255,64,1]{1,0,2,3:T(8,128)(2,1)}, u32[]{:S(2)}) copy-start(bf16[128,255,64,1]{1,0,2,3:T(8,128)(2,1)} %reshape.27) | copy-start | bytes 12533764
  48.4 15.4 %collective-permute-start.1 = (bf16[127,1024]{0,1:T(8,128)(2,1)S(1)}, bf16[127,1024]{0,1:T(8,128)(2,1)S(1)}, u32[]{:S(2)}, u32[]{:S(2)}) collective-permute-start(bf16[127,1024]{0,1:T(8,128)(2,1)S(1)} %slice_bitcast_fusion.1), channel_id=1, source_target_pairs={{0,8},{8,16},{16,24},{24,32},{32,40},{40,48},{48,56},{56,64},{64,7... | collective-permute-start | bytes 780296 | tf_op jit(solution)/shard_map/ppermute | solution.py:12
  64.1 51.2 %copy-start.3 = (f32[1024]{0:T(1024)S(1)}, f32[1024]{0:T(1024)}, u32[]{:S(2)}) copy-start(f32[1024]{0:T(1024)} %param.8) | copy-start | bytes 12292
Sparse Core Ops, SparseCore 0:
  10.4 104.8 all-gather.1
  124.7 39.1 reduce-scatter.1
where the time goes:
time: 171 us
  waiting for transfers between devices  98.9 us (58%)
  local copies, waits for them, and re-layouts  28.3 us (17%)
  between operations  13.6 us (8%)
  matrix products  10.8 us (6%)
  other arithmetic  10.1 us (6%)
  starting transfers between devices  9.04 us (5%)
    all_gather x1, waiting for transfers between devices, local(): lax.all_gather(out_weight, 'seq', axis=1, tiled=True)  48.8 us
    reduce_scatter x1, waiting for transfers between devices, local(): lax.psum_scatter(partial_value.astype(jnp.bfloat16), 'chan', scatter_dime...  39.3 us
    reshape x1, local copies, waits for them, and re-layouts, toeplitz(): tiled[:span * (2 * span - 1)].reshape(span, 2 * span - 1, groups_here)  15.8 us
    ppermute x2, waiting for transfers between devices, from_behind(): return lax.ppermute(array, axis, pairs)  10.1 us
    add x1, other arithmetic, featurize(): total + taps[:, j, None, :] * extended[:, lower:lower + rows, :].astype(j...  9.58 us
    dot_general x1, matrix products, local(): jnp.dot(y_field, lax.all_gather(out_weight, 'seq', axis=1, tiled=True), p...  9.28 us
    ppermute x2, starting transfers between devices, from_behind(): return lax.ppermute(array, axis, pairs)  9 us
    unnamed x14, local copies, waits for them, and re-layouts  5.66 us
  transfers between devices with their start and end apart: 4, of which 3 were waited for; matrix products, arithmetic and copies ran while one was open for 23% of the time, Pallas kernels for 0%

commit v1 on v0

v1 whole, which is shorter than its diff:
```python
import jax
import jax.numpy as jnp
from jax import lax
from jax.experimental import pallas as pl
from jax.experimental.pallas import tpu as pltpu
from jax.sharding import PartitionSpec as P

MESH = pl.DeviceIdType.MESH
F32 = jnp.float32
BF16 = jnp.bfloat16

RING = 8
GROUP = 16
SPAN = 128
FTAPS = 7
ROWS = 384
WIDTH = 1024
BLOCKS = ROWS // SPAN
LANES = 128
STRIPS = WIDTH // LANES
PIECE = 32
HALO = 16
PAD = 8

OFF = (0, 1, -1, 2, -2, 3, -3, 4)
SLOT = {off: slot for slot, off in enumerate(OFF)}
PACKS = ((0, 1), (1, 3), (3, 5), (5, 7), (7, 8))
FAR_UP = (0, 1, 4)
ROUNDS = ((1, 2), (3, 4), (5, 6), (0, 7))


def origin(direction, step):
    return SLOT[4 if step == 4 else -direction * step]


def kernel(
    qkv_ref, taps_ref, filt_ref, skip_ref, w_ref, out_ref,
    w_all, qkv_v, halo, ext, ut, qt, skt, hf, yt,
    ta, sa, qa, tb, sb, qb, ra, rb, fin,
    load_sem, own_sem, halo_sem, tail_sem,
    s1, r1, s2, r2, as1, ar1, as2, ar2, bs1, br1, bs2, br2,
):
    s = lax.axis_index("seq")
    c = lax.axis_index("chan")
    y = lax.div(s, RING)
    z = lax.rem(s, RING)
    x = lax.div(c, 2)
    p = lax.rem(c, 2)

    def y_at(d):
        return {"seq": lax.rem(y + d + RING, RING) * RING + z}

    def z_at(d):
        return {"seq": y * RING + lax.rem(z + d + RING, RING)}

    def seq_at(d):
        return {"seq": lax.rem(s + d + RING * RING, RING * RING)}

    sibling = {"chan": c + 1 - 2 * p}
    minor_at = (z_at, y_at)
    major_at = (y_at, z_at)
    started = []

    def remote(src, dst, send, recv, to):
        return pltpu.make_async_remote_copy(
            src_ref=src, dst_ref=dst, send_sem=send, recv_sem=recv, device_id=to, device_id_type=MESH
        )

    def go(copy):
        copy.start()
        started.append(copy)

    loads = [
        pltpu.make_async_copy(qkv_ref.at[i], qkv_v.at[i], load_sem.at[i]) for i in (1, 2, 0)
    ]
    own = [
        pltpu.make_async_copy(
            w_ref.at[PIECE * kind : PIECE * (kind + 1)], w_all.at[kind, 0, 0], own_sem.at[kind]
        )
        for kind in range(2)
    ]
    for copy in loads + own:
        copy.start()

    barrier = pltpu.get_barrier_semaphore()
    greeted = [{"chan": lax.rem(c + d, 8)} for d in range(1, 8)]
    greeted += [z_at(1), z_at(-1), y_at(1), y_at(-1), seq_at(1), seq_at(-1)]
    for to in greeted:
        pl.semaphore_signal(barrier, inc=1, device_id=to, device_id_type=MESH)
    pl.semaphore_wait(barrier, len(greeted))

    def first(kind, direction, step):
        lane = 0 if direction == 1 else 1
        into = origin(direction, step)
        if step == 1:
            src, dst = w_ref.at[PIECE * kind : PIECE * (kind + 1)], w_all.at[kind, 0, into]
        elif step < 4:
            src, dst = w_all.at[kind, 0, origin(direction, step - 1)], w_all.at[kind, 0, into]
        else:
            half = pl.ds(lane * (PIECE // 2), PIECE // 2)
            src = w_all.at[kind, 0, origin(direction, 3), half]
            dst = w_all.at[kind, 0, into, half]
        at = kind, lane, step - 1
        return remote(src, dst, s1.at[at], r1.at[at], minor_at[kind](direction))

    def second(kind, direction, step, pack):
        lane = 0 if direction == 1 else 1
        lo, hi = PACKS[pack]
        into = origin(direction, step)
        if step == 1 and pack == 0:
            src, dst = w_ref.at[PIECE * kind : PIECE * (kind + 1)], w_all.at[kind, into, 0]
        else:
            came = 0 if step == 1 else origin(direction, step - 1)
            src = w_all.at[kind, came, pl.ds(lo, hi - lo)]
            dst = w_all.at[kind, into, pl.ds(lo, hi - lo)]
        at = kind, lane, step - 1, pack
        return remote(src, dst, s2.at[at], r2.at[at], major_at[kind](direction))

    def lanes_of(step, pack):
        if step < 4:
            return (1, -1)
        return (1,) if pack in FAR_UP else (-1,)

    def first_arrives(step):
        for kind in range(2):
            for direction in (1, -1):
                first(kind, direction, step).wait_recv()
                if step < 4:
                    go(first(kind, direction, step + 1))
        for kind in range(2):
            for direction in (1, -1):
                go(second(kind, direction, 1, step))

    def second_arrives(step, pack):
        for kind in range(2):
            for direction in lanes_of(step, pack):
                second(kind, direction, step, pack).wait_recv()
                if step < 4 and direction in lanes_of(step + 1, pack):
                    go(second(kind, direction, step + 1, pack))

    events = [(2.2 * k, first_arrives, (k,)) for k in range(1, 5)]
    events += [
        (2.6 + 10.5 * (k - 1) + 2.4 * g, second_arrives, (k, g)) for k in range(1, 5) for g in range(5)
    ]
    events.sort(key=lambda e: e[0])
    events = [(at, fn, args) for at, fn, args in events]
    clock = [0.0]
    seen = set()

    def take_event():
        at, fn, args = events.pop(0)
        fn(*args)
        if fn is second_arrives:
            seen.add(args)
        else:
            seen.add(args[0])
        clock[0] = max(clock[0], at)

    def work(cost, fn, *args):
        while events and events[0][0] <= clock[0]:
            take_event()
        fn(*args)
        clock[0] += cost

    def need(step):
        wanted = {(step, g) for g in range(5)}
        while not wanted <= seen:
            take_event()

    halo_copy = remote(
        qkv_ref.at[:, ROWS - HALO : ROWS], halo, halo_sem.at[0], halo_sem.at[1], seq_at(1)
    )
    go(halo_copy)
    for kind in range(2):
        for direction in (1, -1):
            go(first(kind, direction, 1))
    for kind in range(2):
        for direction in (1, -1):
            go(second(kind, direction, 1, 0))

    def widen(strip):
        at = pl.ds(pl.multiple_of(strip * LANES, LANES), LANES)
        for i in range(3):
            ext[i, strip, PAD:, :] = qkv_v[i, :, at].astype(F32)

    def widen_halo(strip):
        at = pl.ds(pl.multiple_of(strip * LANES, LANES), LANES)
        for i in range(3):
            before = halo[i, :, at].astype(F32)[HALO - PAD :]
            ext[i, strip, :PAD, :] = jnp.where(s == 0, 0.0, before)

    def feature(i, block, strip, at):
        total = None
        for j in range(FTAPS):
            term = taps_ref[i, j : j + 1, at] * ext[i, strip, pl.ds(PAD + SPAN * block - j, SPAN), :]
            total = term if total is None else total + term
        return total

    def features(block, strips):
        def body(strip, carry):
            at = pl.ds(pl.multiple_of(strip * LANES, LANES), LANES)
            u = (feature(1, block, strip, at) * feature(2, block, strip, at)).astype(BF16).astype(F32)
            ut[block + 1, at, :] = u.T.astype(BF16)
            qt[block, at, :] = feature(0, block, strip, at).T
            return carry

        lax.fori_loop(strips[0], strips[1], body, 0)

    def widen_all():
        for copy in loads:
            copy.wait()

        def body(strip, carry):
            widen(strip)
            return carry

        lax.fori_loop(0, STRIPS, body, 0)
        hf[...] = filt_ref[...].astype(F32)

    def halo_arrives():
        halo_copy.wait_recv()

        def body(strip, carry):
            widen_halo(strip)
            at = pl.ds(pl.multiple_of(strip * LANES, LANES), LANES)
            skt[at, :] = jnp.broadcast_to(skip_ref[:, at], (LANES, LANES)).T
            return carry

        lax.fori_loop(0, STRIPS, body, 0)

    tail_copy = remote(ut.at[BLOCKS], ut.at[0], tail_sem.at[0], tail_sem.at[1], seq_at(1))

    def send_tail():
        go(tail_copy)

    def tail_arrives():
        tail_copy.wait_recv()

        @pl.when(s == 0)
        def clear():
            ut[0] = jnp.zeros((WIDTH, SPAN), BF16)

    def conv(lo, hi):
        def body(g, carry):
            row = lax.broadcasted_iota(jnp.int32, (SPAN, SPAN), 0)
            col = lax.broadcasted_iota(jnp.int32, (SPAN, SPAN), 1)
            taps = jnp.broadcast_to(hf[pl.ds(g, 1), :], (SPAN, SPAN))
            ring = pltpu.roll(taps, 0, 1, stride=1, stride_axis=0)
            here = jnp.where(row <= col, ring, 0.0)
            before = jnp.where(row > col, ring, 0.0)
            matrix = jnp.concatenate([before, here], axis=0).astype(BF16)
            at = pl.ds(pl.multiple_of(g * GROUP, GROUP), GROUP)
            parts = [ut[b, at, :] for b in range(BLOCKS + 1)]
            window = jnp.concatenate(
                [jnp.concatenate(parts[:BLOCKS], axis=0), jnp.concatenate(parts[1:], axis=0)], axis=1
            )
            mixed = jnp.dot(window, matrix, preferred_element_type=F32)
            for b in range(BLOCKS):
                field = mixed[GROUP * b : GROUP * (b + 1)] + skt[at, :] * parts[b + 1].astype(F32)
                yt[at, SPAN * b : SPAN * (b + 1)] = (qt[b, at, :] * field).astype(BF16)
            return carry

        lax.fori_loop(lo, hi, body, 0, unroll=4)

    def project(pieces):
        rows = jnp.concatenate(pieces, axis=0) if len(pieces) > 1 else pieces[0]
        return jnp.dot(rows, yt[...], preferred_element_type=F32)

    def four(kind, major, half):
        return w_all[kind, major, pl.ds(4 * half, 4)].reshape(4 * PIECE, WIDTH)

    def a_swap(slot):
        return remote(ta.at[slot], sa.at[slot], as1.at[slot], ar1.at[slot], sibling)

    def a_first(slots):
        got = project([four(0, m, 1 - p) for m in slots]).astype(BF16)
        for i, m in enumerate(slots):
            ta[m] = got[4 * PIECE * i : 4 * PIECE * (i + 1)]
            go(a_swap(m))

    def target(slot):
        return lax.rem(y + OFF[slot] + RING, RING)

    def deliver(src, dst, send, recv, to):
        copy = remote(src, dst, send, recv, {"chan": to})

        @pl.when(to == c)
        def keep():
            pltpu.make_async_copy(src, dst, recv).start()

        @pl.when(to != c)
        def post():
            copy.start()

        return to, copy

    delivered = []

    def a_second(slots):
        got = project([four(0, m, p) for m in slots])
        for i, m in enumerate(slots):
            a_swap(m).wait_recv()
            qa[m] = (got[4 * PIECE * i : 4 * PIECE * (i + 1)] + sa[m].astype(F32)).astype(BF16)
            delivered.append(deliver(qa.at[m], ra.at[x, p], as2.at[m], ar2.at[x, p], target(m)))

    def b_swap(turn):
        return remote(tb.at[turn], sb.at[turn], bs1.at[turn], br1.at[turn], sibling)

    def b_rows(turn, half):
        low, high = ROUNDS[turn]
        return w_all[1, low + half * (high - low)].reshape(RING * PIECE, WIDTH)

    def b_first(turn):
        tb[turn] = project([b_rows(turn, 1 - p)]).astype(BF16)
        go(b_swap(turn))

    def b_second(turn):
        got = project([b_rows(turn, p)])
        b_swap(turn).wait_recv()
        qb[turn] = (got + sb[turn].astype(F32)).astype(BF16)
        for m in range(RING):
            delivered.append(
                deliver(
                    qb.at[turn, PIECE * m : PIECE * (m + 1)], rb.at[turn, x, p],
                    bs2.at[turn, m], br2.at[turn, x, p], target(m),
                )
            )

    def own_wait():
        for copy in own:
            copy.wait()

    work(1.0, widen_all)
    for lo in (0, 4):
        work(1.0, features, BLOCKS - 1, (lo, lo + 4))
    work(0.1, send_tail)
    for lo in (0, 4):
        work(1.0, features, 1, (lo, lo + 4))
    work(0.3, halo_arrives)
    for lo in (0, 4):
        work(1.0, features, 0, (lo, lo + 4))
    work(0.1, tail_arrives)
    for lo in range(0, 64, 16):
        work(1.2, conv, lo, lo + 16)
    work(0.1, own_wait)
    need(1)
    work(0.4, a_first, (0,))
    work(0.8, a_first, (1, 2))
    work(0.8, b_first, 0)
    work(0.4, a_second, (0,))
    work(0.8, a_second, (1, 2))
    work(0.8, b_second, 0)
    need(2)
    work(0.8, a_first, (3, 4))
    work(0.8, b_first, 1)
    work(0.8, a_second, (3, 4))
    work(0.8, b_second, 1)
    need(3)
    work(0.8, a_first, (5, 6))
    work(0.8, b_first, 2)
    work(0.8, a_second, (5, 6))
    work(0.8, b_second, 2)
    need(4)
    work(0.4, a_first, (7,))
    work(0.8, b_first, 3)
    work(0.4, a_second, (7,))
    work(0.8, b_second, 3)

    def place(kind, slot, rows):
        at = lax.rem(z + OFF[slot] + RING, RING) * (2 * PIECE) + kind * PIECE
        fin[pl.ds(pl.multiple_of(at, PIECE), PIECE), :] = rows

    def total(ref, half, lead=()):
        found = None
        for chip in range(4):
            term = ref[lead + (chip, half)].astype(F32)
            found = term if found is None else found + term
        return found

    for half in range(2):
        for chip in range(4):
            remote(ra.at[chip, half], ra.at[chip, half], as2.at[0], ar2.at[chip, half], sibling).wait_recv()
    for half in range(2):
        found = total(ra, half)
        for i in range(4):
            place(0, 4 * half + i, found[PIECE * i : PIECE * (i + 1)])
    for turn in range(4):
        for half in range(2):
            for chip in range(4):
                here = rb.at[turn, chip, half]
                remote(here, here, bs2.at[turn, 0], br2.at[turn, chip, half], sibling).wait_recv()
            place(1, ROUNDS[turn][half], total(rb, half, (turn,)))
    for a in range(BLOCKS):
        for n in range(4):
            tile = fin[LANES * n : LANES * (n + 1), SPAN * a : SPAN * (a + 1)]
            out_ref[SPAN * a : SPAN * (a + 1), LANES * n : LANES * (n + 1)] = tile.T.astype(BF16)

    for copy in started:
        copy.wait_send()
    for to, copy in delivered:
        @pl.when(to != c)
        def drain(copy=copy):
            copy.wait_send()


def local(qkv, feat_taps, long_filter, skip_gain, out_weight):
    vmem = pl.BlockSpec(memory_space=pltpu.VMEM)
    anywhere = pl.BlockSpec(memory_space=pl.ANY)
    dma = pltpu.SemaphoreType.DMA
    half_piece = (4 * PIECE, ROWS)
    return pl.pallas_call(
        kernel,
        out_shape=jax.ShapeDtypeStruct((ROWS, 512), BF16),
        in_specs=[anywhere, vmem, vmem, vmem, anywhere],
        out_specs=vmem,
        scratch_shapes=[
            pltpu.VMEM((2, RING, RING, PIECE, WIDTH), BF16),
            pltpu.VMEM((3, ROWS, WIDTH), BF16),
            pltpu.VMEM((3, HALO, WIDTH), BF16),
            pltpu.VMEM((3, STRIPS, PAD + ROWS, LANES), F32),
            pltpu.VMEM((BLOCKS + 1, WIDTH, SPAN), BF16),
            pltpu.VMEM((BLOCKS, WIDTH, SPAN), F32),
            pltpu.VMEM((WIDTH, SPAN), F32),
            pltpu.VMEM((WIDTH // GROUP, SPAN), F32),
            pltpu.VMEM((WIDTH, ROWS), BF16),
            pltpu.VMEM((RING,) + half_piece, BF16),
            pltpu.VMEM((RING,) + half_piece, BF16),
            pltpu.VMEM((RING,) + half_piece, BF16),
            pltpu.VMEM((4, RING * PIECE, ROWS), BF16),
            pltpu.VMEM((4, RING * PIECE, ROWS), BF16),
            pltpu.VMEM((4, RING * PIECE, ROWS), BF16),
            pltpu.VMEM((4, 2) + half_piece, BF16),
            pltpu.VMEM((4, 4, 2, PIECE, ROWS), BF16),
            pltpu.VMEM((512, ROWS), F32),
            dma((3,)), dma((2,)), dma((2,)), dma((2,)),
            dma((2, 2, 4)), dma((2, 2, 4)),
            dma((2, 2, 4, 5)), dma((2, 2, 4, 5)),
            dma((RING,)), dma((RING,)), dma((RING,)), dma((4, 2)),
            dma((4,)), dma((4,)), dma((4, RING)), dma((4, 4, 2)),
        ],
        compiler_params=pltpu.CompilerParams(
            collective_id=0, has_side_effects=True, vmem_limit_bytes=56 * 2**20
        ),
    )(qkv, feat_taps, long_filter.T, skip_gain.reshape(1, WIDTH), out_weight.T)


def solution(mesh):
    return jax.shard_map(
        local,
        mesh=mesh,
        in_specs=(
            P(None, "seq", "chan"),
            P(None, None, "chan"),
            P(None, "chan"),
            P("chan"),
            P("chan", "seq"),
        ),
        out_specs=P("seq", "chan"),
        check_vma=False,
    )
```

time: 171 us -> 85.9 us (0.50)
  the two profiles are of different devices: /device:TPU:8 before, /device:TPU:4 now
where the time goes in v1:
time: 85.9 us; the launch traced here: 85.7 us
  Pallas kernels  83.9 us (98%)
  local copies, waits for them, and re-layouts  1.77 us (2%)
    pallas_call x1, Pallas kernels, local(): pl.pallas_call(kernel, out_shape=jax.ShapeDtypeStruct((ROWS, 512), BF16),...  83.9 us
    unnamed x1, local copies, waits for them, and re-layouts  1.77 us

profile of v1, /device:TPU:4, one launch (start us, length us, event | category | flops | bytes accessed | tf_op | source)
XLA Modules:
  0.0 85.7 jit_solution(5042896669334272088)
XLA Ops:
  0.0 83.9 %shard_map.55 = bf16[384,512]{1,0:T(8,128)(2,1)} custom-call(bf16[3,384,1024]{2,1,0:T(8,128)(2,1)} %qkv_ref.1, f32[3,7,1024]{2,1,0:T(8,128)} %taps_ref.1, bf16[64,128]{1,0:T(8,128)(2,1)} %bitcast.4, f32[1,1024]{1,0:T(1,128)} %bitcast.5, bf16[64,1024]{1,0:T(8,128)(2,1)} %bitcast.3), custom_call_target="tpu_custom_call" | custom-call | tf_op jit(solution)/shard_map/pallas_call | solution.py:411
  84.0 1.8 %copy.7 = bf16[384,512]{1,0:T(8,128)(2,1)} copy(bf16[384,512]{1,0:T(8,128)(2,1)} %shard_map.55) | data formatting | bytes 786432

commit v2 on v1

--- a/solution.py
+++ b/solution.py
@@ -22,11 +22,13 @@
 HALO = 16
 PAD = 8
 
-OFF = (0, 1, -1, 2, -2, 3, -3, 4)
+OFF = (1, -1, 2, -2, 3, -3, 4, 0)
 SLOT = {off: slot for slot, off in enumerate(OFF)}
-PACKS = ((0, 1), (1, 3), (3, 5), (5, 7), (7, 8))
+PACKS = ((7, 8), (0, 2), (2, 4), (4, 6), (6, 7))
 FAR_UP = (0, 1, 4)
-ROUNDS = ((1, 2), (3, 4), (5, 6), (0, 7))
+OWN = SLOT[0]
+FAR = SLOT[4]
+PAIRS = 3
 
 
 def origin(direction, step):
@@ -34,11 +36,12 @@
 
 
 def kernel(
-    qkv_ref, taps_ref, filt_ref, skip_ref, w_ref, out_ref,
+    qkv_ref, taps_hbm, filt_hbm, skip_hbm, w_ref, out_ref,
+    taps_ref, filt_ref, skip_ref,
     w_all, qkv_v, halo, ext, ut, qt, skt, hf, yt,
-    ta, sa, qa, tb, sb, qb, ra, rb, fin,
+    ta, sa, qa, tb, sb, qb, tc, sc, qc, ra, rb, rc, fin,
     load_sem, own_sem, halo_sem, tail_sem,
-    s1, r1, s2, r2, as1, ar1, as2, ar2, bs1, br1, bs2, br2,
+    s1, r1, s2, r2, as1, ar1, as2, ar2, bs1, br1, bs2, br2, cs1, cr1, cs2, cr2,
 ):
     s = lax.axis_index("seq")
     c = lax.axis_index("chan")
@@ -73,9 +76,14 @@
     loads = [
         pltpu.make_async_copy(qkv_ref.at[i], qkv_v.at[i], load_sem.at[i]) for i in (1, 2, 0)
     ]
+    loads += [
+        pltpu.make_async_copy(taps_hbm, taps_ref, load_sem.at[3]),
+        pltpu.make_async_copy(filt_hbm, filt_ref, load_sem.at[4]),
+        pltpu.make_async_copy(skip_hbm, skip_ref, load_sem.at[5]),
+    ]
     own = [
         pltpu.make_async_copy(
-            w_ref.at[PIECE * kind : PIECE * (kind + 1)], w_all.at[kind, 0, 0], own_sem.at[kind]
+            w_ref.at[PIECE * kind : PIECE * (kind + 1)], w_all.at[kind, OWN, OWN], own_sem.at[kind]
         )
         for kind in range(2)
     ]
@@ -93,13 +101,13 @@
         lane = 0 if direction == 1 else 1
         into = origin(direction, step)
         if step == 1:
-            src, dst = w_ref.at[PIECE * kind : PIECE * (kind + 1)], w_all.at[kind, 0, into]
+            src, dst = w_ref.at[PIECE * kind : PIECE * (kind + 1)], w_all.at[kind, OWN, into]
         elif step < 4:
-            src, dst = w_all.at[kind, 0, origin(direction, step - 1)], w_all.at[kind, 0, into]
+            src, dst = w_all.at[kind, OWN, origin(direction, step - 1)], w_all.at[kind, OWN, into]
         else:
             half = pl.ds(lane * (PIECE // 2), PIECE // 2)
-            src = w_all.at[kind, 0, origin(direction, 3), half]
-            dst = w_all.at[kind, 0, into, half]
+            src = w_all.at[kind, OWN, origin(direction, 3), half]
+            dst = w_all.at[kind, OWN, into, half]
         at = kind, lane, step - 1
         return remote(src, dst, s1.at[at], r1.at[at], minor_at[kind](direction))
 
@@ -108,9 +116,9 @@
         lo, hi = PACKS[pack]
         into = origin(direction, step)
         if step == 1 and pack == 0:
-            src, dst = w_ref.at[PIECE * kind : PIECE * (kind + 1)], w_all.at[kind, into, 0]
+            src, dst = w_ref.at[PIECE * kind : PIECE * (kind + 1)], w_all.at[kind, into, OWN]
         else:
-            came = 0 if step == 1 else origin(direction, step - 1)
+            came = OWN if step == 1 else origin(direction, step - 1)
             src = w_all.at[kind, came, pl.ds(lo, hi - lo)]
             dst = w_all.at[kind, into, pl.ds(lo, hi - lo)]
         at = kind, lane, step - 1, pack
@@ -266,49 +274,51 @@
         rows = jnp.concatenate(pieces, axis=0) if len(pieces) > 1 else pieces[0]
         return jnp.dot(rows, yt[...], preferred_element_type=F32)
 
+    def two(kind, major, batch, half):
+        return w_all[kind, major, pl.ds(4 * batch + 2 * half, 2)].reshape(2 * PIECE, WIDTH)
+
     def four(kind, major, half):
-        return w_all[kind, major, pl.ds(4 * half, 4)].reshape(4 * PIECE, WIDTH)
+        return [two(kind, major, batch, half) for batch in range(2)]
+
+    def target(slot):
+        return lax.rem(y + OFF[slot] + RING, RING)
+
+    delivered = []
+
+    def deliver(src, dst, send, recv, to):
+        copy = remote(src, dst, send, recv, {"chan": to})
+
+        @pl.when(to == c)
+        def keep():
+            pltpu.make_async_copy(src, dst, recv).start()
+
+        @pl.when(to != c)
+        def post():
+            copy.start()
+
+        delivered.append((to, copy))
 
     def a_swap(slot):
         return remote(ta.at[slot], sa.at[slot], as1.at[slot], ar1.at[slot], sibling)
 
     def a_first(slots):
-        got = project([four(0, m, 1 - p) for m in slots]).astype(BF16)
+        got = project(sum([four(0, m, 1 - p) for m in slots], [])).astype(BF16)
         for i, m in enumerate(slots):
             ta[m] = got[4 * PIECE * i : 4 * PIECE * (i + 1)]
             go(a_swap(m))
 
-    def target(slot):
-        return lax.rem(y + OFF[slot] + RING, RING)
-
-    def deliver(src, dst, send, recv, to):
-        copy = remote(src, dst, send, recv, {"chan": to})
-
-        @pl.when(to == c)
-        def keep():
-            pltpu.make_async_copy(src, dst, recv).start()
-
-        @pl.when(to != c)
-        def post():
-            copy.start()
-
-        return to, copy
-
-    delivered = []
-
     def a_second(slots):
-        got = project([four(0, m, p) for m in slots])
+        got = project(sum([four(0, m, p) for m in slots], []))
         for i, m in enumerate(slots):
             a_swap(m).wait_recv()
             qa[m] = (got[4 * PIECE * i : 4 * PIECE * (i + 1)] + sa[m].astype(F32)).astype(BF16)
-            delivered.append(deliver(qa.at[m], ra.at[x, p], as2.at[m], ar2.at[x, p], target(m)))
+            deliver(qa.at[m], ra.at[x, p], as2.at[m, 0], ar2.at[x, p], target(m))
 
     def b_swap(turn):
         return remote(tb.at[turn], sb.at[turn], bs1.at[turn], br1.at[turn], sibling)
 
     def b_rows(turn, half):
-        low, high = ROUNDS[turn]
-        return w_all[1, low + half * (high - low)].reshape(RING * PIECE, WIDTH)
+        return w_all[1, 2 * turn + half].reshape(RING * PIECE, WIDTH)
 
     def b_first(turn):
         tb[turn] = project([b_rows(turn, 1 - p)]).astype(BF16)
@@ -319,12 +329,49 @@
         b_swap(turn).wait_recv()
         qb[turn] = (got + sb[turn].astype(F32)).astype(BF16)
         for m in range(RING):
-            delivered.append(
-                deliver(
-                    qb.at[turn, PIECE * m : PIECE * (m + 1)], rb.at[turn, x, p],
-                    bs2.at[turn, m], br2.at[turn, x, p], target(m),
-                )
+            deliver(
+                qb.at[turn, PIECE * m : PIECE * (m + 1)], rb.at[turn, x, p],
+                bs2.at[turn, m], br2.at[turn, x, p], target(m),
             )
+
+    def o_swap(part):
+        at = pl.ds(4 * PIECE * part, 4 * PIECE)
+        return remote(tc.at[at], sc.at[at], cs1.at[part], cr1.at[part], sibling)
+
+    def o_post(single, batch, at):
+        for i in range(2):
+            to = lax.rem(y + jnp.where(p == 0, OFF[4 * batch + i], OFF[4 * batch + 2 + i]) + RING, RING)
+            deliver(
+                qc.at[pl.ds(at + PIECE * i, PIECE)], rc.at[single, x],
+                cs2.at[single, batch, i], cr2.at[single, x], to,
+            )
+
+    def o_first():
+        tc[: 4 * PIECE] = project(four(1, OWN, 1 - p)).astype(BF16)
+        go(o_swap(0))
+
+    def o_second():
+        got = project(four(1, OWN, p))
+        o_swap(0).wait_recv()
+        qc[: 4 * PIECE] = (got + sc[: 4 * PIECE].astype(F32)).astype(BF16)
+        for batch in range(2):
+            o_post(0, batch, 2 * PIECE * batch)
+
+    def far_first(batch):
+        at = pl.ds(4 * PIECE * (batch + 1), 4 * PIECE)
+        tc[at] = project([two(0, FAR, batch, 1 - p), two(1, FAR, batch, 1 - p)]).astype(BF16)
+        go(o_swap(batch + 1))
+
+    def far_second(batch):
+        base = 4 * PIECE * (batch + 1)
+        got = project([two(0, FAR, batch, p), two(1, FAR, batch, p)])
+        o_swap(batch + 1).wait_recv()
+        qc[base : base + 4 * PIECE] = (got + sc[base : base + 4 * PIECE].astype(F32)).astype(BF16)
+        deliver(
+            qc.at[base : base + 2 * PIECE], ra.at[x, p, pl.ds(2 * PIECE * batch, 2 * PIECE)],
+            as2.at[FAR, batch], ar2.at[x, p], target(FAR),
+        )
+        o_post(1, batch, base + 2 * PIECE)
 
     def own_wait():
         for copy in own:
@@ -332,64 +379,66 @@
 
     work(1.0, widen_all)
     for lo in (0, 4):
-        work(1.0, features, BLOCKS - 1, (lo, lo + 4))
+        work(1.4, features, BLOCKS - 1, (lo, lo + 4))
     work(0.1, send_tail)
     for lo in (0, 4):
-        work(1.0, features, 1, (lo, lo + 4))
+        work(1.4, features, 1, (lo, lo + 4))
     work(0.3, halo_arrives)
     for lo in (0, 4):
-        work(1.0, features, 0, (lo, lo + 4))
+        work(1.4, features, 0, (lo, lo + 4))
     work(0.1, tail_arrives)
     for lo in range(0, 64, 16):
-        work(1.2, conv, lo, lo + 16)
+        work(1.5, conv, lo, lo + 16)
     work(0.1, own_wait)
-    need(1)
-    work(0.4, a_first, (0,))
-    work(0.8, a_first, (1, 2))
-    work(0.8, b_first, 0)
-    work(0.4, a_second, (0,))
-    work(0.8, a_second, (1, 2))
-    work(0.8, b_second, 0)
-    need(2)
-    work(0.8, a_first, (3, 4))
-    work(0.8, b_first, 1)
-    work(0.8, a_second, (3, 4))
-    work(0.8, b_second, 1)
-    need(3)
-    work(0.8, a_first, (5, 6))
-    work(0.8, b_first, 2)
-    work(0.8, a_second, (5, 6))
-    work(0.8, b_second, 2)
+    work(0.6, a_first, (OWN,))
+    work(0.6, o_first)
+    work(0.6, a_second, (OWN,))
+    work(0.6, o_second)
+    for k in (1, 2, 3):
+        low, high = SLOT[k], SLOT[-k]
+        need(k)
+        work(1.0, a_first, (low, high))
+        work(1.0, b_first, k - 1)
+        work(1.0, a_second, (low, high))
+        work(1.2, b_second, k - 1)
+    while not {(4, g) for g in (0, 1, 2)} <= seen:
+        take_event()
+    far_first(0)
+    far_second(0)
     need(4)
-    work(0.4, a_first, (7,))
-    work(0.8, b_first, 3)
-    work(0.4, a_second, (7,))
-    work(0.8, b_second, 3)
+    far_first(1)
+    far_second(1)
 
     def place(kind, slot, rows):
         at = lax.rem(z + OFF[slot] + RING, RING) * (2 * PIECE) + kind * PIECE
         fin[pl.ds(pl.multiple_of(at, PIECE), PIECE), :] = rows
 
-    def total(ref, half, lead=()):
+    def total(refs):
         found = None
-        for chip in range(4):
-            term = ref[lead + (chip, half)].astype(F32)
+        for ref in refs:
+            term = ref[...].astype(F32)
             found = term if found is None else found + term
         return found
 
+    def arrived(ref, sem):
+        remote(ref, ref, cs2.at[0, 0, 0], sem, sibling).wait_recv()
+
+    for turn in range(PAIRS):
+        for half in range(2):
+            for chip in range(4):
+                arrived(rb.at[turn, chip, half], br2.at[turn, chip, half])
+            place(1, 2 * turn + half, total([rb.at[turn, chip, half] for chip in range(4)]))
+    for single, slot in ((0, OWN), (1, FAR)):
+        for chip in range(4):
+            arrived(rc.at[single, chip], cr2.at[single, chip])
+        place(1, slot, total([rc.at[single, chip] for chip in range(4)]))
     for half in range(2):
         for chip in range(4):
-            remote(ra.at[chip, half], ra.at[chip, half], as2.at[0], ar2.at[chip, half], sibling).wait_recv()
-    for half in range(2):
-        found = total(ra, half)
+            arrived(ra.at[chip, half], ar2.at[chip, half])
+        found = total([ra.at[chip, half] for chip in range(4)])
         for i in range(4):
-            place(0, 4 * half + i, found[PIECE * i : PIECE * (i + 1)])
-    for turn in range(4):
-        for half in range(2):
-            for chip in range(4):
-                here = rb.at[turn, chip, half]
-                remote(here, here, bs2.at[turn, 0], br2.at[turn, chip, half], sibling).wait_recv()
-            place(1, ROUNDS[turn][half], total(rb, half, (turn,)))
+            slot = 4 * (i // 2) + 2 * half + i % 2
+            place(0, slot, found[PIECE * i : PIECE * (i + 1)])
     for a in range(BLOCKS):
         for n in range(4):
             tile = fin[LANES * n : LANES * (n + 1), SPAN * a : SPAN * (a + 1)]
@@ -411,9 +460,12 @@
     return pl.pallas_call(
         kernel,
         out_shape=jax.ShapeDtypeStruct((ROWS, 512), BF16),
-        in_specs=[anywhere, vmem, vmem, vmem, anywhere],
+        in_specs=[anywhere] * 5,
         out_specs=vmem,
         scratch_shapes=[
+            pltpu.VMEM((3, FTAPS, WIDTH), F32),
+            pltpu.VMEM((WIDTH // GROUP, SPAN), BF16),
+            pltpu.VMEM((1, WIDTH), F32),
             pltpu.VMEM((2, RING, RING, PIECE, WIDTH), BF16),
             pltpu.VMEM((3, ROWS, WIDTH), BF16),
             pltpu.VMEM((3, HALO, WIDTH), BF16),
@@ -426,17 +478,22 @@
             pltpu.VMEM((RING,) + half_piece, BF16),
             pltpu.VMEM((RING,) + half_piece, BF16),
             pltpu.VMEM((RING,) + half_piece, BF16),
-            pltpu.VMEM((4, RING * PIECE, ROWS), BF16),
-            pltpu.VMEM((4, RING * PIECE, ROWS), BF16),
-            pltpu.VMEM((4, RING * PIECE, ROWS), BF16),
+            pltpu.VMEM((PAIRS, RING * PIECE, ROWS), BF16),
+            pltpu.VMEM((PAIRS, RING * PIECE, ROWS), BF16),
+            pltpu.VMEM((PAIRS, RING * PIECE, ROWS), BF16),
+            pltpu.VMEM((12 * PIECE, ROWS), BF16),
+            pltpu.VMEM((12 * PIECE, ROWS), BF16),
+            pltpu.VMEM((12 * PIECE, ROWS), BF16),
             pltpu.VMEM((4, 2) + half_piece, BF16),
-            pltpu.VMEM((4, 4, 2, PIECE, ROWS), BF16),
+            pltpu.VMEM((PAIRS, 4, 2, PIECE, ROWS), BF16),
+            pltpu.VMEM((2, 4, PIECE, ROWS), BF16),
             pltpu.VMEM((512, ROWS), F32),
-            dma((3,)), dma((2,)), dma((2,)), dma((2,)),
+            dma((6,)), dma((2,)), dma((2,)), dma((2,)),
             dma((2, 2, 4)), dma((2, 2, 4)),
             dma((2, 2, 4, 5)), dma((2, 2, 4, 5)),
-            dma((RING,)), dma((RING,)), dma((RING,)), dma((4, 2)),
-            dma((4,)), dma((4,)), dma((4, RING)), dma((4, 4, 2)),
+            dma((RING,)), dma((RING,)), dma((RING, 2)), dma((4, 2)),
+            dma((PAIRS,)), dma((PAIRS,)), dma((PAIRS, RING)), dma((PAIRS, 4, 2)),
+            dma((3,)), dma((3,)), dma((2, 2, 2)), dma((2, 4)),
         ],
         compiler_params=pltpu.CompilerParams(
             collective_id=0, has_side_effects=True, vmem_limit_bytes=56 * 2**20

time: 85.9 us -> 83.7 us (0.974)
  Pallas kernels: 83.9 us -> 81.5 us
    pallas_call x1, Pallas kernels: 83.9 us -> 81.5 us  [local(): pl.pallas_call(kernel, out_shape=jax.ShapeDtypeStruct((ROWS, 512), BF16),...]
where the time goes in v2:
time: 83.7 us; the launch traced here: 83.3 us
  Pallas kernels  81.5 us (97%)
  local copies, waits for them, and re-layouts  1.77 us (2%)
    pallas_call x1, Pallas kernels, local(): pl.pallas_call(kernel, out_shape=jax.ShapeDtypeStruct((ROWS, 512), BF16),...  81.5 us
    unnamed x1, local copies, waits for them, and re-layouts  1.77 us

profile of v2, /device:TPU:4, one launch (start us, length us, event | category | flops | bytes accessed | tf_op | source)
XLA Modules:
  0.0 83.3 jit_solution(10842151980129836521)
XLA Ops:
  0.0 81.5 %shard_map.55 = bf16[384,512]{1,0:T(8,128)(2,1)} custom-call(bf16[3,384,1024]{2,1,0:T(8,128)(2,1)} %qkv_ref.1, f32[3,7,1024]{2,1,0:T(8,128)} %taps_hbm.1, bf16[64,128]{1,0:T(8,128)(2,1)} %bitcast.4, f32[1,1024]{1,0:T(1,128)} %bitcast.5, bf16[64,1024]{1,0:T(8,128)(2,1)} %bitcast.3), custom_call_target="tpu_custom_call" | custom-call | tf_op jit(solution)/shard_map/pallas_call | solution.py:460
  81.6 1.8 %copy.7 = bf16[384,512]{1,0:T(8,128)(2,1)} copy(bf16[384,512]{1,0:T(8,128)(2,1)} %shard_map.55) | data formatting | bytes 786432

commit v3 on v1

v3 whole, which is shorter than its diff:
```python
import jax
import jax.numpy as jnp
from jax import lax
from jax.experimental import pallas as pl
from jax.experimental.pallas import tpu as pltpu
from jax.sharding import PartitionSpec as P

MESH = pl.DeviceIdType.MESH
F32 = jnp.float32
BF16 = jnp.bfloat16

RING = 8
GROUP = 16
SPAN = 128
FTAPS = 7
ROWS = 384
WIDTH = 1024
BLOCKS = ROWS // SPAN
LANES = 128
STRIPS = WIDTH // LANES
PIECE = 32
HALO = 16
PAD = 8

OFF = (1, -1, 2, -2, 3, -3, 4, 0)
SLOT = {off: slot for slot, off in enumerate(OFF)}
OWN = SLOT[0]
GROUPS = ((7,), (0, 1), (2, 3), (4, 5), (6,))
NEAR, CROSS, NEAR_EXT, CROSS_EXT = (pl.ds(2 * PIECE * i, 2 * PIECE) for i in range(4))
PARTS = (NEAR, pl.ds(4 * PIECE, PIECE), CROSS, pl.ds(6 * PIECE, PIECE))
HALF = 4 * PIECE


def origin(direction, step):
    return SLOT[4 if step == 4 else -direction * step]


def kernel(
    qkv_ref, taps_hbm, filt_hbm, skip_hbm, w_ref, out_ref,
    taps_ref, filt_ref, skip_ref,
    w_all, qkv_v, halo, ext_v, ut, qt, skt, hf, yt, yp,
    ta, sa, qa, ra, qp, rp, fin,
    load_sem, own_sem, halo_sem, tail_sem,
    xs, es, er, s2, r2, ys, yr, as1, ar1, as2, ar2, ps,
):
    s = lax.axis_index("seq")
    c = lax.axis_index("chan")
    y = lax.div(s, RING)
    z = lax.rem(s, RING)
    x = lax.div(c, 2)
    p = lax.rem(c, 2)

    def y_at(d):
        return {"seq": lax.rem(y + d + RING, RING) * RING + z}

    def z_at(d):
        return {"seq": y * RING + lax.rem(z + d + 2 * RING, RING)}

    def seq_at(d):
        return {"seq": lax.rem(s + d + RING * RING, RING * RING)}

    sibling = {"chan": c + 1 - 2 * p}
    outer = 2 * lax.rem(z, 2) - 1
    inner = -outer
    started = []

    def remote(src, dst, send, recv, to):
        return pltpu.make_async_remote_copy(
            src_ref=src, dst_ref=dst, send_sem=send, recv_sem=recv, device_id=to, device_id_type=MESH
        )

    def go(copy):
        copy.start()
        started.append(copy)

    loads = [
        pltpu.make_async_copy(qkv_ref.at[i], qkv_v.at[i], load_sem.at[i]) for i in (1, 2, 0)
    ]
    loads += [
        pltpu.make_async_copy(taps_hbm, taps_ref, load_sem.at[3]),
        pltpu.make_async_copy(filt_hbm, filt_ref, load_sem.at[4]),
        pltpu.make_async_copy(skip_hbm, skip_ref, load_sem.at[5]),
    ]
    own = pltpu.make_async_copy(w_ref, w_all.at[OWN, NEAR], own_sem)
    for copy in loads + [own]:
        copy.start()

    barrier = pltpu.get_barrier_semaphore()
    greeted = [{"chan": lax.rem(c + d, 8)} for d in range(1, 8)]
    greeted += [z_at(outer), z_at(inner), z_at(3 * inner), y_at(1), y_at(-1), seq_at(1), seq_at(-1)]
    for to in greeted:
        pl.semaphore_signal(barrier, inc=1, device_id=to, device_id_type=MESH)
    pl.semaphore_wait(barrier, len(greeted))

    def cross():
        return remote(w_ref, w_all.at[OWN, CROSS], xs.at[0], xs.at[1], z_at(3 * inner))

    def ext(which, slot):
        src, dst = ((NEAR, NEAR_EXT), (CROSS, CROSS_EXT))[which]
        if slot != OWN:
            src, dst = [pl.ds(at.start + PIECE, PIECE) for at in (src, dst)]
        found = w_ref if slot == OWN and which == 0 else w_all.at[slot, src]
        return remote(found, w_all.at[slot, dst], es.at[which, slot], er.at[which, slot], z_at(outer))

    def ring(direction, step, part):
        lane = 0 if direction == 1 else 1
        rows = PARTS[part]
        into = origin(direction, step)
        came = OWN if step == 1 else origin(direction, step - 1)
        src = w_ref if step == 1 and part == 0 else w_all.at[came, rows]
        at = lane, step - 1, part
        return remote(src, w_all.at[into, rows], s2.at[at], r2.at[at], y_at(direction))

    def lanes_of(step, part):
        if step < 4:
            return (1, -1)
        return (1,) if part < 2 else (-1,)

    def start_part(part):
        for direction in (1, -1):
            go(ring(direction, 1, part))

    def near_arrives():
        ext(0, OWN).wait_recv()
        start_part(1)

    def cross_arrives():
        cross().wait_recv()
        start_part(2)
        go(ext(1, OWN))

    def cross_ext_arrives():
        ext(1, OWN).wait_recv()
        start_part(3)

    def part_arrives(step, part):
        for direction in lanes_of(step, part):
            ring(direction, step, part).wait_recv()
            if step < 4 and direction in lanes_of(step + 1, part):
                go(ring(direction, step + 1, part))
            if part in (0, 2):
                go(ext(part // 2, origin(direction, step)))

    reach = (2.0, 3.4, 5.0, 6.4)
    events = [(2.2, near_arrives, ()), (3.6, cross_arrives, ()), (5.6, cross_ext_arrives, ())]
    events += [
        (2.0 + 8.5 * (k - 1) + reach[part], part_arrives, (k, part)) for k in range(1, 5) for part in range(4)
    ]
    events.sort(key=lambda e: e[0])
    clock = [0.0]
    seen = set()

    def take_event():
        at, fn, args = events.pop(0)
        fn(*args)
        seen.add(args)
        clock[0] = max(clock[0], at)

    def work(cost, fn, *args):
        while events and events[0][0] <= clock[0]:
            take_event()
        fn(*args)
        clock[0] += cost

    def need(step):
        wanted = {(step, part) for part in range(4)}
        while not wanted <= seen:
            take_event()
        for slot in GROUPS[step]:
            for which in range(2):
                ext(which, slot).wait_recv()

    halo_copy = remote(
        qkv_ref.at[:, ROWS - HALO : ROWS], halo, halo_sem.at[0], halo_sem.at[1], seq_at(1)
    )
    go(cross())
    go(ext(0, OWN))
    start_part(0)
    go(halo_copy)

    def widen(strip):
        at = pl.ds(pl.multiple_of(strip * LANES, LANES), LANES)
        for i in range(3):
            ext_v[i, strip, PAD:, :] = qkv_v[i, :, at].astype(F32)

    def widen_halo(strip):
        at = pl.ds(pl.multiple_of(strip * LANES, LANES), LANES)
        for i in range(3):
            before = halo[i, :, at].astype(F32)[HALO - PAD :]
            ext_v[i, strip, :PAD, :] = jnp.where(s == 0, 0.0, before)

    def feature(i, block, strip, at):
        total = None
        for j in range(FTAPS):
            term = taps_ref[i, j : j + 1, at] * ext_v[i, strip, pl.ds(PAD + SPAN * block - j, SPAN), :]
            total = term if total is None else total + term
        return total

    def features(block, strips):
        def body(strip, carry):
            at = pl.ds(pl.multiple_of(strip * LANES, LANES), LANES)
            u = (feature(1, block, strip, at) * feature(2, block, strip, at)).astype(BF16).astype(F32)
            ut[block + 1, at, :] = u.T.astype(BF16)
            qt[block, at, :] = feature(0, block, strip, at).T
            return carry

        lax.fori_loop(strips[0], strips[1], body, 0)

    def widen_all():
        for copy in loads:
            copy.wait()

        def body(strip, carry):
            widen(strip)
            return carry

        lax.fori_loop(0, STRIPS, body, 0)
        hf[...] = filt_ref[...].astype(F32)

    def halo_arrives():
        halo_copy.wait_recv()

        def body(strip, carry):
            widen_halo(strip)
            at = pl.ds(pl.multiple_of(strip * LANES, LANES), LANES)
            skt[at, :] = jnp.broadcast_to(skip_ref[:, at], (LANES, LANES)).T
            return carry

        lax.fori_loop(0, STRIPS, body, 0)

    tail_copy = remote(ut.at[BLOCKS], ut.at[0], tail_sem.at[0], tail_sem.at[1], seq_at(1))

    def send_tail():
        go(tail_copy)

    def tail_arrives():
        tail_copy.wait_recv()

        @pl.when(s == 0)
        def clear():
            ut[0] = jnp.zeros((WIDTH, SPAN), BF16)

    def conv(lo, hi):
        def body(g, carry):
            row = lax.broadcasted_iota(jnp.int32, (SPAN, SPAN), 0)
            col = lax.broadcasted_iota(jnp.int32, (SPAN, SPAN), 1)
            taps = jnp.broadcast_to(hf[pl.ds(g, 1), :], (SPAN, SPAN))
            ring = pltpu.roll(taps, 0, 1, stride=1, stride_axis=0)
            here = jnp.where(row <= col, ring, 0.0)
            before = jnp.where(row > col, ring, 0.0)
            matrix = jnp.concatenate([before, here], axis=0).astype(BF16)
            at = pl.ds(pl.multiple_of(g * GROUP, GROUP), GROUP)
            parts = [ut[b, at, :] for b in range(BLOCKS + 1)]
            window = jnp.concatenate(
                [jnp.concatenate(parts[:BLOCKS], axis=0), jnp.concatenate(parts[1:], axis=0)], axis=1
            )
            mixed = jnp.dot(window, matrix, preferred_element_type=F32)
            for b in range(BLOCKS):
                field = mixed[GROUP * b : GROUP * (b + 1)] + skt[at, :] * parts[b + 1].astype(F32)
                yt[at, SPAN * b : SPAN * (b + 1)] = (qt[b, at, :] * field).astype(BF16)
            return carry

        lax.fori_loop(lo, hi, body, 0, unroll=4)

    def swap_y(quarter):
        at = pl.ds(quarter * (WIDTH // 4), WIDTH // 4)
        return remote(yt.at[at], yp.at[at], ys.at[quarter], yr.at[quarter], z_at(inner))

    def send_y(quarter):
        go(swap_y(quarter))

    def project(slots, half, tokens):
        rows = [w_all[m, pl.ds(pl.multiple_of(half * HALF, HALF), HALF)] for m in slots]
        rows = jnp.concatenate(rows, axis=0) if len(rows) > 1 else rows[0]
        return jnp.dot(rows, (yt, yp)[tokens][...], preferred_element_type=F32)

    def swap(group, tokens):
        low = GROUPS[group][0]
        at = pl.ds(low * HALF, len(GROUPS[group]) * HALF)
        return remote(
            ta.at[tokens, at], sa.at[tokens, at],
            as1.at[tokens, group], ar1.at[tokens, group], sibling,
        )

    def give(group, tokens):
        low, many = GROUPS[group][0], len(GROUPS[group])
        ta[tokens, low * HALF : (low + many) * HALF] = project(GROUPS[group], 1 - p, tokens).astype(BF16)
        go(swap(group, tokens))

    delivered = []

    def deliver(src, dst, send, recv, to):
        copy = remote(src, dst, send, recv, {"chan": to})

        @pl.when(to == c)
        def keep():
            pltpu.make_async_copy(src, dst, recv).start()

        @pl.when(to != c)
        def post():
            copy.start()

        delivered.append((to, copy))

    def take(group, tokens):
        low, many = GROUPS[group][0], len(GROUPS[group])
        at = slice(low * HALF, (low + many) * HALF)
        got = project(GROUPS[group], p, tokens)
        swap(group, tokens).wait_recv()
        qa[tokens, at] = (got + sa[tokens, at].astype(F32)).astype(BF16)
        for m in GROUPS[group]:
            deliver(
                qa.at[tokens, m * HALF : (m + 1) * HALF], ra.at[tokens, x, p],
                as2.at[tokens, m], ar2.at[tokens, x, p], lax.rem(y + OFF[m] + RING, RING),
            )

    def gathered(tokens, half):
        found = None
        for chip in range(4):
            here = ra.at[tokens, chip, half]
            remote(here, here, as2.at[tokens, 0], ar2.at[tokens, chip, half], sibling).wait_recv()
        for chip in range(4):
            term = ra[tokens, chip, half].astype(F32)
            found = term if found is None else found + term
        return found

    hand = remote(qp, rp, ps.at[0], ps.at[1], z_at(inner))
    ahead = lax.rem(c - y + RING, RING)
    my_group = jnp.minimum(ahead, RING - ahead)

    def finish(group):
        @pl.when(my_group == group)
        def partner_sum():
            for half in range(2):
                qp[half * HALF : (half + 1) * HALF] = gathered(1, half).astype(BF16)
            hand.start()

    def own_wait():
        own.wait()

    work(1.0, widen_all)
    for lo in (0, 4):
        work(1.4, features, BLOCKS - 1, (lo, lo + 4))
    work(0.1, send_tail)
    for lo in (0, 4):
        work(1.4, features, 1, (lo, lo + 4))
    work(0.3, halo_arrives)
    for lo in (0, 4):
        work(1.4, features, 0, (lo, lo + 4))
    work(0.1, tail_arrives)
    for quarter in range(4):
        work(1.5, conv, 16 * quarter, 16 * quarter + 16)
        work(0.1, send_y, quarter)
    work(0.1, own_wait)
    work(0.6, give, 0, 0)
    need(1)
    work(1.0, give, 1, 0)
    work(0.6, take, 0, 0)
    work(1.0, take, 1, 0)
    need(2)
    work(1.0, give, 2, 0)
    work(1.0, take, 2, 0)
    for quarter in range(4):
        swap_y(quarter).wait_recv()
    work(0.6, give, 0, 1)
    work(1.0, give, 1, 1)
    work(0.6, take, 0, 1)
    work(1.0, take, 1, 1)
    work(1.0, give, 2, 1)
    work(1.0, take, 2, 1)
    need(3)
    work(1.0, give, 3, 1)
    work(1.0, give, 3, 0)
    work(0.1, finish, 0)
    work(0.1, finish, 1)
    work(1.0, take, 3, 1)
    work(1.0, take, 3, 0)
    need(4)
    give(4, 1)
    give(4, 0)
    finish(2)
    take(4, 1)
    take(4, 0)
    finish(3)
    finish(4)

    def place(z_from, rows):
        at = lax.rem(z + z_from + 2 * RING, RING) * (2 * PIECE)
        fin[pl.ds(pl.multiple_of(at, 2 * PIECE), 2 * PIECE), :] = rows

    for half in range(2):
        found = gathered(0, half)
        for i, z_from in enumerate(((0, outer + 4), (outer, 4))[half]):
            place(z_from, found[2 * PIECE * i : 2 * PIECE * (i + 1)])
    hand.wait_recv()
    for i, z_from in enumerate((inner, 2 * inner + 4, 2 * inner, inner + 4)):
        place(z_from, rp[2 * PIECE * i : 2 * PIECE * (i + 1)].astype(F32))
    for a in range(BLOCKS):
        for n in range(4):
            tile = fin[LANES * n : LANES * (n + 1), SPAN * a : SPAN * (a + 1)]
            out_ref[SPAN * a : SPAN * (a + 1), LANES * n : LANES * (n + 1)] = tile.T.astype(BF16)

    for copy in started:
        copy.wait_send()
    hand.wait_send()
    for to, copy in delivered:
        @pl.when(to != c)
        def drain(copy=copy):
            copy.wait_send()


def local(qkv, feat_taps, long_filter, skip_gain, out_weight):
    vmem = pl.BlockSpec(memory_space=pltpu.VMEM)
    anywhere = pl.BlockSpec(memory_space=pl.ANY)
    dma = pltpu.SemaphoreType.DMA
    return pl.pallas_call(
        kernel,
        out_shape=jax.ShapeDtypeStruct((ROWS, 512), BF16),
        in_specs=[anywhere] * 5,
        out_specs=vmem,
        scratch_shapes=[
            pltpu.VMEM((3, FTAPS, WIDTH), F32),
            pltpu.VMEM((WIDTH // GROUP, SPAN), BF16),
            pltpu.VMEM((1, WIDTH), F32),
            pltpu.VMEM((RING, 8 * PIECE, WIDTH), BF16),
            pltpu.VMEM((3, ROWS, WIDTH), BF16),
            pltpu.VMEM((3, HALO, WIDTH), BF16),
            pltpu.VMEM((3, STRIPS, PAD + ROWS, LANES), F32),
            pltpu.VMEM((BLOCKS + 1, WIDTH, SPAN), BF16),
            pltpu.VMEM((BLOCKS, WIDTH, SPAN), F32),
            pltpu.VMEM((WIDTH, SPAN), F32),
            pltpu.VMEM((WIDTH // GROUP, SPAN), F32),
            pltpu.VMEM((WIDTH, ROWS), BF16),
            pltpu.VMEM((WIDTH, ROWS), BF16),
            pltpu.VMEM((2, RING * HALF, ROWS), BF16),
            pltpu.VMEM((2, RING * HALF, ROWS), BF16),
            pltpu.VMEM((2, RING * HALF, ROWS), BF16),
            pltpu.VMEM((2, 4, 2, HALF, ROWS), BF16),
            pltpu.VMEM((2 * HALF, ROWS), BF16),
            pltpu.VMEM((2 * HALF, ROWS), BF16),
            pltpu.VMEM((512, ROWS), F32),
            dma((6,)), dma, dma((2,)), dma((2,)),
            dma((2,)), dma((2, RING)), dma((2, RING)),
            dma((2, 4, 4)), dma((2, 4, 4)), dma((4,)), dma((4,)),
            dma((2, 5)), dma((2, 5)), dma((2, RING)), dma((2, 4, 2)), dma((2,)),
        ],
        compiler_params=pltpu.CompilerParams(
            collective_id=0, has_side_effects=True, vmem_limit_bytes=56 * 2**20
        ),
    )(qkv, feat_taps, long_filter.T, skip_gain.reshape(1, WIDTH), out_weight.T)


def solution(mesh):
    return jax.shard_map(
        local,
        mesh=mesh,
        in_specs=(
            P(None, "seq", "chan"),
            P(None, None, "chan"),
            P(None, "chan"),
            P("chan"),
            P("chan", "seq"),
        ),
        out_specs=P("seq", "chan"),
        check_vma=False,
    )
```

time: 85.9 us -> 90.3 us (1.051)
  Pallas kernels: 83.9 us -> 88.3 us
    pallas_call x1, Pallas kernels: 83.9 us -> 88.3 us  [local(): pl.pallas_call(kernel, out_shape=jax.ShapeDtypeStruct((ROWS, 512), BF16),...]
where the time goes in v3:
time: 90.3 us; the launch traced here: 90.1 us
  Pallas kernels  88.3 us (98%)
  local copies, waits for them, and re-layouts  1.77 us (2%)
    pallas_call x1, Pallas kernels, local(): pl.pallas_call(kernel, out_shape=jax.ShapeDtypeStruct((ROWS, 512), BF16),...  88.3 us

profile of v3, /device:TPU:4, one launch (start us, length us, event | category | flops | bytes accessed | tf_op | source)
XLA Modules:
  0.0 90.1 jit_solution(11557052264424162189)
XLA Ops:
  0.0 88.3 %shard_map.55 = bf16[384,512]{1,0:T(8,128)(2,1)} custom-call(bf16[3,384,1024]{2,1,0:T(8,128)(2,1)} %qkv_ref.1, f32[3,7,1024]{2,1,0:T(8,128)} %taps_hbm.1, bf16[64,128]{1,0:T(8,128)(2,1)} %bitcast.4, f32[1,1024]{1,0:T(1,128)} %bitcast.5, bf16[64,1024]{1,0:T(8,128)(2,1)} %bitcast.3), custom_call_target="tpu_custom_call" | custom-call | tf_op jit(solution)/shard_map/pallas_call | solution.py:416
  88.3 1.8 %copy.7 = bf16[384,512]{1,0:T(8,128)(2,1)} copy(bf16[384,512]{1,0:T(8,128)(2,1)} %shard_map.55) | data formatting | bytes 786432

commit v4 on v3

--- a/solution.py
+++ b/solution.py
@@ -21,6 +21,9 @@
 PIECE = 32
 HALO = 16
 PAD = 8
+PITCH = 49
+SUBS = 8
+TALL = PITCH * SUBS
 
 OFF = (1, -1, 2, -2, 3, -3, 4, 0)
 SLOT = {off: slot for slot, off in enumerate(OFF)}
@@ -29,6 +32,7 @@
 NEAR, CROSS, NEAR_EXT, CROSS_EXT = (pl.ds(2 * PIECE * i, 2 * PIECE) for i in range(4))
 PARTS = (NEAR, pl.ds(4 * PIECE, PIECE), CROSS, pl.ds(6 * PIECE, PIECE))
 HALF = 4 * PIECE
+BATCH = 8
 
 
 def origin(direction, step):
@@ -38,7 +42,7 @@
 def kernel(
     qkv_ref, taps_hbm, filt_hbm, skip_hbm, w_ref, out_ref,
     taps_ref, filt_ref, skip_ref,
-    w_all, qkv_v, halo, ext_v, ut, qt, skt, hf, yt, yp,
+    w_all, qkv_v, halo, ext_v, ub, qb, ut, qt, skt, hf, mats, yt, yp,
     ta, sa, qa, ra, qp, rp, fin,
     load_sem, own_sem, halo_sem, tail_sem,
     xs, es, er, s2, r2, ys, yr, as1, ar1, as2, ar2, ps,
@@ -78,11 +82,11 @@
     ]
     loads += [
         pltpu.make_async_copy(taps_hbm, taps_ref, load_sem.at[3]),
+        pltpu.make_async_copy(skip_hbm, skip_ref, load_sem.at[5]),
         pltpu.make_async_copy(filt_hbm, filt_ref, load_sem.at[4]),
-        pltpu.make_async_copy(skip_hbm, skip_ref, load_sem.at[5]),
     ]
     own = pltpu.make_async_copy(w_ref, w_all.at[OWN, NEAR], own_sem)
-    for copy in loads + [own]:
+    for copy in loads[::-1] + [own]:
         copy.start()
 
     barrier = pltpu.get_barrier_semaphore()
@@ -90,6 +94,26 @@
     greeted += [z_at(outer), z_at(inner), z_at(3 * inner), y_at(1), y_at(-1), seq_at(1), seq_at(-1)]
     for to in greeted:
         pl.semaphore_signal(barrier, inc=1, device_id=to, device_id_type=MESH)
+
+    def toeplitz(low, high):
+        def body(step, carry):
+            row = lax.broadcasted_iota(jnp.int32, (SPAN, SPAN), 0)
+            col = lax.broadcasted_iota(jnp.int32, (SPAN, SPAN), 1)
+            for i in range(4):
+                g = step * 4 + i
+                taps = jnp.broadcast_to(hf[pl.ds(g, 1), :], (SPAN, SPAN))
+                turned = pltpu.roll(taps, 0, 1, stride=1, stride_axis=0)
+                mats[g, :SPAN] = jnp.where(row > col, turned, 0.0).astype(BF16)
+                mats[g, SPAN:] = jnp.where(row <= col, turned, 0.0).astype(BF16)
+            return carry
+
+        lax.fori_loop(low // 4, high // 4, body, 0)
+
+    for copy in loads[5:]:
+        copy.wait()
+    hf[...] = filt_ref[...].astype(F32)
+    toeplitz(0, 32)
+
     pl.semaphore_wait(barrier, len(greeted))
 
     def cross():
@@ -178,89 +202,109 @@
     start_part(0)
     go(halo_copy)
 
-    def widen(strip):
-        at = pl.ds(pl.multiple_of(strip * LANES, LANES), LANES)
-        for i in range(3):
-            ext_v[i, strip, PAD:, :] = qkv_v[i, :, at].astype(F32)
-
-    def widen_halo(strip):
-        at = pl.ds(pl.multiple_of(strip * LANES, LANES), LANES)
-        for i in range(3):
-            before = halo[i, :, at].astype(F32)[HALO - PAD :]
-            ext_v[i, strip, :PAD, :] = jnp.where(s == 0, 0.0, before)
-
-    def feature(i, block, strip, at):
-        total = None
-        for j in range(FTAPS):
-            term = taps_ref[i, j : j + 1, at] * ext_v[i, strip, pl.ds(PAD + SPAN * block - j, SPAN), :]
-            total = term if total is None else total + term
-        return total
-
-    def features(block, strips):
+    def widen():
+        for copy in loads[:5]:
+            copy.wait()
+
         def body(strip, carry):
             at = pl.ds(pl.multiple_of(strip * LANES, LANES), LANES)
-            u = (feature(1, block, strip, at) * feature(2, block, strip, at)).astype(BF16).astype(F32)
-            ut[block + 1, at, :] = u.T.astype(BF16)
-            qt[block, at, :] = feature(0, block, strip, at).T
+            for i in range(3):
+                ext_v[i, strip, PAD : PAD + ROWS, :] = qkv_v[i, :, at].astype(F32)
+                ext_v[i, strip, PAD + ROWS :, :] = jnp.zeros((TALL - ROWS, LANES), F32)
+            skt[at, :] = jnp.broadcast_to(skip_ref[:, at], (LANES, LANES)).T
             return carry
 
-        lax.fori_loop(strips[0], strips[1], body, 0)
-
-    def widen_all():
-        for copy in loads:
-            copy.wait()
-
-        def body(strip, carry):
-            widen(strip)
-            return carry
-
         lax.fori_loop(0, STRIPS, body, 0)
-        hf[...] = filt_ref[...].astype(F32)
 
     def halo_arrives():
         halo_copy.wait_recv()
 
         def body(strip, carry):
-            widen_halo(strip)
             at = pl.ds(pl.multiple_of(strip * LANES, LANES), LANES)
-            skt[at, :] = jnp.broadcast_to(skip_ref[:, at], (LANES, LANES)).T
+            for i in range(3):
+                before = halo[i, :, at].astype(F32)[HALO - PAD :]
+                ext_v[i, strip, :PAD, :] = jnp.where(s == 0, 0.0, before)
             return carry
 
         lax.fori_loop(0, STRIPS, body, 0)
 
-    tail_copy = remote(ut.at[BLOCKS], ut.at[0], tail_sem.at[0], tail_sem.at[1], seq_at(1))
-
-    def send_tail():
-        go(tail_copy)
-
-    def tail_arrives():
-        tail_copy.wait_recv()
+    def features(low, high):
+        def body(strip, carry):
+            at = pl.ds(pl.multiple_of(strip * LANES, LANES), LANES)
+            taps = [
+                [jnp.broadcast_to(taps_ref[i, j : j + 1, at], (SUBS, LANES)) for j in range(FTAPS)]
+                for i in range(3)
+            ]
+
+            def load(i, r):
+                return ext_v[i, strip, pl.ds(PAD + r, SUBS, stride=PITCH), :]
+
+            def line(i, window):
+                total = taps[i][0] * window[-1]
+                for j in range(1, FTAPS):
+                    total = total + taps[i][j] * window[-1 - j]
+                return total
+
+            windows = [[load(i, r) for r in range(1 - FTAPS, 0)] for i in (1, 2)]
+            for r in range(PITCH):
+                found = []
+                for i in (1, 2):
+                    windows[i - 1] = windows[i - 1][1 - FTAPS :] + [load(i, r)]
+                    found.append(line(i, windows[i - 1]))
+                ub[strip, pl.ds(r, SUBS, stride=PITCH), :] = found[0] * found[1]
+            window = [load(0, r) for r in range(1 - FTAPS, 0)]
+            for r in range(PITCH):
+                window = window[1 - FTAPS :] + [load(0, r)]
+                qb[strip, pl.ds(r, SUBS, stride=PITCH), :] = line(0, window)
+            for b in range(BLOCKS):
+                ut[b + 1, at, :] = ub[strip, SPAN * b : SPAN * (b + 1), :].T.astype(BF16)
+                qt[b, at, :] = qb[strip, SPAN * b : SPAN * (b + 1), :].T
+            return carry
+
+        lax.fori_loop(low, high, body, 0)
+
+    def tail(quarter):
+        at = pl.ds(quarter * (WIDTH // 4), WIDTH // 4)
+        return remote(
+            ut.at[BLOCKS, at], ut.at[0, at], tail_sem.at[0, quarter], tail_sem.at[1, quarter], seq_at(1)
+        )
+
+    def send_tail(quarter):
+        go(tail(quarter))
+
+    def tail_arrives(quarter):
+        tail(quarter).wait_recv()
 
         @pl.when(s == 0)
         def clear():
-            ut[0] = jnp.zeros((WIDTH, SPAN), BF16)
-
-    def conv(lo, hi):
-        def body(g, carry):
-            row = lax.broadcasted_iota(jnp.int32, (SPAN, SPAN), 0)
-            col = lax.broadcasted_iota(jnp.int32, (SPAN, SPAN), 1)
-            taps = jnp.broadcast_to(hf[pl.ds(g, 1), :], (SPAN, SPAN))
-            ring = pltpu.roll(taps, 0, 1, stride=1, stride_axis=0)
-            here = jnp.where(row <= col, ring, 0.0)
-            before = jnp.where(row > col, ring, 0.0)
-            matrix = jnp.concatenate([before, here], axis=0).astype(BF16)
-            at = pl.ds(pl.multiple_of(g * GROUP, GROUP), GROUP)
-            parts = [ut[b, at, :] for b in range(BLOCKS + 1)]
-            window = jnp.concatenate(
-                [jnp.concatenate(parts[:BLOCKS], axis=0), jnp.concatenate(parts[1:], axis=0)], axis=1
-            )
-            mixed = jnp.dot(window, matrix, preferred_element_type=F32)
-            for b in range(BLOCKS):
-                field = mixed[GROUP * b : GROUP * (b + 1)] + skt[at, :] * parts[b + 1].astype(F32)
-                yt[at, SPAN * b : SPAN * (b + 1)] = (qt[b, at, :] * field).astype(BF16)
+            ut[0, quarter * (WIDTH // 4) : (quarter + 1) * (WIDTH // 4)] = jnp.zeros((WIDTH // 4, SPAN), BF16)
+
+    def conv(low, high):
+        def body(step, carry):
+            base = step * BATCH
+            spots = [pl.ds(pl.multiple_of((base + i) * GROUP, GROUP), GROUP) for i in range(BATCH)]
+            parts = [[ut[b, at, :] for b in range(BLOCKS + 1)] for at in spots]
+            mixed = []
+            for i in range(BATCH):
+                window = jnp.concatenate(
+                    [
+                        jnp.concatenate(parts[i][:BLOCKS], axis=0),
+                        jnp.concatenate(parts[i][1:], axis=0),
+                    ],
+                    axis=1,
+                )
+                mixed.append(jnp.dot(window, mats[base + i], preferred_element_type=F32))
+            found = []
+            for i, at in enumerate(spots):
+                for b in range(BLOCKS):
+                    field = mixed[i][GROUP * b : GROUP * (b + 1)] + skt[at, :] * parts[i][b + 1].astype(F32)
+                    found.append((qt[b, at, :] * field).astype(BF16))
+            for i, at in enumerate(spots):
+                for b in range(BLOCKS):
+                    yt[at, SPAN * b : SPAN * (b + 1)] = found[BLOCKS * i + b]
             return carry
 
-        lax.fori_loop(lo, hi, body, 0, unroll=4)
+        lax.fori_loop(low // BATCH, high // BATCH, body, 0)
 
     def swap_y(quarter):
         at = pl.ds(quarter * (WIDTH // 4), WIDTH // 4)
@@ -338,18 +382,15 @@
     def own_wait():
         own.wait()
 
-    work(1.0, widen_all)
-    for lo in (0, 4):
-        work(1.4, features, BLOCKS - 1, (lo, lo + 4))
-    work(0.1, send_tail)
-    for lo in (0, 4):
-        work(1.4, features, 1, (lo, lo + 4))
-    work(0.3, halo_arrives)
-    for lo in (0, 4):
-        work(1.4, features, 0, (lo, lo + 4))
-    work(0.1, tail_arrives)
+    work(0.8, widen)
+    work(1.0, toeplitz, 32, 64)
+    work(0.2, halo_arrives)
     for quarter in range(4):
-        work(1.5, conv, 16 * quarter, 16 * quarter + 16)
+        work(0.9, features, 2 * quarter, 2 * quarter + 2)
+        work(0.1, send_tail, quarter)
+    for quarter in range(4):
+        work(0.1, tail_arrives, quarter)
+        work(0.8, conv, 16 * quarter, 16 * quarter + 16)
         work(0.1, send_y, quarter)
     work(0.1, own_wait)
     work(0.6, give, 0, 0)
@@ -425,11 +466,14 @@
             pltpu.VMEM((RING, 8 * PIECE, WIDTH), BF16),
             pltpu.VMEM((3, ROWS, WIDTH), BF16),
             pltpu.VMEM((3, HALO, WIDTH), BF16),
-            pltpu.VMEM((3, STRIPS, PAD + ROWS, LANES), F32),
+            pltpu.VMEM((3, STRIPS, PAD + TALL, LANES), F32),
+            pltpu.VMEM((STRIPS, TALL, LANES), F32),
+            pltpu.VMEM((STRIPS, TALL, LANES), F32),
             pltpu.VMEM((BLOCKS + 1, WIDTH, SPAN), BF16),
             pltpu.VMEM((BLOCKS, WIDTH, SPAN), F32),
             pltpu.VMEM((WIDTH, SPAN), F32),
             pltpu.VMEM((WIDTH // GROUP, SPAN), F32),
+            pltpu.VMEM((WIDTH // GROUP, 2 * SPAN, SPAN), BF16),
             pltpu.VMEM((WIDTH, ROWS), BF16),
             pltpu.VMEM((WIDTH, ROWS), BF16),
             pltpu.VMEM((2, RING * HALF, ROWS), BF16),
@@ -439,7 +483,7 @@
             pltpu.VMEM((2 * HALF, ROWS), BF16),
             pltpu.VMEM((2 * HALF, ROWS), BF16),
             pltpu.VMEM((512, ROWS), F32),
-            dma((6,)), dma, dma((2,)), dma((2,)),
+            dma((6,)), dma, dma((2,)), dma((2, 4)),
             dma((2,)), dma((2, RING)), dma((2, RING)),
             dma((2, 4, 4)), dma((2, 4, 4)), dma((4,)), dma((4,)),
             dma((2, 5)), dma((2, 5)), dma((2, RING)), dma((2, 4, 2)), dma((2,)),

time: 90.3 us -> 91.6 us (1.014)
  the two profiles are of different devices: /device:TPU:4 before, /device:TPU:68 now
where the time goes in v4:
time: 91.6 us; the launch traced here: 91.5 us
  Pallas kernels  89.7 us (98%)
  local copies, waits for them, and re-layouts  1.77 us (2%)
    pallas_call x1, Pallas kernels, local(): pl.pallas_call(kernel, out_shape=jax.ShapeDtypeStruct((ROWS, 512), BF16),...  89.7 us

profile of v4, /device:TPU:68, one launch (start us, length us, event | category | flops | bytes accessed | tf_op | source)
XLA Modules:
  0.0 91.5 jit_solution(17285986213368985472)
XLA Ops:
  0.0 89.7 %shard_map.55 = bf16[384,512]{1,0:T(8,128)(2,1)} custom-call(bf16[3,384,1024]{2,1,0:T(8,128)(2,1)} %qkv_ref.1, f32[3,7,1024]{2,1,0:T(8,128)} %taps_hbm.1, bf16[64,128]{1,0:T(8,128)(2,1)} %bitcast.4, f32[1,1024]{1,0:T(1,128)} %bitcast.5, bf16[64,1024]{1,0:T(8,128)(2,1)} %bitcast.3), custom_call_target="tpu_custom_call" | custom-call | tf_op jit(solution)/shard_map/pallas_call | solution.py:457
  89.7 1.8 %copy.7 = bf16[384,512]{1,0:T(8,128)(2,1)} copy(bf16[384,512]{1,0:T(8,128)(2,1)} %shard_map.55) | data formatting | bytes 786432

commit v5 on v4

v5 whole, which is shorter than its diff:
```python
import jax
import jax.numpy as jnp
from jax import lax
from jax.experimental import pallas as pl
from jax.experimental.pallas import tpu as pltpu
from jax.sharding import PartitionSpec as P

MESH = pl.DeviceIdType.MESH
F32 = jnp.float32
BF16 = jnp.bfloat16

RING = 8
GROUP = 16
SPAN = 128
FTAPS = 7
ROWS = 384
WIDTH = 1024
BLOCKS = ROWS // SPAN
LANES = 128
STRIPS = WIDTH // LANES
PIECE = 32
HALO = 16
PAD = 8
PITCH = 49
SUBS = 8
TALL = PITCH * SUBS

OFF = (1, -1, 2, -2, 3, -3, 4, 0)
SLOT = {off: slot for slot, off in enumerate(OFF)}
OWN = SLOT[0]
GROUPS = ((7,), (0, 1), (2, 3), (4, 5), (6,))
NEAR, CROSS, NEAR_EXT, CROSS_EXT = (pl.ds(2 * PIECE * i, 2 * PIECE) for i in range(4))
PARTS = (NEAR, pl.ds(4 * PIECE, PIECE), CROSS, pl.ds(6 * PIECE, PIECE))
HALF = 4 * PIECE
BATCH = 8
JOBS = 16


def origin(direction, step):
    return SLOT[4 if step == 4 else -direction * step]


def kernel(
    qkv_ref, taps_hbm, filt_hbm, skip_hbm, w_ref, out_ref,
    taps_ref, filt_ref, skip_ref,
    w_all, qkv_v, halo, ext_v, ub, qb, ut, qt, skt, hf, mats, y2,
    ta, sa, qa, ra, qp, rp, fin,
    load_sem, own_sem, halo_sem, tail_sem,
    xs, es, er, s2, r2, ys, yr, as1, ar1, as2, ar2, ps,
):
    s = lax.axis_index("seq")
    c = lax.axis_index("chan")
    y = lax.div(s, RING)
    z = lax.rem(s, RING)
    x = lax.div(c, 2)
    p = lax.rem(c, 2)

    def y_at(d):
        return {"seq": lax.rem(y + d + RING, RING) * RING + z}

    def z_at(d):
        return {"seq": y * RING + lax.rem(z + d + 2 * RING, RING)}

    def seq_at(d):
        return {"seq": lax.rem(s + d + RING * RING, RING * RING)}

    sibling = {"chan": c + 1 - 2 * p}
    outer = 2 * lax.rem(z, 2) - 1
    inner = -outer
    started = []

    def remote(src, dst, send, recv, to):
        return pltpu.make_async_remote_copy(
            src_ref=src, dst_ref=dst, send_sem=send, recv_sem=recv, device_id=to, device_id_type=MESH
        )

    def go(make, *args):
        make(*args).start()
        if (make, args) not in started:
            started.append((make, args))

    loads = [
        pltpu.make_async_copy(qkv_ref.at[i], qkv_v.at[i], load_sem.at[i]) for i in (1, 2, 0)
    ]
    loads += [
        pltpu.make_async_copy(taps_hbm, taps_ref, load_sem.at[3]),
        pltpu.make_async_copy(skip_hbm, skip_ref, load_sem.at[5]),
        pltpu.make_async_copy(filt_hbm, filt_ref, load_sem.at[4]),
    ]
    own = pltpu.make_async_copy(w_ref, w_all.at[OWN, NEAR], own_sem)
    for copy in loads[::-1] + [own]:
        copy.start()

    barrier = pltpu.get_barrier_semaphore()
    greeted = [{"chan": lax.rem(c + d, 8)} for d in range(1, 8)]
    greeted += [z_at(outer), z_at(inner), z_at(3 * inner), y_at(1), y_at(-1), seq_at(1), seq_at(-1)]
    for to in greeted:
        pl.semaphore_signal(barrier, inc=1, device_id=to, device_id_type=MESH)

    def toeplitz():
        loads[5].wait()
        hf[...] = filt_ref[...].astype(F32)

        def body(step, carry):
            row = lax.broadcasted_iota(jnp.int32, (SPAN, SPAN), 0)
            col = lax.broadcasted_iota(jnp.int32, (SPAN, SPAN), 1)
            for i in range(4):
                g = step * 4 + i
                taps = jnp.broadcast_to(hf[pl.ds(g, 1), :], (SPAN, SPAN))
                turned = pltpu.roll(taps, 0, 1, stride=1, stride_axis=0)
                mats[g, :SPAN] = jnp.where(row > col, turned, 0.0).astype(BF16)
                mats[g, SPAN:] = jnp.where(row <= col, turned, 0.0).astype(BF16)
            return carry

        lax.fori_loop(0, 16, body, 0)

    def widen():
        for copy in loads[:5]:
            copy.wait()

        def body(strip, carry):
            at = pl.ds(pl.multiple_of(strip * LANES, LANES), LANES)
            for i in range(3):
                ext_v[i, strip, PAD : PAD + ROWS, :] = qkv_v[i, :, at].astype(F32)
                ext_v[i, strip, PAD + ROWS :, :] = jnp.zeros((TALL - ROWS, LANES), F32)
            skt[at, :] = jnp.broadcast_to(skip_ref[:, at], (LANES, LANES)).T
            return carry

        lax.fori_loop(0, STRIPS, body, 0)

    widen()
    pl.semaphore_wait(barrier, len(greeted))

    def cross():
        return remote(w_ref, w_all.at[OWN, CROSS], xs.at[0], xs.at[1], z_at(3 * inner))

    def ext(which, slot):
        src, dst = ((NEAR, NEAR_EXT), (CROSS, CROSS_EXT))[which]
        if slot != OWN:
            src, dst = [pl.ds(at.start + PIECE, PIECE) for at in (src, dst)]
        found = w_ref if slot == OWN and which == 0 else w_all.at[slot, src]
        return remote(found, w_all.at[slot, dst], es.at[which, slot], er.at[which, slot], z_at(outer))

    def ring(direction, step, part):
        lane = 0 if direction == 1 else 1
        rows = PARTS[part]
        into = origin(direction, step)
        came = OWN if step == 1 else origin(direction, step - 1)
        src = w_ref if step == 1 and part == 0 else w_all.at[came, rows]
        at = lane, step - 1, part
        return remote(src, w_all.at[into, rows], s2.at[at], r2.at[at], y_at(direction))

    def lanes_of(step, part):
        if step < 4:
            return (1, -1)
        return (1,) if part < 2 else (-1,)

    def start_part(part):
        for direction in (1, -1):
            go(ring, direction, 1, part)

    def near_arrives():
        ext(0, OWN).wait_recv()
        start_part(1)

    def cross_arrives():
        cross().wait_recv()
        start_part(2)
        go(ext, 1, OWN)

    def cross_ext_arrives():
        ext(1, OWN).wait_recv()
        start_part(3)

    def part_arrives(step, part):
        for direction in lanes_of(step, part):
            ring(direction, step, part).wait_recv()
            if step < 4 and direction in lanes_of(step + 1, part):
                go(ring, direction, step + 1, part)
            if part in (0, 2):
                go(ext, part // 2, origin(direction, step))

    def settle(step):
        for slot in GROUPS[step]:
            for which in range(2):
                ext(which, slot).wait_recv()

    def happen(step, table):
        for at, calls in table.items():
            @pl.when(step == at)
            def run(calls=calls):
                for fn, *args in calls:
                    fn(*args)

    def halo_copy():
        return remote(
            qkv_ref.at[:, ROWS - HALO : ROWS], halo, halo_sem.at[0], halo_sem.at[1], seq_at(1)
        )

    go(cross)
    go(ext, 0, OWN)
    start_part(0)
    go(halo_copy)
    toeplitz()
    near_arrives()

    def halo_arrives():
        halo_copy().wait_recv()

        def body(strip, carry):
            at = pl.ds(pl.multiple_of(strip * LANES, LANES), LANES)
            for i in range(3):
                before = halo[i, :, at].astype(F32)[HALO - PAD :]
                ext_v[i, strip, :PAD, :] = jnp.where(s == 0, 0.0, before)
            return carry

        lax.fori_loop(0, STRIPS, body, 0)

    def features(strip):
        at = pl.ds(pl.multiple_of(strip * LANES, LANES), LANES)
        taps = [
            [jnp.broadcast_to(taps_ref[i, j : j + 1, at], (SUBS, LANES)) for j in range(FTAPS)]
            for i in range(3)
        ]

        def load(i, r):
            return ext_v[i, strip, pl.ds(PAD + r, SUBS, stride=PITCH), :]

        def line(i, window):
            total = taps[i][0] * window[-1]
            for j in range(1, FTAPS):
                total = total + taps[i][j] * window[-1 - j]
            return total

        def some(turn, windows):
            windows = [list(w) for w in windows]
            for step in range(FTAPS):
                r = turn * FTAPS + step
                found = []
                for i in range(3):
                    windows[i] = windows[i][1 - FTAPS :] + [load(i, r)]
                    found.append(line(i, windows[i]))
                ub[strip, pl.ds(r, SUBS, stride=PITCH), :] = found[1] * found[2]
                qb[strip, pl.ds(r, SUBS, stride=PITCH), :] = found[0]
            return tuple(tuple(w[1 - FTAPS :]) for w in windows)

        start = tuple(tuple(load(i, r) for r in range(1 - FTAPS, 0)) for i in range(3))
        lax.fori_loop(0, PITCH // FTAPS, some, start)
        for b in range(BLOCKS):
            ut[b + 1, at, :] = ub[strip, SPAN * b : SPAN * (b + 1), :].T.astype(BF16)
            qt[b, at, :] = qb[strip, SPAN * b : SPAN * (b + 1), :].T

    def tail(quarter):
        at = pl.ds(pl.multiple_of(quarter * (WIDTH // 4), WIDTH // 4), WIDTH // 4)
        return remote(
            ut.at[BLOCKS, at], ut.at[0, at], tail_sem.at[0, quarter], tail_sem.at[1, quarter], seq_at(1)
        )

    def tail_arrives(quarter):
        tail(quarter).wait_recv()

        @pl.when(s == 0)
        def clear():
            at = pl.ds(pl.multiple_of(quarter * (WIDTH // 4), WIDTH // 4), WIDTH // 4)
            ut[0, at] = jnp.zeros((WIDTH // 4, SPAN), BF16)

    def conv(quarter):
        def body(step, carry):
            base = step * BATCH
            spots = [pl.ds(pl.multiple_of((base + i) * GROUP, GROUP), GROUP) for i in range(BATCH)]
            parts = [[ut[b, at, :] for b in range(BLOCKS + 1)] for at in spots]
            mixed = []
            for i in range(BATCH):
                window = jnp.concatenate(
                    [
                        jnp.concatenate(parts[i][:BLOCKS], axis=0),
                        jnp.concatenate(parts[i][1:], axis=0),
                    ],
                    axis=1,
                )
                mixed.append(jnp.dot(window, mats[base + i], preferred_element_type=F32))
            found = []
            for i, at in enumerate(spots):
                for b in range(BLOCKS):
                    field = mixed[i][GROUP * b : GROUP * (b + 1)] + skt[at, :] * parts[i][b + 1].astype(F32)
                    found.append((qt[b, at, :] * field).astype(BF16))
            for i, at in enumerate(spots):
                for b in range(BLOCKS):
                    y2[0, at, SPAN * b : SPAN * (b + 1)] = found[BLOCKS * i + b]
            return carry

        lax.fori_loop(quarter * 2, quarter * 2 + 2, body, 0)

    def swap_y(quarter):
        at = pl.ds(pl.multiple_of(quarter * (WIDTH // 4), WIDTH // 4), WIDTH // 4)
        return remote(y2.at[0, at], y2.at[1, at], ys.at[quarter], yr.at[quarter], z_at(inner))

    def slot_of(job):
        late = lax.div(job - 10, 2) + 4
        return jnp.where(job >= 10, late, lax.rem(lax.rem(job, 5) + 7, RING))

    def tokens_of(job):
        late = 1 - lax.rem(job, 2)
        return jnp.where(job >= 10, late, jnp.where(job >= 5, 1, 0))

    def target_of(job):
        slot = slot_of(job)
        off = (lax.div(slot, 2) + 1) * (1 - 2 * lax.rem(slot, 2))
        return lax.rem(y + jnp.where(slot == OWN, 0, off) + RING, RING)

    def project(job, half):
        rows = w_all[slot_of(job), pl.ds(pl.multiple_of(half * HALF, HALF), HALF)]
        return jnp.dot(rows, y2[tokens_of(job)], preferred_element_type=F32)

    def swap(job):
        return remote(ta.at[job], sa.at[job], as1.at[job], ar1.at[job], sibling)

    def give(job):
        ta[job] = project(job, 1 - p).astype(BF16)
        swap(job).start()

    def delivery(job):
        tokens = tokens_of(job)
        return remote(
            qa.at[job], ra.at[tokens, x, p], as2.at[job], ar2.at[tokens, x, p], {"chan": target_of(job)}
        )

    def take(job):
        got = project(job, p)
        swap(job).wait_recv()
        qa[job] = (got + sa[job].astype(F32)).astype(BF16)
        to, tokens = target_of(job), tokens_of(job)

        @pl.when(to == c)
        def keep():
            pltpu.make_async_copy(qa.at[job], ra.at[tokens, x, p], ar2.at[tokens, x, p]).start()

        @pl.when(to != c)
        def post():
            delivery(job).start()

    def gathered(tokens, half):
        found = None
        for chip in range(4):
            here = ra.at[tokens, chip, half]
            remote(here, here, as2.at[0], ar2.at[tokens, chip, half], sibling).wait_recv()
        for chip in range(4):
            term = ra[tokens, chip, half].astype(F32)
            found = term if found is None else found + term
        return found

    def hand():
        return remote(qp, rp, ps.at[0], ps.at[1], z_at(inner))

    ahead = lax.rem(c - y + RING, RING)
    my_group = jnp.minimum(ahead, RING - ahead)
    ready = jnp.where(my_group <= 1, 13, jnp.where(my_group == 2, 14, jnp.where(my_group == 3, 17, 18)))

    def finish():
        for half in range(2):
            qp[half * HALF : (half + 1) * HALF] = gathered(1, half).astype(BF16)
        hand().start()

    def partner_y():
        for quarter in range(4):
            swap_y(quarter).wait_recv()

    halo_arrives()
    cross_arrives()

    def feature_quarter(quarter, carry):
        lax.fori_loop(quarter * 2, quarter * 2 + 2, lambda strip, carry: (features(strip), carry)[1], 0)
        tail(quarter).start()
        happen(quarter, {
            0: [(part_arrives, 1, 0)],
            1: [(cross_ext_arrives,), (part_arrives, 1, 1)],
            2: [(part_arrives, 1, 2)],
            3: [(part_arrives, 1, 3)],
        })
        return carry

    lax.fori_loop(0, 4, feature_quarter, 0)

    def conv_quarter(quarter, carry):
        tail_arrives(quarter)
        conv(quarter)
        swap_y(quarter).start()
        happen(quarter, {2: [(part_arrives, 2, 0)], 3: [(part_arrives, 2, 1)]})
        return carry

    lax.fori_loop(0, 4, conv_quarter, 0)
    own.wait()

    def turn(n, carry):
        @pl.when((n >= 2) & (n < JOBS + 2))
        def second():
            take(n - 2)

        @pl.when(n == ready)
        def partner_sum():
            finish()

        happen(n, {
            1: [(settle, 1)],
            2: [(part_arrives, 2, 2), (part_arrives, 2, 3)],
            3: [(settle, 2)],
            5: [(partner_y,), (part_arrives, 3, 0)],
            6: [(part_arrives, 3, 1)],
            7: [(part_arrives, 3, 2)],
            8: [(part_arrives, 3, 3)],
            10: [(settle, 3)],
            11: [(part_arrives, 4, 0)],
            12: [(part_arrives, 4, 1), (part_arrives, 4, 2)],
            13: [(part_arrives, 4, 3)],
            14: [(settle, 4)],
        })

        @pl.when(n < JOBS)
        def first():
            give(n)

        return carry

    lax.fori_loop(0, JOBS + 3, turn, 0)

    def place(z_from, rows):
        at = lax.rem(z + z_from + 2 * RING, RING) * (2 * PIECE)
        fin[pl.ds(pl.multiple_of(at, 2 * PIECE), 2 * PIECE), :] = rows

    for half in range(2):
        found = gathered(0, half)
        for i, z_from in enumerate(((0, outer + 4), (outer, 4))[half]):
            place(z_from, found[2 * PIECE * i : 2 * PIECE * (i + 1)])
    hand().wait_recv()
    for i, z_from in enumerate((inner, 2 * inner + 4, 2 * inner, inner + 4)):
        place(z_from, rp[2 * PIECE * i : 2 * PIECE * (i + 1)].astype(F32))
    for a in range(BLOCKS):
        for n in range(4):
            tile = fin[LANES * n : LANES * (n + 1), SPAN * a : SPAN * (a + 1)]
            out_ref[SPAN * a : SPAN * (a + 1), LANES * n : LANES * (n + 1)] = tile.T.astype(BF16)

    for make, args in started:
        make(*args).wait_send()
    hand().wait_send()

    def drain_quarter(quarter, carry):
        tail(quarter).wait_send()
        swap_y(quarter).wait_send()
        return carry

    lax.fori_loop(0, 4, drain_quarter, 0)

    def drain(job, carry):
        swap(job).wait_send()

        @pl.when(target_of(job) != c)
        def sent():
            delivery(job).wait_send()

        return carry

    lax.fori_loop(0, JOBS, drain, 0)


def local(qkv, feat_taps, long_filter, skip_gain, out_weight):
    vmem = pl.BlockSpec(memory_space=pltpu.VMEM)
    anywhere = pl.BlockSpec(memory_space=pl.ANY)
    dma = pltpu.SemaphoreType.DMA
    return pl.pallas_call(
        kernel,
        out_shape=jax.ShapeDtypeStruct((ROWS, 512), BF16),
        in_specs=[anywhere] * 5,
        out_specs=vmem,
        scratch_shapes=[
            pltpu.VMEM((3, FTAPS, WIDTH), F32),
            pltpu.VMEM((WIDTH // GROUP, SPAN), BF16),
            pltpu.VMEM((1, WIDTH), F32),
            pltpu.VMEM((RING, 8 * PIECE, WIDTH), BF16),
            pltpu.VMEM((3, ROWS, WIDTH), BF16),
            pltpu.VMEM((3, HALO, WIDTH), BF16),
            pltpu.VMEM((3, STRIPS, PAD + TALL, LANES), F32),
            pltpu.VMEM((STRIPS, TALL, LANES), F32),
            pltpu.VMEM((STRIPS, TALL, LANES), F32),
            pltpu.VMEM((BLOCKS + 1, WIDTH, SPAN), BF16),
            pltpu.VMEM((BLOCKS, WIDTH, SPAN), F32),
            pltpu.VMEM((WIDTH, SPAN), F32),
            pltpu.VMEM((WIDTH // GROUP, SPAN), F32),
            pltpu.VMEM((WIDTH // GROUP, 2 * SPAN, SPAN), BF16),
            pltpu.VMEM((2, WIDTH, ROWS), BF16),
            pltpu.VMEM((JOBS, HALF, ROWS), BF16),
            pltpu.VMEM((JOBS, HALF, ROWS), BF16),
            pltpu.VMEM((JOBS, HALF, ROWS), BF16),
            pltpu.VMEM((2, 4, 2, HALF, ROWS), BF16),
            pltpu.VMEM((2 * HALF, ROWS), BF16),
            pltpu.VMEM((2 * HALF, ROWS), BF16),
            pltpu.VMEM((512, ROWS), F32),
            dma((6,)), dma, dma((2,)), dma((2, 4)),
            dma((2,)), dma((2, RING)), dma((2, RING)),
            dma((2, 4, 4)), dma((2, 4, 4)), dma((4,)), dma((4,)),
            dma((JOBS,)), dma((JOBS,)), dma((JOBS,)), dma((2, 4, 2)), dma((2,)),
        ],
        compiler_params=pltpu.CompilerParams(
            collective_id=0, has_side_effects=True, vmem_limit_bytes=56 * 2**20
        ),
    )(qkv, feat_taps, long_filter.T, skip_gain.reshape(1, WIDTH), out_weight.T)


def solution(mesh):
    return jax.shard_map(
        local,
        mesh=mesh,
        in_specs=(
            P(None, "seq", "chan"),
            P(None, None, "chan"),
            P(None, "chan"),
            P("chan"),
            P("chan", "seq"),
        ),
        out_specs=P("seq", "chan"),
        check_vma=False,
    )
```

time: 91.6 us -> 90.1 us (0.984)
  Pallas kernels: 89.7 us -> 88.1 us
    pallas_call x1, Pallas kernels: 89.7 us -> 88.1 us  [local(): pl.pallas_call(kernel, out_shape=jax.ShapeDtypeStruct((ROWS, 512), BF16),...]
where the time goes in v5:
time: 90.1 us; the launch traced here: 89.9 us
  Pallas kernels  88.1 us (98%)
  local copies, waits for them, and re-layouts  1.77 us (2%)
    pallas_call x1, Pallas kernels, local(): pl.pallas_call(kernel, out_shape=jax.ShapeDtypeStruct((ROWS, 512), BF16),...  88.1 us

profile of v5, /device:TPU:68, one launch (start us, length us, event | category | flops | bytes accessed | tf_op | source)
XLA Modules:
  0.0 89.9 jit_solution(16904028161389001752)
XLA Ops:
  0.0 88.1 %shard_map.55 = bf16[384,512]{1,0:T(8,128)(2,1)} custom-call(bf16[3,384,1024]{2,1,0:T(8,128)(2,1)} %qkv_ref.1, f32[3,7,1024]{2,1,0:T(8,128)} %taps_hbm.1, bf16[64,128]{1,0:T(8,128)(2,1)} %bitcast.4, f32[1,1024]{1,0:T(1,128)} %bitcast.5, bf16[64,1024]{1,0:T(8,128)(2,1)} %bitcast.3), custom_call_target="tpu_custom_call" | custom-call | tf_op jit(solution)/shard_map/pallas_call | solution.py:469
  88.1 1.8 %copy.7 = bf16[384,512]{1,0:T(8,128)(2,1)} copy(bf16[384,512]{1,0:T(8,128)(2,1)} %shard_map.55) | data formatting | bytes 786432

commit v6 on v5

--- a/solution.py
+++ b/solution.py
@@ -25,15 +25,16 @@
 SUBS = 8
 TALL = PITCH * SUBS
 
-OFF = (1, -1, 2, -2, 3, -3, 4, 0)
+OFF = (0, 1, -1, 2, -2, 3, -3, 4)
 SLOT = {off: slot for slot, off in enumerate(OFF)}
 OWN = SLOT[0]
-GROUPS = ((7,), (0, 1), (2, 3), (4, 5), (6,))
+GROUPS = ((0,), (1, 2), (3, 4), (5, 6), (7,))
 NEAR, CROSS, NEAR_EXT, CROSS_EXT = (pl.ds(2 * PIECE * i, 2 * PIECE) for i in range(4))
 PARTS = (NEAR, pl.ds(4 * PIECE, PIECE), CROSS, pl.ds(6 * PIECE, PIECE))
 HALF = 4 * PIECE
 BATCH = 8
-JOBS = 16
+JOBS = 8
+CHIPS = 4
 
 
 def origin(direction, step):
@@ -44,9 +45,9 @@
     qkv_ref, taps_hbm, filt_hbm, skip_hbm, w_ref, out_ref,
     taps_ref, filt_ref, skip_ref,
     w_all, qkv_v, halo, ext_v, ub, qb, ut, qt, skt, hf, mats, y2,
-    ta, sa, qa, ra, qp, rp, fin,
+    ta, sa, qa, rb, oa,
     load_sem, own_sem, halo_sem, tail_sem,
-    xs, es, er, s2, r2, ys, yr, as1, ar1, as2, ar2, ps,
+    xs, es, er, s2, r2, ys, yr, as1, ar1, bs, br, cs, cr,
 ):
     s = lax.axis_index("seq")
     c = lax.axis_index("chan")
@@ -93,7 +94,8 @@
 
     barrier = pltpu.get_barrier_semaphore()
     greeted = [{"chan": lax.rem(c + d, 8)} for d in range(1, 8)]
-    greeted += [z_at(outer), z_at(inner), z_at(3 * inner), y_at(1), y_at(-1), seq_at(1), seq_at(-1)]
+    greeted += [z_at(outer), z_at(3 * inner), y_at(1), y_at(-1), seq_at(1), seq_at(-1)]
+    greeted += [{**z_at(inner), "chan": lax.rem(c + d, 8)} for d in range(8)]
     for to in greeted:
         pl.semaphore_signal(barrier, inc=1, device_id=to, device_id_type=MESH)
 
@@ -295,22 +297,12 @@
         at = pl.ds(pl.multiple_of(quarter * (WIDTH // 4), WIDTH // 4), WIDTH // 4)
         return remote(y2.at[0, at], y2.at[1, at], ys.at[quarter], yr.at[quarter], z_at(inner))
 
-    def slot_of(job):
-        late = lax.div(job - 10, 2) + 4
-        return jnp.where(job >= 10, late, lax.rem(lax.rem(job, 5) + 7, RING))
-
-    def tokens_of(job):
-        late = 1 - lax.rem(job, 2)
-        return jnp.where(job >= 10, late, jnp.where(job >= 5, 1, 0))
-
-    def target_of(job):
-        slot = slot_of(job)
-        off = (lax.div(slot, 2) + 1) * (1 - 2 * lax.rem(slot, 2))
-        return lax.rem(y + jnp.where(slot == OWN, 0, off) + RING, RING)
-
     def project(job, half):
-        rows = w_all[slot_of(job), pl.ds(pl.multiple_of(half * HALF, HALF), HALF)]
-        return jnp.dot(rows, y2[tokens_of(job)], preferred_element_type=F32)
+        pair = lax.rem(job, 4)
+        rows = w_all[pl.ds(2 * pair, 2), pl.ds(pl.multiple_of(half * HALF, HALF), HALF)]
+        return jnp.dot(
+            rows.reshape(2 * HALF, WIDTH), y2[lax.div(job, 4)], preferred_element_type=F32
+        )
 
     def swap(job):
         return remote(ta.at[job], sa.at[job], as1.at[job], ar1.at[job], sibling)
@@ -319,47 +311,62 @@
         ta[job] = project(job, 1 - p).astype(BF16)
         swap(job).start()
 
-    def delivery(job):
-        tokens = tokens_of(job)
+    def scatter(job, step):
+        to = lax.rem(x + step, CHIPS)
         return remote(
-            qa.at[job], ra.at[tokens, x, p], as2.at[job], ar2.at[tokens, x, p], {"chan": target_of(job)}
+            qa.at[job, to], rb.at[job, step - 1], bs.at[job, step - 1], br.at[job, step - 1],
+            {"chan": 2 * to + p},
         )
 
     def take(job):
         got = project(job, p)
         swap(job).wait_recv()
-        qa[job] = (got + sa[job].astype(F32)).astype(BF16)
-        to, tokens = target_of(job), tokens_of(job)
-
-        @pl.when(to == c)
-        def keep():
-            pltpu.make_async_copy(qa.at[job], ra.at[tokens, x, p], ar2.at[tokens, x, p]).start()
-
-        @pl.when(to != c)
-        def post():
-            delivery(job).start()
-
-    def gathered(tokens, half):
-        found = None
-        for chip in range(4):
-            here = ra.at[tokens, chip, half]
-            remote(here, here, as2.at[0], ar2.at[tokens, chip, half], sibling).wait_recv()
-        for chip in range(4):
-            term = ra[tokens, chip, half].astype(F32)
-            found = term if found is None else found + term
-        return found
-
-    def hand():
-        return remote(qp, rp, ps.at[0], ps.at[1], z_at(inner))
-
-    ahead = lax.rem(c - y + RING, RING)
-    my_group = jnp.minimum(ahead, RING - ahead)
-    ready = jnp.where(my_group <= 1, 13, jnp.where(my_group == 2, 14, jnp.where(my_group == 3, 17, 18)))
-
-    def finish():
-        for half in range(2):
-            qp[half * HALF : (half + 1) * HALF] = gathered(1, half).astype(BF16)
-        hand().start()
+        got = (got + sa[job].astype(F32)).astype(BF16)
+        for i in range(2):
+            for chip in range(CHIPS):
+                at = HALF * i + PIECE * chip
+                qa[job, chip, PIECE * i : PIECE * (i + 1)] = got[at : at + PIECE]
+        for step in (2, 1, 3):
+            scatter(job, step).start()
+
+    def columns(z_here, outer_here, chip, core):
+        first = jnp.where(core == 0, 0, outer_here)
+        second = jnp.where(core == 0, outer_here + 4, 4)
+        shard = lax.rem(z_here + jnp.where(chip < 2, first, second) + 2 * RING, RING)
+        at = shard * (2 * PIECE) + lax.rem(chip, 2) * PIECE
+        return out_ref.at[pl.ds(pl.multiple_of(at, PIECE), PIECE)]
+
+    def target_of(job, i):
+        slot = 2 * lax.rem(job, 4) + i
+        off = lax.div(slot + 1, 2) * (2 * lax.rem(slot, 2) - 1)
+        return lax.rem(y + off + RING, RING)
+
+    def delivery(job, i):
+        tokens = lax.div(job, 4)
+        to = {"seq": y * RING + lax.rem(z + tokens * inner + RING, RING), "chan": target_of(job, i)}
+        return remote(
+            oa.at[job, i], columns(z, outer, x, p), cs.at[job, i], cr.at[tokens, x, p], to
+        )
+
+    def stays(job, i):
+        return (job < 4) & (target_of(job, i) == c)
+
+    def reduce(job):
+        total = qa[job, x].astype(F32)
+        for step in (1, 3, 2):
+            scatter(job, step).wait_recv()
+            total = total + rb[job, step - 1].astype(F32)
+        total = total.astype(BF16)
+        for i in range(2):
+            oa[job, i] = total[PIECE * i : PIECE * (i + 1)]
+        for i in range(2):
+            @pl.when(stays(job, i))
+            def keep():
+                pltpu.make_async_copy(oa.at[job, i], columns(z, outer, x, p), cr.at[0, x, p]).start()
+
+            @pl.when(jnp.logical_not(stays(job, i)))
+            def post():
+                delivery(job, i).start()
 
     def partner_y():
         for quarter in range(4):
@@ -368,51 +375,47 @@
     halo_arrives()
     cross_arrives()
 
-    def feature_quarter(quarter, carry):
-        lax.fori_loop(quarter * 2, quarter * 2 + 2, lambda strip, carry: (features(strip), carry)[1], 0)
-        tail(quarter).start()
-        happen(quarter, {
+    def quarters(n, carry):
+        @pl.when(n < 4)
+        def feature_quarter():
+            lax.fori_loop(n * 2, n * 2 + 2, lambda strip, carry: (features(strip), carry)[1], 0)
+            tail(n).start()
+
+        happen(n, {
             0: [(part_arrives, 1, 0)],
             1: [(cross_ext_arrives,), (part_arrives, 1, 1)],
             2: [(part_arrives, 1, 2)],
             3: [(part_arrives, 1, 3)],
+            4: [(part_arrives, 2, 0)],
+            5: [(part_arrives, 2, 1)],
         })
+
+        @pl.when(n >= 2)
+        def conv_quarter():
+            tail_arrives(n - 2)
+            conv(n - 2)
+            swap_y(n - 2).start()
+
         return carry
 
-    lax.fori_loop(0, 4, feature_quarter, 0)
-
-    def conv_quarter(quarter, carry):
-        tail_arrives(quarter)
-        conv(quarter)
-        swap_y(quarter).start()
-        happen(quarter, {2: [(part_arrives, 2, 0)], 3: [(part_arrives, 2, 1)]})
-        return carry
-
-    lax.fori_loop(0, 4, conv_quarter, 0)
+    lax.fori_loop(0, 6, quarters, 0)
     own.wait()
 
     def turn(n, carry):
-        @pl.when((n >= 2) & (n < JOBS + 2))
+        @pl.when((n >= 1) & (n < JOBS + 1))
         def second():
-            take(n - 2)
-
-        @pl.when(n == ready)
-        def partner_sum():
-            finish()
+            take(n - 1)
+
+        @pl.when(n >= 3)
+        def third():
+            reduce(n - 3)
 
         happen(n, {
-            1: [(settle, 1)],
-            2: [(part_arrives, 2, 2), (part_arrives, 2, 3)],
-            3: [(settle, 2)],
-            5: [(partner_y,), (part_arrives, 3, 0)],
-            6: [(part_arrives, 3, 1)],
-            7: [(part_arrives, 3, 2)],
-            8: [(part_arrives, 3, 3)],
-            10: [(settle, 3)],
-            11: [(part_arrives, 4, 0)],
-            12: [(part_arrives, 4, 1), (part_arrives, 4, 2)],
-            13: [(part_arrives, 4, 3)],
-            14: [(settle, 4)],
+            0: [(part_arrives, 2, 2), (settle, 1)],
+            1: [(part_arrives, 2, 3), (settle, 2)],
+            2: [(part_arrives, 3, part) for part in range(4)] + [(settle, 3)],
+            3: [(part_arrives, 4, part) for part in range(4)] + [(settle, 4)],
+            4: [(partner_y,)],
         })
 
         @pl.when(n < JOBS)
@@ -423,25 +426,14 @@
 
     lax.fori_loop(0, JOBS + 3, turn, 0)
 
-    def place(z_from, rows):
-        at = lax.rem(z + z_from + 2 * RING, RING) * (2 * PIECE)
-        fin[pl.ds(pl.multiple_of(at, 2 * PIECE), 2 * PIECE), :] = rows
-
-    for half in range(2):
-        found = gathered(0, half)
-        for i, z_from in enumerate(((0, outer + 4), (outer, 4))[half]):
-            place(z_from, found[2 * PIECE * i : 2 * PIECE * (i + 1)])
-    hand().wait_recv()
-    for i, z_from in enumerate((inner, 2 * inner + 4, 2 * inner, inner + 4)):
-        place(z_from, rp[2 * PIECE * i : 2 * PIECE * (i + 1)].astype(F32))
-    for a in range(BLOCKS):
-        for n in range(4):
-            tile = fin[LANES * n : LANES * (n + 1), SPAN * a : SPAN * (a + 1)]
-            out_ref[SPAN * a : SPAN * (a + 1), LANES * n : LANES * (n + 1)] = tile.T.astype(BF16)
+    for core in range(2):
+        for chip in range(CHIPS):
+            for tokens in range(2):
+                here = columns(z + tokens * inner, outer * (1 - 2 * tokens), chip, core)
+                remote(oa.at[0, 0], here, cs.at[0, 0], cr.at[tokens, chip, core], sibling).wait_recv()
 
     for make, args in started:
         make(*args).wait_send()
-    hand().wait_send()
 
     def drain_quarter(quarter, carry):
         tail(quarter).wait_send()
@@ -452,10 +444,12 @@
 
     def drain(job, carry):
         swap(job).wait_send()
-
-        @pl.when(target_of(job) != c)
-        def sent():
-            delivery(job).wait_send()
+        for step in (1, 2, 3):
+            scatter(job, step).wait_send()
+        for i in range(2):
+            @pl.when(jnp.logical_not(stays(job, i)))
+            def sent():
+                delivery(job, i).wait_send()
 
         return carry
 
@@ -463,14 +457,13 @@
 
 
 def local(qkv, feat_taps, long_filter, skip_gain, out_weight):
-    vmem = pl.BlockSpec(memory_space=pltpu.VMEM)
     anywhere = pl.BlockSpec(memory_space=pl.ANY)
     dma = pltpu.SemaphoreType.DMA
     return pl.pallas_call(
         kernel,
-        out_shape=jax.ShapeDtypeStruct((ROWS, 512), BF16),
+        out_shape=jax.ShapeDtypeStruct((512, ROWS), BF16),
         in_specs=[anywhere] * 5,
-        out_specs=vmem,
+        out_specs=anywhere,
         scratch_shapes=[
             pltpu.VMEM((3, FTAPS, WIDTH), F32),
             pltpu.VMEM((WIDTH // GROUP, SPAN), BF16),
@@ -487,22 +480,21 @@
             pltpu.VMEM((WIDTH // GROUP, SPAN), F32),
             pltpu.VMEM((WIDTH // GROUP, 2 * SPAN, SPAN), BF16),
             pltpu.VMEM((2, WIDTH, ROWS), BF16),
-            pltpu.VMEM((JOBS, HALF, ROWS), BF16),
-            pltpu.VMEM((JOBS, HALF, ROWS), BF16),
-            pltpu.VMEM((JOBS, HALF, ROWS), BF16),
-            pltpu.VMEM((2, 4, 2, HALF, ROWS), BF16),
-            pltpu.VMEM((2 * HALF, ROWS), BF16),
-            pltpu.VMEM((2 * HALF, ROWS), BF16),
-            pltpu.VMEM((512, ROWS), F32),
+            pltpu.VMEM((JOBS, 2 * HALF, ROWS), BF16),
+            pltpu.VMEM((JOBS, 2 * HALF, ROWS), BF16),
+            pltpu.VMEM((JOBS, CHIPS, 2 * PIECE, ROWS), BF16),
+            pltpu.VMEM((JOBS, CHIPS - 1, 2 * PIECE, ROWS), BF16),
+            pltpu.VMEM((JOBS, 2, PIECE, ROWS), BF16),
             dma((6,)), dma, dma((2,)), dma((2, 4)),
             dma((2,)), dma((2, RING)), dma((2, RING)),
             dma((2, 4, 4)), dma((2, 4, 4)), dma((4,)), dma((4,)),
-            dma((JOBS,)), dma((JOBS,)), dma((JOBS,)), dma((2, 4, 2)), dma((2,)),
+            dma((JOBS,)), dma((JOBS,)), dma((JOBS, CHIPS - 1)), dma((JOBS, CHIPS - 1)),
+            dma((JOBS, 2)), dma((2, CHIPS, 2)),
         ],
         compiler_params=pltpu.CompilerParams(
             collective_id=0, has_side_effects=True, vmem_limit_bytes=56 * 2**20
         ),
-    )(qkv, feat_taps, long_filter.T, skip_gain.reshape(1, WIDTH), out_weight.T)
+    )(qkv, feat_taps, long_filter.T, skip_gain.reshape(1, WIDTH), out_weight.T).T
 
 
 def solution(mesh):

time: 90.1 us -> 89.3 us (level)
  the two profiles are of different devices: /device:TPU:68 before, /device:TPU:67 now
where the time goes in v6:
time: 89.3 us; the launch traced here: 89.2 us
  Pallas kernels  87.2 us (98%)
  local copies, waits for them, and re-layouts  1.92 us (2%)
    pallas_call x1, Pallas kernels, local(): pl.pallas_call(kernel, out_shape=jax.ShapeDtypeStruct((512, ROWS), BF16),...  87.2 us
    transpose x1, local copies, waits for them, and re-layouts, local(): return pl.pallas_call(kernel, out_shape=jax.ShapeDtypeStruct((512, ROWS),...  1.92 us

profile of v6, /device:TPU:67, one launch (start us, length us, event | category | flops | bytes accessed | tf_op | source)
XLA Modules:
  0.0 89.2 jit_solution(973996014669277926)
XLA Ops:
  0.0 87.2 %shard_map.55 = bf16[512,384]{1,0:T(8,128)(2,1)} custom-call(bf16[3,384,1024]{2,1,0:T(8,128)(2,1)} %qkv_ref.1, f32[3,7,1024]{2,1,0:T(8,128)} %taps_hbm.1, bf16[64,128]{1,0:T(8,128)(2,1)} %bitcast.6, f32[1,1024]{1,0:T(1,128)} %bitcast.7, bf16[64,1024]{1,0:T(8,128)(2,1)} %bitcast.5), custom_call_target="tpu_custom_call" | custom-call | tf_op jit(solution)/shard_map/pallas_call | solution.py:462
  87.2 1.9 %copy.6 = bf16[384,512]{1,0:T(8,128)(2,1)} copy(bf16[384,512]{0,1:T(8,128)(2,1)} %bitcast.4) | data formatting | bytes 786432 | tf_op jit(solution)/shard_map/transpose | solution.py:497

commit v7 on v6

--- a/solution.py
+++ b/solution.py
@@ -41,45 +41,46 @@
     return SLOT[4 if step == 4 else -direction * step]
 
 
-def kernel(
-    qkv_ref, taps_hbm, filt_hbm, skip_hbm, w_ref, out_ref,
+class Place:
+    def __init__(self):
+        self.s = lax.axis_index("seq")
+        self.c = lax.axis_index("chan")
+        self.y = lax.div(self.s, RING)
+        self.z = lax.rem(self.s, RING)
+        self.x = lax.div(self.c, 2)
+        self.p = lax.rem(self.c, 2)
+
+    def y_at(self, d):
+        return {"seq": lax.rem(self.y + d + RING, RING) * RING + self.z}
+
+    def z_at(self, d):
+        return {"seq": self.y * RING + lax.rem(self.z + d + 2 * RING, RING)}
+
+    def seq_at(self, d):
+        return {"seq": lax.rem(self.s + d + RING * RING, RING * RING)}
+
+
+def remote(src, dst, send, recv, to):
+    return pltpu.make_async_remote_copy(
+        src_ref=src, dst_ref=dst, send_sem=send, recv_sem=recv, device_id=to, device_id_type=MESH
+    )
+
+
+def greet(devices):
+    barrier = pltpu.get_barrier_semaphore()
+    for to in devices:
+        pl.semaphore_signal(barrier, inc=1, device_id=to, device_id_type=MESH)
+    return barrier
+
+
+def mixer(
+    qkv_ref, taps_hbm, filt_hbm, skip_hbm, y_ref,
     taps_ref, filt_ref, skip_ref,
-    w_all, qkv_v, halo, ext_v, ub, qb, ut, qt, skt, hf, mats, y2,
-    ta, sa, qa, rb, oa,
-    load_sem, own_sem, halo_sem, tail_sem,
-    xs, es, er, s2, r2, ys, yr, as1, ar1, bs, br, cs, cr,
+    qkv_v, halo, ext_v, ub, qb, ut, qt, skt, hf, mats,
+    load_sem, halo_sem, tail_sem,
 ):
-    s = lax.axis_index("seq")
-    c = lax.axis_index("chan")
-    y = lax.div(s, RING)
-    z = lax.rem(s, RING)
-    x = lax.div(c, 2)
-    p = lax.rem(c, 2)
-
-    def y_at(d):
-        return {"seq": lax.rem(y + d + RING, RING) * RING + z}
-
-    def z_at(d):
-        return {"seq": y * RING + lax.rem(z + d + 2 * RING, RING)}
-
-    def seq_at(d):
-        return {"seq": lax.rem(s + d + RING * RING, RING * RING)}
-
-    sibling = {"chan": c + 1 - 2 * p}
-    outer = 2 * lax.rem(z, 2) - 1
-    inner = -outer
-    started = []
-
-    def remote(src, dst, send, recv, to):
-        return pltpu.make_async_remote_copy(
-            src_ref=src, dst_ref=dst, send_sem=send, recv_sem=recv, device_id=to, device_id_type=MESH
-        )
-
-    def go(make, *args):
-        make(*args).start()
-        if (make, args) not in started:
-            started.append((make, args))
-
+    place = Place()
+    s, seq_at = place.s, place.seq_at
     loads = [
         pltpu.make_async_copy(qkv_ref.at[i], qkv_v.at[i], load_sem.at[i]) for i in (1, 2, 0)
     ]
@@ -88,30 +89,32 @@
         pltpu.make_async_copy(skip_hbm, skip_ref, load_sem.at[5]),
         pltpu.make_async_copy(filt_hbm, filt_ref, load_sem.at[4]),
     ]
-    own = pltpu.make_async_copy(w_ref, w_all.at[OWN, NEAR], own_sem)
-    for copy in loads[::-1] + [own]:
+    for copy in loads[::-1]:
         copy.start()
-
-    barrier = pltpu.get_barrier_semaphore()
-    greeted = [{"chan": lax.rem(c + d, 8)} for d in range(1, 8)]
-    greeted += [z_at(outer), z_at(3 * inner), y_at(1), y_at(-1), seq_at(1), seq_at(-1)]
-    greeted += [{**z_at(inner), "chan": lax.rem(c + d, 8)} for d in range(8)]
-    for to in greeted:
-        pl.semaphore_signal(barrier, inc=1, device_id=to, device_id_type=MESH)
+    barrier = greet([seq_at(1), seq_at(-1)])
 
     def toeplitz():
         loads[5].wait()
         hf[...] = filt_ref[...].astype(F32)
 
         def body(step, carry):
-            row = lax.broadcasted_iota(jnp.int32, (SPAN, SPAN), 0)
-            col = lax.broadcasted_iota(jnp.int32, (SPAN, SPAN), 1)
+            row = lax.broadcasted_iota(jnp.int32, (SUBS, SPAN), 0)
+            col = lax.broadcasted_iota(jnp.int32, (SUBS, SPAN), 1)
             for i in range(4):
                 g = step * 4 + i
-                taps = jnp.broadcast_to(hf[pl.ds(g, 1), :], (SPAN, SPAN))
-                turned = pltpu.roll(taps, 0, 1, stride=1, stride_axis=0)
-                mats[g, :SPAN] = jnp.where(row > col, turned, 0.0).astype(BF16)
-                mats[g, SPAN:] = jnp.where(row <= col, turned, 0.0).astype(BF16)
+                base = jnp.broadcast_to(hf[pl.ds(g, 1), :], (SUBS, SPAN))
+                for bit in (1, 2, 4):
+                    base = jnp.where((row & bit) != 0, pltpu.roll(base, bit, 1), base)
+                for pair in range(SPAN // (2 * SUBS)):
+                    above, below = [], []
+                    for k in (2 * pair, 2 * pair + 1):
+                        turned = pltpu.roll(base, SUBS * k, 1) if k else base
+                        under = row + SUBS * k > col
+                        above.append(jnp.where(under, turned, 0.0))
+                        below.append(jnp.where(under, 0.0, turned))
+                    at = 2 * SUBS * pair
+                    mats[g, at : at + 2 * SUBS] = jnp.concatenate(above, axis=0).astype(BF16)
+                    mats[g, SPAN + at : SPAN + at + 2 * SUBS] = jnp.concatenate(below, axis=0).astype(BF16)
             return carry
 
         lax.fori_loop(0, 16, body, 0)
@@ -131,80 +134,15 @@
         lax.fori_loop(0, STRIPS, body, 0)
 
     widen()
-    pl.semaphore_wait(barrier, len(greeted))
-
-    def cross():
-        return remote(w_ref, w_all.at[OWN, CROSS], xs.at[0], xs.at[1], z_at(3 * inner))
-
-    def ext(which, slot):
-        src, dst = ((NEAR, NEAR_EXT), (CROSS, CROSS_EXT))[which]
-        if slot != OWN:
-            src, dst = [pl.ds(at.start + PIECE, PIECE) for at in (src, dst)]
-        found = w_ref if slot == OWN and which == 0 else w_all.at[slot, src]
-        return remote(found, w_all.at[slot, dst], es.at[which, slot], er.at[which, slot], z_at(outer))
-
-    def ring(direction, step, part):
-        lane = 0 if direction == 1 else 1
-        rows = PARTS[part]
-        into = origin(direction, step)
-        came = OWN if step == 1 else origin(direction, step - 1)
-        src = w_ref if step == 1 and part == 0 else w_all.at[came, rows]
-        at = lane, step - 1, part
-        return remote(src, w_all.at[into, rows], s2.at[at], r2.at[at], y_at(direction))
-
-    def lanes_of(step, part):
-        if step < 4:
-            return (1, -1)
-        return (1,) if part < 2 else (-1,)
-
-    def start_part(part):
-        for direction in (1, -1):
-            go(ring, direction, 1, part)
-
-    def near_arrives():
-        ext(0, OWN).wait_recv()
-        start_part(1)
-
-    def cross_arrives():
-        cross().wait_recv()
-        start_part(2)
-        go(ext, 1, OWN)
-
-    def cross_ext_arrives():
-        ext(1, OWN).wait_recv()
-        start_part(3)
-
-    def part_arrives(step, part):
-        for direction in lanes_of(step, part):
-            ring(direction, step, part).wait_recv()
-            if step < 4 and direction in lanes_of(step + 1, part):
-                go(ring, direction, step + 1, part)
-            if part in (0, 2):
-                go(ext, part // 2, origin(direction, step))
-
-    def settle(step):
-        for slot in GROUPS[step]:
-            for which in range(2):
-                ext(which, slot).wait_recv()
-
-    def happen(step, table):
-        for at, calls in table.items():
-            @pl.when(step == at)
-            def run(calls=calls):
-                for fn, *args in calls:
-                    fn(*args)
+    pl.semaphore_wait(barrier, 2)
 
     def halo_copy():
         return remote(
             qkv_ref.at[:, ROWS - HALO : ROWS], halo, halo_sem.at[0], halo_sem.at[1], seq_at(1)
         )
 
-    go(cross)
-    go(ext, 0, OWN)
-    start_part(0)
-    go(halo_copy)
+    halo_copy().start()
     toeplitz()
-    near_arrives()
 
     def halo_arrives():
         halo_copy().wait_recv()
@@ -288,14 +226,131 @@
                     found.append((qt[b, at, :] * field).astype(BF16))
             for i, at in enumerate(spots):
                 for b in range(BLOCKS):
-                    y2[0, at, SPAN * b : SPAN * (b + 1)] = found[BLOCKS * i + b]
+                    y_ref[at, SPAN * b : SPAN * (b + 1)] = found[BLOCKS * i + b]
             return carry
 
         lax.fori_loop(quarter * 2, quarter * 2 + 2, body, 0)
 
-    def swap_y(quarter):
-        at = pl.ds(pl.multiple_of(quarter * (WIDTH // 4), WIDTH // 4), WIDTH // 4)
-        return remote(y2.at[0, at], y2.at[1, at], ys.at[quarter], yr.at[quarter], z_at(inner))
+    halo_arrives()
+
+    def quarters(n, carry):
+        @pl.when(n < 4)
+        def feature_quarter():
+            lax.fori_loop(n * 2, n * 2 + 2, lambda strip, carry: (features(strip), carry)[1], 0)
+            tail(n).start()
+
+        @pl.when(n >= 2)
+        def conv_quarter():
+            tail_arrives(n - 2)
+            conv(n - 2)
+
+        return carry
+
+    lax.fori_loop(0, 6, quarters, 0)
+    halo_copy().wait_send()
+
+    def drain(quarter, carry):
+        tail(quarter).wait_send()
+        return carry
+
+    lax.fori_loop(0, 4, drain, 0)
+
+
+def projector(
+    y_ref, w_ref, out_ref,
+    w_all, y2, ta, sa, qa, rb, oa,
+    own_sem, xs, es, er, s2, r2, ys, as1, ar1, bs, br, cs, cr,
+):
+    place = Place()
+    c, y, z, x, p = place.c, place.y, place.z, place.x, place.p
+    y_at, z_at, seq_at = place.y_at, place.z_at, place.seq_at
+    sibling = {"chan": c + 1 - 2 * p}
+    outer = 2 * lax.rem(z, 2) - 1
+    inner = -outer
+    started = []
+
+    def go(make, *args):
+        make(*args).start()
+        if (make, args) not in started:
+            started.append((make, args))
+
+    own = pltpu.make_async_copy(w_ref, w_all.at[OWN, NEAR], own_sem.at[0])
+    mine = pltpu.make_async_copy(y_ref, y2.at[0], own_sem.at[1])
+    own.start()
+    mine.start()
+    greeted = [{"chan": lax.rem(c + d, 8)} for d in range(1, 8)]
+    greeted += [z_at(outer), z_at(3 * inner), y_at(1), y_at(-1)]
+    greeted += [{**z_at(inner), "chan": lax.rem(c + d, 8)} for d in range(8)]
+    pl.semaphore_wait(greet(greeted), len(greeted))
+
+    def cross():
+        return remote(w_ref, w_all.at[OWN, CROSS], xs.at[0], xs.at[1], z_at(3 * inner))
+
+    def ext(which, slot):
+        src, dst = ((NEAR, NEAR_EXT), (CROSS, CROSS_EXT))[which]
+        if slot != OWN:
+            src, dst = [pl.ds(at.start + PIECE, PIECE) for at in (src, dst)]
+        found = w_ref if slot == OWN and which == 0 else w_all.at[slot, src]
+        return remote(found, w_all.at[slot, dst], es.at[which, slot], er.at[which, slot], z_at(outer))
+
+    def ring(direction, step, part):
+        lane = 0 if direction == 1 else 1
+        rows = PARTS[part]
+        into = origin(direction, step)
+        came = OWN if step == 1 else origin(direction, step - 1)
+        src = w_ref if step == 1 and part == 0 else w_all.at[came, rows]
+        at = lane, step - 1, part
+        return remote(src, w_all.at[into, rows], s2.at[at], r2.at[at], y_at(direction))
+
+    def lanes_of(step, part):
+        if step < 4:
+            return (1, -1)
+        return (1,) if part < 2 else (-1,)
+
+    def start_part(part):
+        for direction in (1, -1):
+            go(ring, direction, 1, part)
+
+    def near_arrives():
+        ext(0, OWN).wait_recv()
+        start_part(1)
+
+    def cross_arrives():
+        cross().wait_recv()
+        start_part(2)
+        go(ext, 1, OWN)
+
+    def cross_ext_arrives():
+        ext(1, OWN).wait_recv()
+        start_part(3)
+
+    def part_arrives(step, part):
+        for direction in lanes_of(step, part):
+            ring(direction, step, part).wait_recv()
+            if step < 4 and direction in lanes_of(step + 1, part):
+                go(ring, direction, step + 1, part)
+            if part in (0, 2):
+                go(ext, part // 2, origin(direction, step))
+
+    def settle(step):
+        for slot in GROUPS[step]:
+            for which in range(2):
+                ext(which, slot).wait_recv()
+
+    def happen(step, table):
+        for at, calls in table.items():
+            @pl.when(step == at)
+            def run(calls=calls):
+                for fn, *args in calls:
+                    fn(*args)
+
+    def swap_y():
+        return remote(y_ref, y2.at[1], ys.at[0], ys.at[1], z_at(inner))
+
+    go(cross)
+    go(ext, 0, OWN)
+    start_part(0)
+    go(swap_y)
 
     def project(job, half):
         pair = lax.rem(job, 4)
@@ -368,40 +423,22 @@
             def post():
                 delivery(job, i).start()
 
-    def partner_y():
-        for quarter in range(4):
-            swap_y(quarter).wait_recv()
-
-    halo_arrives()
+    near_arrives()
     cross_arrives()
-
-    def quarters(n, carry):
-        @pl.when(n < 4)
-        def feature_quarter():
-            lax.fori_loop(n * 2, n * 2 + 2, lambda strip, carry: (features(strip), carry)[1], 0)
-            tail(n).start()
-
+    cross_ext_arrives()
+    for part in range(4):
+        part_arrives(1, part)
+    part_arrives(2, 0)
+    own.wait()
+    mine.wait()
+
+    def turn(n, carry):
         happen(n, {
-            0: [(part_arrives, 1, 0)],
-            1: [(cross_ext_arrives,), (part_arrives, 1, 1)],
-            2: [(part_arrives, 1, 2)],
-            3: [(part_arrives, 1, 3)],
-            4: [(part_arrives, 2, 0)],
-            5: [(part_arrives, 2, 1)],
+            1: [(part_arrives, 2, 1)],
+            2: [(part_arrives, 3, 1)],
+            3: [(part_arrives, 4, 1)],
         })
 
-        @pl.when(n >= 2)
-        def conv_quarter():
-            tail_arrives(n - 2)
-            conv(n - 2)
-            swap_y(n - 2).start()
-
-        return carry
-
-    lax.fori_loop(0, 6, quarters, 0)
-    own.wait()
-
-    def turn(n, carry):
         @pl.when((n >= 1) & (n < JOBS + 1))
         def second():
             take(n - 1)
@@ -411,11 +448,11 @@
             reduce(n - 3)
 
         happen(n, {
-            0: [(part_arrives, 2, 2), (settle, 1)],
-            1: [(part_arrives, 2, 3), (settle, 2)],
-            2: [(part_arrives, 3, part) for part in range(4)] + [(settle, 3)],
-            3: [(part_arrives, 4, part) for part in range(4)] + [(settle, 4)],
-            4: [(partner_y,)],
+            0: [(settle, 1)],
+            1: [(part_arrives, 2, 2), (part_arrives, 2, 3), (part_arrives, 3, 0), (settle, 2)],
+            2: [(part_arrives, 3, 2), (part_arrives, 3, 3), (part_arrives, 4, 0), (settle, 3)],
+            3: [(part_arrives, 4, 2), (part_arrives, 4, 3), (settle, 4)],
+            4: [(lambda: swap_y().wait_recv(),)],
         })
 
         @pl.when(n < JOBS)
@@ -434,13 +471,6 @@
 
     for make, args in started:
         make(*args).wait_send()
-
-    def drain_quarter(quarter, carry):
-        tail(quarter).wait_send()
-        swap_y(quarter).wait_send()
-        return carry
-
-    lax.fori_loop(0, 4, drain_quarter, 0)
 
     def drain(job, carry):
         swap(job).wait_send()
@@ -459,16 +489,16 @@
 def local(qkv, feat_taps, long_filter, skip_gain, out_weight):
     anywhere = pl.BlockSpec(memory_space=pl.ANY)
     dma = pltpu.SemaphoreType.DMA
-    return pl.pallas_call(
-        kernel,
-        out_shape=jax.ShapeDtypeStruct((512, ROWS), BF16),
-        in_specs=[anywhere] * 5,
-        out_specs=anywhere,
+    grant = 56 * 2**20
+    y = pl.pallas_call(
+        mixer,
+        out_shape=jax.ShapeDtypeStruct((WIDTH, ROWS), BF16),
+        in_specs=[anywhere] * 4,
+        out_specs=pl.BlockSpec(memory_space=pltpu.VMEM),
         scratch_shapes=[
             pltpu.VMEM((3, FTAPS, WIDTH), F32),
             pltpu.VMEM((WIDTH // GROUP, SPAN), BF16),
             pltpu.VMEM((1, WIDTH), F32),
-            pltpu.VMEM((RING, 8 * PIECE, WIDTH), BF16),
             pltpu.VMEM((3, ROWS, WIDTH), BF16),
             pltpu.VMEM((3, HALO, WIDTH), BF16),
             pltpu.VMEM((3, STRIPS, PAD + TALL, LANES), F32),
@@ -479,22 +509,34 @@
             pltpu.VMEM((WIDTH, SPAN), F32),
             pltpu.VMEM((WIDTH // GROUP, SPAN), F32),
             pltpu.VMEM((WIDTH // GROUP, 2 * SPAN, SPAN), BF16),
+            dma((6,)), dma((2,)), dma((2, 4)),
+        ],
+        compiler_params=pltpu.CompilerParams(
+            collective_id=1, has_side_effects=True, vmem_limit_bytes=grant
+        ),
+    )(qkv, feat_taps, long_filter.T, skip_gain.reshape(1, WIDTH))
+    return pl.pallas_call(
+        projector,
+        out_shape=jax.ShapeDtypeStruct((512, ROWS), BF16),
+        in_specs=[anywhere] * 2,
+        out_specs=anywhere,
+        scratch_shapes=[
+            pltpu.VMEM((RING, 8 * PIECE, WIDTH), BF16),
             pltpu.VMEM((2, WIDTH, ROWS), BF16),
             pltpu.VMEM((JOBS, 2 * HALF, ROWS), BF16),
             pltpu.VMEM((JOBS, 2 * HALF, ROWS), BF16),
             pltpu.VMEM((JOBS, CHIPS, 2 * PIECE, ROWS), BF16),
             pltpu.VMEM((JOBS, CHIPS - 1, 2 * PIECE, ROWS), BF16),
             pltpu.VMEM((JOBS, 2, PIECE, ROWS), BF16),
-            dma((6,)), dma, dma((2,)), dma((2, 4)),
-            dma((2,)), dma((2, RING)), dma((2, RING)),
-            dma((2, 4, 4)), dma((2, 4, 4)), dma((4,)), dma((4,)),
+            dma((2,)), dma((2,)), dma((2, RING)), dma((2, RING)),
+            dma((2, 4, 4)), dma((2, 4, 4)), dma((2,)),
             dma((JOBS,)), dma((JOBS,)), dma((JOBS, CHIPS - 1)), dma((JOBS, CHIPS - 1)),
             dma((JOBS, 2)), dma((2, CHIPS, 2)),
         ],
         compiler_params=pltpu.CompilerParams(
-            collective_id=0, has_side_effects=True, vmem_limit_bytes=56 * 2**20
+            collective_id=0, has_side_effects=True, vmem_limit_bytes=grant
         ),
-    )(qkv, feat_taps, long_filter.T, skip_gain.reshape(1, WIDTH), out_weight.T).T
+    )(y, out_weight.T).T
 
 
 def solution(mesh):

time: 89.3 us -> 103 us (1.15)
  the two profiles are of different devices: /device:TPU:67 before, /device:TPU:131 now
where the time goes in v7:
time: 103 us
  Pallas kernels  101 us (98%)
  local copies, waits for them, and re-layouts  1.92 us (2%)
    pallas_call x1, Pallas kernels, local(): pl.pallas_call(projector, out_shape=jax.ShapeDtypeStruct((512, ROWS), BF1...  76.9 us
    pallas_call x1, Pallas kernels, local(): pl.pallas_call(mixer, out_shape=jax.ShapeDtypeStruct((WIDTH, ROWS), BF16)...  24.2 us

profile of v7, /device:TPU:131, one launch (start us, length us, event | category | flops | bytes accessed | tf_op | source)
XLA Modules:
  0.0 103.0 jit_solution(11806414928806979468)
XLA Ops:
  0.0 24.2 %shard_map.55.y_ref = bf16[1024,384]{1,0:T(8,128)(2,1)} custom-call(bf16[3,384,1024]{2,1,0:T(8,128)(2,1)} %qkv_ref.1, f32[3,7,1024]{2,1,0:T(8,128)} %taps_hbm.1, bf16[64,128]{1,0:T(8,128)(2,1)} %bitcast.6, f32[1,1024]{1,0:T(1,128)} %bitcast.7), custom_call_target="tpu_custom_call" | custom-call | tf_op jit(solution)/shard_map/pallas_call | solution.py:493
  24.2 76.9 %shard_map.56 = bf16[512,384]{1,0:T(8,128)(2,1)} custom-call(bf16[1024,384]{1,0:T(8,128)(2,1)} %shard_map.55.y_ref, bf16[64,1024]{1,0:T(8,128)(2,1)} %bitcast.5), custom_call_target="tpu_custom_call" | custom-call | tf_op jit(solution)/shard_map/pallas_call | solution.py:518
  101.0 1.9 %copy.6 = bf16[384,512]{1,0:T(8,128)(2,1)} copy(bf16[384,512]{0,1:T(8,128)(2,1)} %bitcast.4) | data formatting | bytes 786432 | tf_op jit(solution)/shard_map/transpose | solution.py:539

commit v8 on v2

--- a/solution.py
+++ b/solution.py
@@ -21,6 +21,10 @@
 PIECE = 32
 HALO = 16
 PAD = 8
+PITCH = 49
+SUBS = 8
+TALL = PITCH * SUBS
+BATCH = 8
 
 OFF = (1, -1, 2, -2, 3, -3, 4, 0)
 SLOT = {off: slot for slot, off in enumerate(OFF)}
@@ -38,8 +42,8 @@
 def kernel(
     qkv_ref, taps_hbm, filt_hbm, skip_hbm, w_ref, out_ref,
     taps_ref, filt_ref, skip_ref,
-    w_all, qkv_v, halo, ext, ut, qt, skt, hf, yt,
-    ta, sa, qa, tb, sb, qb, tc, sc, qc, ra, rb, rc, fin,
+    w_all, qkv_v, halo, ext_v, ub, qs, ut, qt, skt, hf, mats, yt,
+    ta, sa, qa, tb, sb, qb, tc, sc, qc, ra, rb, rc,
     load_sem, own_sem, halo_sem, tail_sem,
     s1, r1, s2, r2, as1, ar1, as2, ar2, bs1, br1, bs2, br2, cs1, cr1, cs2, cr2,
 ):
@@ -69,17 +73,18 @@
             src_ref=src, dst_ref=dst, send_sem=send, recv_sem=recv, device_id=to, device_id_type=MESH
         )
 
-    def go(copy):
-        copy.start()
-        started.append(copy)
+    def go(make, *args):
+        make(*args).start()
+        if (make, args) not in started:
+            started.append((make, args))
 
     loads = [
         pltpu.make_async_copy(qkv_ref.at[i], qkv_v.at[i], load_sem.at[i]) for i in (1, 2, 0)
     ]
     loads += [
         pltpu.make_async_copy(taps_hbm, taps_ref, load_sem.at[3]),
+        pltpu.make_async_copy(skip_hbm, skip_ref, load_sem.at[5]),
         pltpu.make_async_copy(filt_hbm, filt_ref, load_sem.at[4]),
-        pltpu.make_async_copy(skip_hbm, skip_ref, load_sem.at[5]),
     ]
     own = [
         pltpu.make_async_copy(
@@ -87,7 +92,7 @@
         )
         for kind in range(2)
     ]
-    for copy in loads + own:
+    for copy in loads[::-1] + own:
         copy.start()
 
     barrier = pltpu.get_barrier_semaphore()
@@ -95,6 +100,47 @@
     greeted += [z_at(1), z_at(-1), y_at(1), y_at(-1), seq_at(1), seq_at(-1)]
     for to in greeted:
         pl.semaphore_signal(barrier, inc=1, device_id=to, device_id_type=MESH)
+    def toeplitz():
+        loads[5].wait()
+        hf[...] = filt_ref[...].astype(F32)
+
+        def body(step, carry):
+            row = lax.broadcasted_iota(jnp.int32, (SUBS, SPAN), 0)
+            col = lax.broadcasted_iota(jnp.int32, (SUBS, SPAN), 1)
+            for i in range(4):
+                g = step * 4 + i
+                base = jnp.broadcast_to(hf[pl.ds(g, 1), :], (SUBS, SPAN))
+                for bit in (1, 2, 4):
+                    base = jnp.where((row & bit) != 0, pltpu.roll(base, bit, 1), base)
+                for pair in range(SPAN // (2 * SUBS)):
+                    above, below = [], []
+                    for k in (2 * pair, 2 * pair + 1):
+                        turned = pltpu.roll(base, SUBS * k, 1) if k else base
+                        under = row + SUBS * k > col
+                        above.append(jnp.where(under, turned, 0.0))
+                        below.append(jnp.where(under, 0.0, turned))
+                    at = 2 * SUBS * pair
+                    mats[g, at : at + 2 * SUBS] = jnp.concatenate(above, axis=0).astype(BF16)
+                    mats[g, SPAN + at : SPAN + at + 2 * SUBS] = jnp.concatenate(below, axis=0).astype(BF16)
+            return carry
+
+        lax.fori_loop(0, 16, body, 0)
+
+    def widen():
+        for copy in loads[:5]:
+            copy.wait()
+
+        def body(strip, carry):
+            at = pl.ds(pl.multiple_of(strip * LANES, LANES), LANES)
+            for i in range(3):
+                ext_v[i, strip, PAD : PAD + ROWS, :] = qkv_v[i, :, at].astype(F32)
+                ext_v[i, strip, PAD + ROWS :, :] = jnp.zeros((TALL - ROWS, LANES), F32)
+            skt[at, :] = jnp.broadcast_to(skip_ref[:, at], (LANES, LANES)).T
+            return carry
+
+        lax.fori_loop(0, STRIPS, body, 0)
+
+    widen()
     pl.semaphore_wait(barrier, len(greeted))
 
     def first(kind, direction, step):
@@ -134,34 +180,40 @@
             for direction in (1, -1):
                 first(kind, direction, step).wait_recv()
                 if step < 4:
-                    go(first(kind, direction, step + 1))
+                    go(first, kind, direction, step + 1)
         for kind in range(2):
             for direction in (1, -1):
-                go(second(kind, direction, 1, step))
+                go(second, kind, direction, 1, step)
 
     def second_arrives(step, pack):
         for kind in range(2):
             for direction in lanes_of(step, pack):
                 second(kind, direction, step, pack).wait_recv()
                 if step < 4 and direction in lanes_of(step + 1, pack):
-                    go(second(kind, direction, step + 1, pack))
-
-    events = [(2.2 * k, first_arrives, (k,)) for k in range(1, 5)]
-    events += [
-        (2.6 + 10.5 * (k - 1) + 2.4 * g, second_arrives, (k, g)) for k in range(1, 5) for g in range(5)
-    ]
+                    go(second, kind, direction, step + 1, pack)
+
+    events = [(2.9 + 11.7 * (k - 1) + 3.5 * (g + 1), second_arrives, (k, g)) for k in range(1, 5) for g in range(5)]
     events.sort(key=lambda e: e[0])
-    events = [(at, fn, args) for at, fn, args in events]
+
+    def happen(step, table):
+        for at, calls in table.items():
+            @pl.when(step == at)
+            def run(calls=calls):
+                for fn, *args in calls:
+                    fn(*args)
+
+    def early(number):
+        at, fn, args = events[number]
+        seen.add(args)
+        return fn, *args
+
     clock = [0.0]
     seen = set()
 
     def take_event():
         at, fn, args = events.pop(0)
         fn(*args)
-        if fn is second_arrives:
-            seen.add(args)
-        else:
-            seen.add(args[0])
+        seen.add(args)
         clock[0] = max(clock[0], at)
 
     def work(cost, fn, *args):
@@ -175,100 +227,97 @@
         while not wanted <= seen:
             take_event()
 
-    halo_copy = remote(
-        qkv_ref.at[:, ROWS - HALO : ROWS], halo, halo_sem.at[0], halo_sem.at[1], seq_at(1)
-    )
+    def halo_copy():
+        return remote(
+            qkv_ref.at[:, ROWS - HALO : ROWS], halo, halo_sem.at[0], halo_sem.at[1], seq_at(1)
+        )
+
     go(halo_copy)
     for kind in range(2):
         for direction in (1, -1):
-            go(first(kind, direction, 1))
+            go(first, kind, direction, 1)
     for kind in range(2):
         for direction in (1, -1):
-            go(second(kind, direction, 1, 0))
-
-    def widen(strip):
-        at = pl.ds(pl.multiple_of(strip * LANES, LANES), LANES)
-        for i in range(3):
-            ext[i, strip, PAD:, :] = qkv_v[i, :, at].astype(F32)
-
-    def widen_halo(strip):
-        at = pl.ds(pl.multiple_of(strip * LANES, LANES), LANES)
-        for i in range(3):
-            before = halo[i, :, at].astype(F32)[HALO - PAD :]
-            ext[i, strip, :PAD, :] = jnp.where(s == 0, 0.0, before)
-
-    def feature(i, block, strip, at):
-        total = None
-        for j in range(FTAPS):
-            term = taps_ref[i, j : j + 1, at] * ext[i, strip, pl.ds(PAD + SPAN * block - j, SPAN), :]
-            total = term if total is None else total + term
-        return total
-
-    def features(block, strips):
+            go(second, kind, direction, 1, 0)
+
+    def halo_arrives():
+        halo_copy().wait_recv()
+
         def body(strip, carry):
             at = pl.ds(pl.multiple_of(strip * LANES, LANES), LANES)
-            u = (feature(1, block, strip, at) * feature(2, block, strip, at)).astype(BF16).astype(F32)
-            ut[block + 1, at, :] = u.T.astype(BF16)
-            qt[block, at, :] = feature(0, block, strip, at).T
+            for i in range(3):
+                before = halo[i, :, at].astype(F32)[HALO - PAD :]
+                ext_v[i, strip, :PAD, :] = jnp.where(s == 0, 0.0, before)
             return carry
 
-        lax.fori_loop(strips[0], strips[1], body, 0)
-
-    def widen_all():
-        for copy in loads:
-            copy.wait()
-
-        def body(strip, carry):
-            widen(strip)
-            return carry
-
         lax.fori_loop(0, STRIPS, body, 0)
-        hf[...] = filt_ref[...].astype(F32)
-
-    def halo_arrives():
-        halo_copy.wait_recv()
-
-        def body(strip, carry):
-            widen_halo(strip)
-            at = pl.ds(pl.multiple_of(strip * LANES, LANES), LANES)
-            skt[at, :] = jnp.broadcast_to(skip_ref[:, at], (LANES, LANES)).T
-            return carry
-
-        lax.fori_loop(0, STRIPS, body, 0)
-
-    tail_copy = remote(ut.at[BLOCKS], ut.at[0], tail_sem.at[0], tail_sem.at[1], seq_at(1))
-
-    def send_tail():
-        go(tail_copy)
-
-    def tail_arrives():
-        tail_copy.wait_recv()
+
+    def features(strip):
+        at = pl.ds(pl.multiple_of(strip * LANES, LANES), LANES)
+        taps = [
+            [jnp.broadcast_to(taps_ref[i, j : j + 1, at], (SUBS, LANES)) for j in range(FTAPS)]
+            for i in range(3)
+        ]
+
+        def load(i, r):
+            return ext_v[i, strip, pl.ds(PAD + r, SUBS, stride=PITCH), :]
+
+        def line(i, window):
+            total = taps[i][0] * window[-1]
+            for j in range(1, FTAPS):
+                total = total + taps[i][j] * window[-1 - j]
+            return total
+
+        def some(turn, windows):
+            windows = [list(w) for w in windows]
+            for step in range(FTAPS):
+                r = turn * FTAPS + step
+                found = []
+                for i in range(3):
+                    windows[i] = windows[i][1 - FTAPS :] + [load(i, r)]
+                    found.append(line(i, windows[i]))
+                ub[strip, pl.ds(r, SUBS, stride=PITCH), :] = found[1] * found[2]
+                qs[strip, pl.ds(r, SUBS, stride=PITCH), :] = found[0]
+            return tuple(tuple(w[1 - FTAPS :]) for w in windows)
+
+        start = tuple(tuple(load(i, r) for r in range(1 - FTAPS, 0)) for i in range(3))
+        lax.fori_loop(0, PITCH // FTAPS, some, start)
+        for b in range(BLOCKS):
+            ut[b + 1, at, :] = ub[strip, SPAN * b : SPAN * (b + 1), :].T.astype(BF16)
+            qt[b, at, :] = qs[strip, SPAN * b : SPAN * (b + 1), :].T
+
+    def tail(quarter):
+        at = pl.ds(pl.multiple_of(quarter * (WIDTH // 4), WIDTH // 4), WIDTH // 4)
+        return remote(
+            ut.at[BLOCKS, at], ut.at[0, at], tail_sem.at[0, quarter], tail_sem.at[1, quarter], seq_at(1)
+        )
+
+    def tail_arrives(quarter):
+        tail(quarter).wait_recv()
 
         @pl.when(s == 0)
         def clear():
-            ut[0] = jnp.zeros((WIDTH, SPAN), BF16)
-
-    def conv(lo, hi):
-        def body(g, carry):
-            row = lax.broadcasted_iota(jnp.int32, (SPAN, SPAN), 0)
-            col = lax.broadcasted_iota(jnp.int32, (SPAN, SPAN), 1)
-            taps = jnp.broadcast_to(hf[pl.ds(g, 1), :], (SPAN, SPAN))
-            ring = pltpu.roll(taps, 0, 1, stride=1, stride_axis=0)
-            here = jnp.where(row <= col, ring, 0.0)
-            before = jnp.where(row > col, ring, 0.0)
-            matrix = jnp.concatenate([before, here], axis=0).astype(BF16)
-            at = pl.ds(pl.multiple_of(g * GROUP, GROUP), GROUP)
-            parts = [ut[b, at, :] for b in range(BLOCKS + 1)]
-            window = jnp.concatenate(
-                [jnp.concatenate(parts[:BLOCKS], axis=0), jnp.concatenate(parts[1:], axis=0)], axis=1
+            at = pl.ds(pl.multiple_of(quarter * (WIDTH // 4), WIDTH // 4), WIDTH // 4)
+            ut[0, at] = jnp.zeros((WIDTH // 4, SPAN), BF16)
+
+    def conv(step):
+        base = step * BATCH
+        spots = [pl.ds(pl.multiple_of((base + i) * GROUP, GROUP), GROUP) for i in range(BATCH)]
+        parts = [[ut[b, at, :] for b in range(BLOCKS + 1)] for at in spots]
+        mixed = []
+        for i in range(BATCH):
+            window = [jnp.concatenate(parts[i][b : b + 2], axis=1) for b in range(BLOCKS)]
+            mixed.append(
+                jnp.dot(jnp.concatenate(window, axis=0), mats[base + i], preferred_element_type=F32)
             )
-            mixed = jnp.dot(window, matrix, preferred_element_type=F32)
+        found = []
+        for i, at in enumerate(spots):
             for b in range(BLOCKS):
-                field = mixed[GROUP * b : GROUP * (b + 1)] + skt[at, :] * parts[b + 1].astype(F32)
-                yt[at, SPAN * b : SPAN * (b + 1)] = (qt[b, at, :] * field).astype(BF16)
-            return carry
-
-        lax.fori_loop(lo, hi, body, 0, unroll=4)
+                field = mixed[i][GROUP * b : GROUP * (b + 1)] + skt[at, :] * parts[i][b + 1].astype(F32)
+                found.append((qt[b, at, :] * field).astype(BF16))
+        for i, at in enumerate(spots):
+            for b in range(BLOCKS):
+                yt[at, SPAN * b : SPAN * (b + 1)] = found[BLOCKS * i + b]
 
     def project(pieces):
         rows = jnp.concatenate(pieces, axis=0) if len(pieces) > 1 else pieces[0]
@@ -305,7 +354,7 @@
         got = project(sum([four(0, m, 1 - p) for m in slots], [])).astype(BF16)
         for i, m in enumerate(slots):
             ta[m] = got[4 * PIECE * i : 4 * PIECE * (i + 1)]
-            go(a_swap(m))
+            go(a_swap, m)
 
     def a_second(slots):
         got = project(sum([four(0, m, p) for m in slots], []))
@@ -322,7 +371,7 @@
 
     def b_first(turn):
         tb[turn] = project([b_rows(turn, 1 - p)]).astype(BF16)
-        go(b_swap(turn))
+        go(b_swap, turn)
 
     def b_second(turn):
         got = project([b_rows(turn, p)])
@@ -348,7 +397,7 @@
 
     def o_first():
         tc[: 4 * PIECE] = project(four(1, OWN, 1 - p)).astype(BF16)
-        go(o_swap(0))
+        go(o_swap, 0)
 
     def o_second():
         got = project(four(1, OWN, p))
@@ -360,7 +409,7 @@
     def far_first(batch):
         at = pl.ds(4 * PIECE * (batch + 1), 4 * PIECE)
         tc[at] = project([two(0, FAR, batch, 1 - p), two(1, FAR, batch, 1 - p)]).astype(BF16)
-        go(o_swap(batch + 1))
+        go(o_swap, batch + 1)
 
     def far_second(batch):
         base = 4 * PIECE * (batch + 1)
@@ -377,18 +426,69 @@
         for copy in own:
             copy.wait()
 
-    work(1.0, widen_all)
-    for lo in (0, 4):
-        work(1.4, features, BLOCKS - 1, (lo, lo + 4))
-    work(0.1, send_tail)
-    for lo in (0, 4):
-        work(1.4, features, 1, (lo, lo + 4))
-    work(0.3, halo_arrives)
-    for lo in (0, 4):
-        work(1.4, features, 0, (lo, lo + 4))
-    work(0.1, tail_arrives)
-    for lo in range(0, 64, 16):
-        work(1.5, conv, lo, lo + 16)
+    def place(kind, slot, rows):
+        at = lax.rem(z + OFF[slot] + RING, RING) * (2 * PIECE) + kind * PIECE
+        out_ref[pl.ds(pl.multiple_of(at, PIECE), PIECE), :] = rows.astype(BF16)
+
+    def total(refs):
+        found = None
+        for ref in refs:
+            term = ref[...].astype(F32)
+            found = term if found is None else found + term
+        return found
+
+    def arrived(ref, sem):
+        remote(ref, ref, cs2.at[0, 0, 0], sem, sibling).wait_recv()
+
+    def pair_sums(turn):
+        for half in range(2):
+            for chip in range(4):
+                arrived(rb.at[turn, chip, half], br2.at[turn, chip, half])
+            place(1, 2 * turn + half, total([rb.at[turn, chip, half] for chip in range(4)]))
+
+    def single_sums(single, slot):
+        for chip in range(4):
+            arrived(rc.at[single, chip], cr2.at[single, chip])
+        place(1, slot, total([rc.at[single, chip] for chip in range(4)]))
+
+    def row_sums():
+        for half in range(2):
+            for chip in range(4):
+                arrived(ra.at[chip, half], ar2.at[chip, half])
+            found = total([ra.at[chip, half] for chip in range(4)])
+            for i in range(4):
+                slot = 4 * (i // 2) + 2 * half + i % 2
+                place(0, slot, found[PIECE * i : PIECE * (i + 1)])
+
+    toeplitz()
+    first_arrives(1)
+    halo_arrives()
+
+    def feature_strip(strip, carry):
+        features(strip)
+
+        @pl.when(lax.rem(strip, 2) == 1)
+        def send():
+            tail(lax.div(strip, 2)).start()
+
+        happen(strip, {1: [(first_arrives, 2)], 4: [(first_arrives, 3)], 6: [early(0)]})
+        return carry
+
+    lax.fori_loop(0, STRIPS, feature_strip, 0)
+    first_arrives(4)
+
+    def conv_step(step, carry):
+        @pl.when(lax.rem(step, 2) == 0)
+        def wait():
+            tail_arrives(lax.div(step, 2))
+
+        conv(step)
+        happen(step, {1: [early(1)], 5: [early(2)]})
+        return carry
+
+    lax.fori_loop(0, 64 // BATCH, conv_step, 0)
+    del events[:3]
+    clock[0] = 15.0
     work(0.1, own_wait)
     work(0.6, a_first, (OWN,))
     work(0.6, o_first)
@@ -407,45 +507,22 @@
     far_second(0)
     need(4)
     far_first(1)
+    pair_sums(0)
+    pair_sums(1)
+    single_sums(0, OWN)
     far_second(1)
-
-    def place(kind, slot, rows):
-        at = lax.rem(z + OFF[slot] + RING, RING) * (2 * PIECE) + kind * PIECE
-        fin[pl.ds(pl.multiple_of(at, PIECE), PIECE), :] = rows
-
-    def total(refs):
-        found = None
-        for ref in refs:
-            term = ref[...].astype(F32)
-            found = term if found is None else found + term
-        return found
-
-    def arrived(ref, sem):
-        remote(ref, ref, cs2.at[0, 0, 0], sem, sibling).wait_recv()
-
-    for turn in range(PAIRS):
-        for half in range(2):
-            for chip in range(4):
-                arrived(rb.at[turn, chip, half], br2.at[turn, chip, half])
-            place(1, 2 * turn + half, total([rb.at[turn, chip, half] for chip in range(4)]))
-    for single, slot in ((0, OWN), (1, FAR)):
-        for chip in range(4):
-            arrived(rc.at[single, chip], cr2.at[single, chip])
-        place(1, slot, total([rc.at[single, chip] for chip in range(4)]))
-    for half in range(2):
-        for chip in range(4):
-            arrived(ra.at[chip, half], ar2.at[chip, half])
-        found = total([ra.at[chip, half] for chip in range(4)])
-        for i in range(4):
-            slot = 4 * (i // 2) + 2 * half + i % 2
-            place(0, slot, found[PIECE * i : PIECE * (i + 1)])
-    for a in range(BLOCKS):
-        for n in range(4):
-            tile = fin[LANES * n : LANES * (n + 1), SPAN * a : SPAN * (a + 1)]
-            out_ref[SPAN * a : SPAN * (a + 1), LANES * n : LANES * (n + 1)] = tile.T.astype(BF16)
-
-    for copy in started:
-        copy.wait_send()
+    pair_sums(2)
+    single_sums(1, FAR)
+    row_sums()
+
+    for make, args in started:
+        make(*args).wait_send()
+
+    def drain_tail(quarter, carry):
+        tail(quarter).wait_send()
+        return carry
+
+    lax.fori_loop(0, 4, drain_tail, 0)
     for to, copy in delivered:
         @pl.when(to != c)
         def drain(copy=copy):
@@ -459,7 +536,7 @@
     half_piece = (4 * PIECE, ROWS)
     return pl.pallas_call(
         kernel,
-        out_shape=jax.ShapeDtypeStruct((ROWS, 512), BF16),
+        out_shape=jax.ShapeDtypeStruct((512, ROWS), BF16),
         in_specs=[anywhere] * 5,
         out_specs=vmem,
         scratch_shapes=[
@@ -469,11 +546,14 @@
             pltpu.VMEM((2, RING, RING, PIECE, WIDTH), BF16),
             pltpu.VMEM((3, ROWS, WIDTH), BF16),
             pltpu.VMEM((3, HALO, WIDTH), BF16),
-            pltpu.VMEM((3, STRIPS, PAD + ROWS, LANES), F32),
+            pltpu.VMEM((3, STRIPS, PAD + TALL, LANES), F32),
+            pltpu.VMEM((STRIPS, TALL, LANES), F32),
+            pltpu.VMEM((STRIPS, TALL, LANES), F32),
             pltpu.VMEM((BLOCKS + 1, WIDTH, SPAN), BF16),
             pltpu.VMEM((BLOCKS, WIDTH, SPAN), F32),
             pltpu.VMEM((WIDTH, SPAN), F32),
             pltpu.VMEM((WIDTH // GROUP, SPAN), F32),
+            pltpu.VMEM((WIDTH // GROUP, 2 * SPAN, SPAN), BF16),
             pltpu.VMEM((WIDTH, ROWS), BF16),
             pltpu.VMEM((RING,) + half_piece, BF16),
             pltpu.VMEM((RING,) + half_piece, BF16),
@@ -487,8 +567,7 @@
             pltpu.VMEM((4, 2) + half_piece, BF16),
             pltpu.VMEM((PAIRS, 4, 2, PIECE, ROWS), BF16),
             pltpu.VMEM((2, 4, PIECE, ROWS), BF16),
-            pltpu.VMEM((512, ROWS), F32),
-            dma((6,)), dma((2,)), dma((2,)), dma((2,)),
+            dma((6,)), dma((2,)), dma((2,)), dma((2, 4)),
             dma((2, 2, 4)), dma((2, 2, 4)),
             dma((2, 2, 4, 5)), dma((2, 2, 4, 5)),
             dma((RING,)), dma((RING,)), dma((RING, 2)), dma((4, 2)),
@@ -498,7 +577,7 @@
         compiler_params=pltpu.CompilerParams(
             collective_id=0, has_side_effects=True, vmem_limit_bytes=56 * 2**20
         ),
-    )(qkv, feat_taps, long_filter.T, skip_gain.reshape(1, WIDTH), out_weight.T)
+    )(qkv, feat_taps, long_filter.T, skip_gain.reshape(1, WIDTH), out_weight.T).T
 
 
 def solution(mesh):

time: 83.7 us -> 87.1 us (1.041)
  Pallas kernels: 81.5 us -> 84.7 us
    pallas_call x1, Pallas kernels: 81.5 us -> 84.7 us  [local(): pl.pallas_call(kernel, out_shape=jax.ShapeDtypeStruct((512, ROWS), BF16),...]
    transpose x0 -> x1, local copies, waits for them, and re-layouts: none -> 1.92 us  [local(): return pl.pallas_call(kernel, out_shape=jax.ShapeDtypeStruct((512, ROWS),...]
    unnamed x1 -> x0, local copies, waits for them, and re-layouts: 1.77 us -> none
where the time goes in v8:
time: 87.1 us; the launch traced here: 86.6 us
  Pallas kernels  84.7 us (97%)
  local copies, waits for them, and re-layouts  1.92 us (2%)
    pallas_call x1, Pallas kernels, local(): pl.pallas_call(kernel, out_shape=jax.ShapeDtypeStruct((512, ROWS), BF16),...  84.7 us
    transpose x1, local copies, waits for them, and re-layouts, local(): return pl.pallas_call(kernel, out_shape=jax.ShapeDtypeStruct((512, ROWS),...  1.92 us

profile of v8, /device:TPU:4, one launch (start us, length us, event | category | flops | bytes accessed | tf_op | source)
XLA Modules:
  0.0 86.6 jit_solution(7255388368858937357)
XLA Ops:
  0.0 84.7 %shard_map.55 = bf16[512,384]{1,0:T(8,128)(2,1)} custom-call(bf16[3,384,1024]{2,1,0:T(8,128)(2,1)} %qkv_ref.1, f32[3,7,1024]{2,1,0:T(8,128)} %taps_hbm.1, bf16[64,128]{1,0:T(8,128)(2,1)} %bitcast.6, f32[1,1024]{1,0:T(1,128)} %bitcast.7, bf16[64,1024]{1,0:T(8,128)(2,1)} %bitcast.5), custom_call_target="tpu_custom_call" | custom-call | tf_op jit(solution)/shard_map/pallas_call | solution.py:537
  84.7 1.9 %copy.6 = bf16[384,512]{1,0:T(8,128)(2,1)} copy(bf16[384,512]{0,1:T(8,128)(2,1)} %bitcast.4) | data formatting | bytes 786432 | tf_op jit(solution)/shard_map/transpose | solution.py:580

commit v9 on v8

--- a/solution.py
+++ b/solution.py
@@ -100,10 +100,7 @@
     greeted += [z_at(1), z_at(-1), y_at(1), y_at(-1), seq_at(1), seq_at(-1)]
     for to in greeted:
         pl.semaphore_signal(barrier, inc=1, device_id=to, device_id_type=MESH)
-    def toeplitz():
-        loads[5].wait()
-        hf[...] = filt_ref[...].astype(F32)
-
+    def toeplitz(low, high):
         def body(step, carry):
             row = lax.broadcasted_iota(jnp.int32, (SUBS, SPAN), 0)
             col = lax.broadcasted_iota(jnp.int32, (SUBS, SPAN), 1)
@@ -124,7 +121,7 @@
                     mats[g, SPAN + at : SPAN + at + 2 * SUBS] = jnp.concatenate(below, axis=0).astype(BF16)
             return carry
 
-        lax.fori_loop(0, 16, body, 0)
+        lax.fori_loop(low, high, body, 0)
 
     def widen():
         for copy in loads[:5]:
@@ -140,7 +137,6 @@
 
         lax.fori_loop(0, STRIPS, body, 0)
 
-    widen()
     pl.semaphore_wait(barrier, len(greeted))
 
     def first(kind, direction, step):
@@ -460,8 +456,17 @@
                 slot = 4 * (i // 2) + 2 * half + i % 2
                 place(0, slot, found[PIECE * i : PIECE * (i + 1)])
 
-    toeplitz()
-    first_arrives(1)
+    loads[5].wait()
+    hf[...] = filt_ref[...].astype(F32)
+
+    def filters(n, carry):
+        toeplitz(n * 6, jnp.minimum(n * 6 + 6, 16))
+        happen(n, {0: [(first_arrives, 1)], 2: [(first_arrives, 2)]})
+        return carry
+
+    lax.fori_loop(0, 3, filters, 0)
+    widen()
+    first_arrives(3)
     halo_arrives()
 
     def feature_strip(strip, carry):
@@ -471,11 +476,10 @@
         def send():
             tail(lax.div(strip, 2)).start()
 
-        happen(strip, {1: [(first_arrives, 2)], 4: [(first_arrives, 3)], 6: [early(0)]})
+        happen(strip, {0: [(first_arrives, 4)], 2: [early(0)], 4: [early(1)], 7: [early(2)]})
         return carry
 
     lax.fori_loop(0, STRIPS, feature_strip, 0)
-    first_arrives(4)
 
     def conv_step(step, carry):
         @pl.when(lax.rem(step, 2) == 0)
@@ -483,12 +487,12 @@
             tail_arrives(lax.div(step, 2))
 
         conv(step)
-        happen(step, {1: [early(1)], 5: [early(2)]})
+        happen(step, {3: [early(3)], 7: [early(4)]})
         return carry
 
     lax.fori_loop(0, 64 // BATCH, conv_step, 0)
-    del events[:3]
-    clock[0] = 15.0
+    del events[:5]
+    clock[0] = 18.0
     work(0.1, own_wait)
     work(0.6, a_first, (OWN,))
     work(0.6, o_first)
@@ -497,9 +501,9 @@
     for k in (1, 2, 3):
         low, high = SLOT[k], SLOT[-k]
         need(k)
-        work(1.0, a_first, (low, high))
-        work(1.0, b_first, k - 1)
-        work(1.0, a_second, (low, high))
+        work(1.2, a_first, (low, high))
+        work(1.2, b_first, k - 1)
+        work(1.2, a_second, (low, high))
         work(1.2, b_second, k - 1)
     while not {(4, g) for g in (0, 1, 2)} <= seen:
         take_event()

time: 87.1 us -> 87.2 us (level)
  no operation moved by 1% of the time
where the time goes in v9:
time: 87.2 us; the launch traced here: 86.8 us
  Pallas kernels  84.8 us (97%)
  local copies, waits for them, and re-layouts  1.92 us (2%)
    pallas_call x1, Pallas kernels, local(): pl.pallas_call(kernel, out_shape=jax.ShapeDtypeStruct((512, ROWS), BF16),...  84.8 us
    transpose x1, local copies, waits for them, and re-layouts, local(): return pl.pallas_call(kernel, out_shape=jax.ShapeDtypeStruct((512, ROWS),...  1.92 us

profile of v9, /device:TPU:4, one launch (start us, length us, event | category | flops | bytes accessed | tf_op | source)
XLA Modules:
  0.0 86.8 jit_solution(6064995711604804214)
XLA Ops:
  0.0 84.8 %shard_map.55 = bf16[512,384]{1,0:T(8,128)(2,1)} custom-call(bf16[3,384,1024]{2,1,0:T(8,128)(2,1)} %qkv_ref.1, f32[3,7,1024]{2,1,0:T(8,128)} %taps_hbm.1, bf16[64,128]{1,0:T(8,128)(2,1)} %bitcast.6, f32[1,1024]{1,0:T(1,128)} %bitcast.7, bf16[64,1024]{1,0:T(8,128)(2,1)} %bitcast.5), custom_call_target="tpu_custom_call" | custom-call | tf_op jit(solution)/shard_map/pallas_call | solution.py:541
  84.8 1.9 %copy.6 = bf16[384,512]{1,0:T(8,128)(2,1)} copy(bf16[384,512]{0,1:T(8,128)(2,1)} %bitcast.4) | data formatting | bytes 786432 | tf_op jit(solution)/shard_map/transpose | solution.py:584

commit v10 on v9

--- a/solution.py
+++ b/solution.py
@@ -188,7 +188,7 @@
                 if step < 4 and direction in lanes_of(step + 1, pack):
                     go(second, kind, direction, step + 1, pack)
 
-    events = [(2.9 + 11.7 * (k - 1) + 3.5 * (g + 1), second_arrives, (k, g)) for k in range(1, 5) for g in range(5)]
+    events = [(2.6 + 10.5 * (k - 1) + 2.4 * g, second_arrives, (k, g)) for k in range(1, 5) for g in range(5)]
     events.sort(key=lambda e: e[0])
 
     def happen(step, table):
@@ -202,6 +202,10 @@
         at, fn, args = events[number]
         seen.add(args)
         return fn, *args
+
+    def run_early(number):
+        fn, *args = early(number)
+        fn(*args)
 
     clock = [0.0]
     seen = set()
@@ -461,12 +465,12 @@
 
     def filters(n, carry):
         toeplitz(n * 6, jnp.minimum(n * 6 + 6, 16))
-        happen(n, {0: [(first_arrives, 1)], 2: [(first_arrives, 2)]})
+        happen(n, {0: [(first_arrives, 1)], 1: [early(0)], 2: [(first_arrives, 2)]})
         return carry
 
     lax.fori_loop(0, 3, filters, 0)
     widen()
-    first_arrives(3)
+    run_early(1)
     halo_arrives()
 
     def feature_strip(strip, carry):
@@ -476,7 +480,9 @@
         def send():
             tail(lax.div(strip, 2)).start()
 
-        happen(strip, {0: [(first_arrives, 4)], 2: [early(0)], 4: [early(1)], 7: [early(2)]})
+        happen(strip, {
+            0: [(first_arrives, 3)], 2: [early(2)], 3: [(first_arrives, 4)], 5: [early(3)], 7: [early(4)],
+        })
         return carry
 
     lax.fori_loop(0, STRIPS, feature_strip, 0)
@@ -487,11 +493,11 @@
             tail_arrives(lax.div(step, 2))
 
         conv(step)
-        happen(step, {3: [early(3)], 7: [early(4)]})
+        happen(step, {1: [early(5)], 4: [early(6)], 7: [early(7)]})
         return carry
 
     lax.fori_loop(0, 64 // BATCH, conv_step, 0)
-    del events[:5]
+    del events[:8]
     clock[0] = 18.0
     work(0.1, own_wait)
     work(0.6, a_first, (OWN,))
@@ -501,10 +507,10 @@
     for k in (1, 2, 3):
         low, high = SLOT[k], SLOT[-k]
         need(k)
-        work(1.2, a_first, (low, high))
-        work(1.2, b_first, k - 1)
-        work(1.2, a_second, (low, high))
-        work(1.2, b_second, k - 1)
+        work(1.0, a_first, (low, high))
+        work(1.0, b_first, k - 1)
+        work(1.0, a_second, (low, high))
+        work(1.0, b_second, k - 1)
     while not {(4, g) for g in (0, 1, 2)} <= seen:
         take_event()
     far_first(0)

time: 87.2 us -> 84.6 us (0.970)
  the two profiles are of different devices: /device:TPU:4 before, /device:TPU:3 now
where the time goes in v10:
time: 84.6 us; the launch traced here: 84.4 us
  Pallas kernels  82.5 us (98%)
  local copies, waits for them, and re-layouts  1.92 us (2%)
    pallas_call x1, Pallas kernels, local(): pl.pallas_call(kernel, out_shape=jax.ShapeDtypeStruct((512, ROWS), BF16),...  82.5 us
    transpose x1, local copies, waits for them, and re-layouts, local(): return pl.pallas_call(kernel, out_shape=jax.ShapeDtypeStruct((512, ROWS),...  1.92 us

profile of v10, /device:TPU:3, one launch (start us, length us, event | category | flops | bytes accessed | tf_op | source)
XLA Modules:
  0.0 84.4 jit_solution(705433865564178394)
XLA Ops:
  0.0 82.5 %shard_map.55 = bf16[512,384]{1,0:T(8,128)(2,1)} custom-call(bf16[3,384,1024]{2,1,0:T(8,128)(2,1)} %qkv_ref.1, f32[3,7,1024]{2,1,0:T(8,128)} %taps_hbm.1, bf16[64,128]{1,0:T(8,128)(2,1)} %bitcast.6, f32[1,1024]{1,0:T(1,128)} %bitcast.7, bf16[64,1024]{1,0:T(8,128)(2,1)} %bitcast.5), custom_call_target="tpu_custom_call" | custom-call | tf_op jit(solution)/shard_map/pallas_call | solution.py:547
  82.5 1.9 %copy.6 = bf16[384,512]{1,0:T(8,128)(2,1)} copy(bf16[384,512]{0,1:T(8,128)(2,1)} %bitcast.4) | data formatting | bytes 786432 | tf_op jit(solution)/shard_map/transpose | solution.py:590

commit v11 on v2

--- a/solution.py
+++ b/solution.py
@@ -39,9 +39,9 @@
     qkv_ref, taps_hbm, filt_hbm, skip_hbm, w_ref, out_ref,
     taps_ref, filt_ref, skip_ref,
     w_all, qkv_v, halo, ext, ut, qt, skt, hf, yt,
-    ta, sa, qa, tb, sb, qb, tc, sc, qc, ra, rb, rc, fin,
+    ta, sa, qa, ra, rb, rc,
     load_sem, own_sem, halo_sem, tail_sem,
-    s1, r1, s2, r2, as1, ar1, as2, ar2, bs1, br1, bs2, br2, cs1, cr1, cs2, cr2,
+    s1, r1, s2, r2, as1, ar1, as2, ar2, bs2, br2, cs2, cr2,
 ):
     s = lax.axis_index("seq")
     c = lax.axis_index("chan")
@@ -298,84 +298,107 @@
 
         delivered.append((to, copy))
 
-    def a_swap(slot):
-        return remote(ta.at[slot], sa.at[slot], as1.at[slot], ar1.at[slot], sibling)
-
-    def a_first(slots):
-        got = project(sum([four(0, m, 1 - p) for m in slots], [])).astype(BF16)
-        for i, m in enumerate(slots):
-            ta[m] = got[4 * PIECE * i : 4 * PIECE * (i + 1)]
-            go(a_swap(m))
-
-    def a_second(slots):
-        got = project(sum([four(0, m, p) for m in slots], []))
-        for i, m in enumerate(slots):
-            a_swap(m).wait_recv()
-            qa[m] = (got[4 * PIECE * i : 4 * PIECE * (i + 1)] + sa[m].astype(F32)).astype(BF16)
-            deliver(qa.at[m], ra.at[x, p], as2.at[m, 0], ar2.at[x, p], target(m))
-
-    def b_swap(turn):
-        return remote(tb.at[turn], sb.at[turn], bs1.at[turn], br1.at[turn], sibling)
+    STARTS = (0, 256, 768, 1280, 1792, 1920)
+    COUNTS = (256, 512, 512, 512, 128, 128)
 
     def b_rows(turn, half):
         return w_all[1, 2 * turn + half].reshape(RING * PIECE, WIDTH)
 
-    def b_first(turn):
-        tb[turn] = project([b_rows(turn, 1 - p)]).astype(BF16)
-        go(b_swap(turn))
-
-    def b_second(turn):
-        got = project([b_rows(turn, p)])
-        b_swap(turn).wait_recv()
-        qb[turn] = (got + sb[turn].astype(F32)).astype(BF16)
-        for m in range(RING):
-            deliver(
-                qb.at[turn, PIECE * m : PIECE * (m + 1)], rb.at[turn, x, p],
-                bs2.at[turn, m], br2.at[turn, x, p], target(m),
-            )
-
-    def o_swap(part):
-        at = pl.ds(4 * PIECE * part, 4 * PIECE)
-        return remote(tc.at[at], sc.at[at], cs1.at[part], cr1.at[part], sibling)
-
-    def o_post(single, batch, at):
+    def pieces(bundle, half):
+        if bundle == 0:
+            return four(0, OWN, half) + four(1, OWN, half)
+        if bundle < 4:
+            low = 2 * (bundle - 1)
+            return four(0, low, half) + four(0, low + 1, half) + [b_rows(bundle - 1, half)]
+        return [two(kind, FAR, bundle - 4, half) for kind in range(2)]
+
+    def rows_of(bundle):
+        return slice(STARTS[bundle], STARTS[bundle] + COUNTS[bundle])
+
+    def swap(bundle):
+        at = pl.ds(STARTS[bundle], COUNTS[bundle])
+        return remote(ta.at[at], sa.at[at], as1.at[bundle], ar1.at[bundle], sibling)
+
+    def give(bundle):
+        ta[rows_of(bundle)] = project(pieces(bundle, 1 - p)).astype(BF16)
+        copy = swap(bundle)
+        go(copy)
+
+    def post_row(slot, at, many, batch):
+        deliver(
+            qa.at[at : at + many], ra.at[x, p, pl.ds(2 * PIECE * batch, many)],
+            as2.at[slot, batch], ar2.at[x, p], target(slot),
+        )
+
+    def post_single(single, batch, at):
         for i in range(2):
             to = lax.rem(y + jnp.where(p == 0, OFF[4 * batch + i], OFF[4 * batch + 2 + i]) + RING, RING)
             deliver(
-                qc.at[pl.ds(at + PIECE * i, PIECE)], rc.at[single, x],
+                qa.at[at + PIECE * i : at + PIECE * (i + 1)], rc.at[single, x],
                 cs2.at[single, batch, i], cr2.at[single, x], to,
             )
 
-    def o_first():
-        tc[: 4 * PIECE] = project(four(1, OWN, 1 - p)).astype(BF16)
-        go(o_swap(0))
-
-    def o_second():
-        got = project(four(1, OWN, p))
-        o_swap(0).wait_recv()
-        qc[: 4 * PIECE] = (got + sc[: 4 * PIECE].astype(F32)).astype(BF16)
-        for batch in range(2):
-            o_post(0, batch, 2 * PIECE * batch)
-
-    def far_first(batch):
-        at = pl.ds(4 * PIECE * (batch + 1), 4 * PIECE)
-        tc[at] = project([two(0, FAR, batch, 1 - p), two(1, FAR, batch, 1 - p)]).astype(BF16)
-        go(o_swap(batch + 1))
-
-    def far_second(batch):
-        base = 4 * PIECE * (batch + 1)
-        got = project([two(0, FAR, batch, p), two(1, FAR, batch, p)])
-        o_swap(batch + 1).wait_recv()
-        qc[base : base + 4 * PIECE] = (got + sc[base : base + 4 * PIECE].astype(F32)).astype(BF16)
-        deliver(
-            qc.at[base : base + 2 * PIECE], ra.at[x, p, pl.ds(2 * PIECE * batch, 2 * PIECE)],
-            as2.at[FAR, batch], ar2.at[x, p], target(FAR),
-        )
-        o_post(1, batch, base + 2 * PIECE)
+    def take(bundle):
+        got = project(pieces(bundle, p))
+        swap(bundle).wait_recv()
+        at = rows_of(bundle)
+        qa[at] = (got + sa[at].astype(F32)).astype(BF16)
+        start = STARTS[bundle]
+        if bundle == 0:
+            post_row(OWN, start, 4 * PIECE, 0)
+            for batch in range(2):
+                post_single(0, batch, start + 4 * PIECE + 2 * PIECE * batch)
+        elif bundle < 4:
+            turn = bundle - 1
+            for i in range(2):
+                post_row(2 * turn + i, start + 4 * PIECE * i, 4 * PIECE, 0)
+            for m in range(RING):
+                from_row = start + 8 * PIECE + PIECE * m
+                deliver(
+                    qa.at[from_row : from_row + PIECE], rb.at[turn, x, p],
+                    bs2.at[turn, m], br2.at[turn, x, p], target(m),
+                )
+        else:
+            post_row(FAR, start, 2 * PIECE, bundle - 4)
+            post_single(1, bundle - 4, start + 2 * PIECE)
 
     def own_wait():
         for copy in own:
             copy.wait()
+
+    def place(kind, slot, rows):
+        at = lax.rem(z + OFF[slot] + RING, RING) * (2 * PIECE) + kind * PIECE
+        out_ref[pl.ds(pl.multiple_of(at, PIECE), PIECE), :] = rows.astype(BF16)
+
+    def total(refs):
+        found = None
+        for ref in refs:
+            term = ref[...].astype(F32)
+            found = term if found is None else found + term
+        return found
+
+    def arrived(ref, sem):
+        remote(ref, ref, cs2.at[0, 0, 0], sem, sibling).wait_recv()
+
+    def pair_sums(turn):
+        for half in range(2):
+            for chip in range(4):
+                arrived(rb.at[turn, chip, half], br2.at[turn, chip, half])
+            place(1, 2 * turn + half, total([rb.at[turn, chip, half] for chip in range(4)]))
+
+    def single_sums(single, slot):
+        for chip in range(4):
+            arrived(rc.at[single, chip], cr2.at[single, chip])
+        place(1, slot, total([rc.at[single, chip] for chip in range(4)]))
+
+    def row_sums():
+        for half in range(2):
+            for chip in range(4):
+                arrived(ra.at[chip, half], ar2.at[chip, half])
+            found = total([ra.at[chip, half] for chip in range(4)])
+            for i in range(4):
+                slot = 4 * (i // 2) + 2 * half + i % 2
+                place(0, slot, found[PIECE * i : PIECE * (i + 1)])
 
     work(1.0, widen_all)
     for lo in (0, 4):
@@ -390,59 +413,25 @@
     for lo in range(0, 64, 16):
         work(1.5, conv, lo, lo + 16)
     work(0.1, own_wait)
-    work(0.6, a_first, (OWN,))
-    work(0.6, o_first)
-    work(0.6, a_second, (OWN,))
-    work(0.6, o_second)
+    work(1.0, give, 0)
+    work(1.0, take, 0)
     for k in (1, 2, 3):
-        low, high = SLOT[k], SLOT[-k]
         need(k)
-        work(1.0, a_first, (low, high))
-        work(1.0, b_first, k - 1)
-        work(1.0, a_second, (low, high))
-        work(1.2, b_second, k - 1)
+        work(1.8, give, k)
+        work(2.2, take, k)
     while not {(4, g) for g in (0, 1, 2)} <= seen:
         take_event()
-    far_first(0)
-    far_second(0)
+    give(4)
+    take(4)
     need(4)
-    far_first(1)
-    far_second(1)
-
-    def place(kind, slot, rows):
-        at = lax.rem(z + OFF[slot] + RING, RING) * (2 * PIECE) + kind * PIECE
-        fin[pl.ds(pl.multiple_of(at, PIECE), PIECE), :] = rows
-
-    def total(refs):
-        found = None
-        for ref in refs:
-            term = ref[...].astype(F32)
-            found = term if found is None else found + term
-        return found
-
-    def arrived(ref, sem):
-        remote(ref, ref, cs2.at[0, 0, 0], sem, sibling).wait_recv()
-
-    for turn in range(PAIRS):
-        for half in range(2):
-            for chip in range(4):
-                arrived(rb.at[turn, chip, half], br2.at[turn, chip, half])
-            place(1, 2 * turn + half, total([rb.at[turn, chip, half] for chip in range(4)]))
-    for single, slot in ((0, OWN), (1, FAR)):
-        for chip in range(4):
-            arrived(rc.at[single, chip], cr2.at[single, chip])
-        place(1, slot, total([rc.at[single, chip] for chip in range(4)]))
-    for half in range(2):
-        for chip in range(4):
-            arrived(ra.at[chip, half], ar2.at[chip, half])
-        found = total([ra.at[chip, half] for chip in range(4)])
-        for i in range(4):
-            slot = 4 * (i // 2) + 2 * half + i % 2
-            place(0, slot, found[PIECE * i : PIECE * (i + 1)])
-    for a in range(BLOCKS):
-        for n in range(4):
-            tile = fin[LANES * n : LANES * (n + 1), SPAN * a : SPAN * (a + 1)]
-            out_ref[SPAN * a : SPAN * (a + 1), LANES * n : LANES * (n + 1)] = tile.T.astype(BF16)
+    give(5)
+    pair_sums(0)
+    pair_sums(1)
+    single_sums(0, OWN)
+    take(5)
+    pair_sums(2)
+    single_sums(1, FAR)
+    row_sums()
 
     for copy in started:
         copy.wait_send()
@@ -459,7 +448,7 @@
     half_piece = (4 * PIECE, ROWS)
     return pl.pallas_call(
         kernel,
-        out_shape=jax.ShapeDtypeStruct((ROWS, 512), BF16),
+        out_shape=jax.ShapeDtypeStruct((512, ROWS), BF16),
         in_specs=[anywhere] * 5,
         out_specs=vmem,
         scratch_shapes=[
@@ -475,30 +464,22 @@
             pltpu.VMEM((WIDTH, SPAN), F32),
             pltpu.VMEM((WIDTH // GROUP, SPAN), F32),
             pltpu.VMEM((WIDTH, ROWS), BF16),
-            pltpu.VMEM((RING,) + half_piece, BF16),
-            pltpu.VMEM((RING,) + half_piece, BF16),
-            pltpu.VMEM((RING,) + half_piece, BF16),
-            pltpu.VMEM((PAIRS, RING * PIECE, ROWS), BF16),
-            pltpu.VMEM((PAIRS, RING * PIECE, ROWS), BF16),
-            pltpu.VMEM((PAIRS, RING * PIECE, ROWS), BF16),
-            pltpu.VMEM((12 * PIECE, ROWS), BF16),
-            pltpu.VMEM((12 * PIECE, ROWS), BF16),
-            pltpu.VMEM((12 * PIECE, ROWS), BF16),
+            pltpu.VMEM((2048, ROWS), BF16),
+            pltpu.VMEM((2048, ROWS), BF16),
+            pltpu.VMEM((2048, ROWS), BF16),
             pltpu.VMEM((4, 2) + half_piece, BF16),
             pltpu.VMEM((PAIRS, 4, 2, PIECE, ROWS), BF16),
             pltpu.VMEM((2, 4, PIECE, ROWS), BF16),
-            pltpu.VMEM((512, ROWS), F32),
             dma((6,)), dma((2,)), dma((2,)), dma((2,)),
             dma((2, 2, 4)), dma((2, 2, 4)),
             dma((2, 2, 4, 5)), dma((2, 2, 4, 5)),
-            dma((RING,)), dma((RING,)), dma((RING, 2)), dma((4, 2)),
-            dma((PAIRS,)), dma((PAIRS,)), dma((PAIRS, RING)), dma((PAIRS, 4, 2)),
-            dma((3,)), dma((3,)), dma((2, 2, 2)), dma((2, 4)),
+            dma((6,)), dma((6,)), dma((RING, 2)), dma((4, 2)),
+            dma((PAIRS, RING)), dma((PAIRS, 4, 2)), dma((2, 2, 2)), dma((2, 4)),
         ],
         compiler_params=pltpu.CompilerParams(
             collective_id=0, has_side_effects=True, vmem_limit_bytes=56 * 2**20
         ),
-    )(qkv, feat_taps, long_filter.T, skip_gain.reshape(1, WIDTH), out_weight.T)
+    )(qkv, feat_taps, long_filter.T, skip_gain.reshape(1, WIDTH), out_weight.T).T
 
 
 def solution(mesh):

time: 83.7 us -> 84.5 us (level)
  Pallas kernels: 81.5 us -> 82.4 us
    transpose x0 -> x1, local copies, waits for them, and re-layouts: none -> 1.92 us  [local(): return pl.pallas_call(kernel, out_shape=jax.ShapeDtypeStruct((512, ROWS),...]
    unnamed x1 -> x0, local copies, waits for them, and re-layouts: 1.77 us -> none
    pallas_call x1, Pallas kernels: 81.5 us -> 82.4 us  [local(): pl.pallas_call(kernel, out_shape=jax.ShapeDtypeStruct((512, ROWS), BF16),...]
where the time goes in v11:
time: 84.5 us; the launch traced here: 84.3 us
  Pallas kernels  82.4 us (98%)
  local copies, waits for them, and re-layouts  1.92 us (2%)
    pallas_call x1, Pallas kernels, local(): pl.pallas_call(kernel, out_shape=jax.ShapeDtypeStruct((512, ROWS), BF16),...  82.4 us
    transpose x1, local copies, waits for them, and re-layouts, local(): return pl.pallas_call(kernel, out_shape=jax.ShapeDtypeStruct((512, ROWS),...  1.92 us

profile of v11, /device:TPU:4, one launch (start us, length us, event | category | flops | bytes accessed | tf_op | source)
XLA Modules:
  0.0 84.3 jit_solution(7994064235909083281)
XLA Ops:
  0.0 82.4 %shard_map.55 = bf16[512,384]{1,0:T(8,128)(2,1)} custom-call(bf16[3,384,1024]{2,1,0:T(8,128)(2,1)} %qkv_ref.1, f32[3,7,1024]{2,1,0:T(8,128)} %taps_hbm.1, bf16[64,128]{1,0:T(8,128)(2,1)} %bitcast.6, f32[1,1024]{1,0:T(1,128)} %bitcast.7, bf16[64,1024]{1,0:T(8,128)(2,1)} %bitcast.5), custom_call_target="tpu_custom_call" | custom-call | tf_op jit(solution)/shard_map/pallas_call | solution.py:449
  82.4 1.9 %copy.6 = bf16[384,512]{1,0:T(8,128)(2,1)} copy(bf16[384,512]{0,1:T(8,128)(2,1)} %bitcast.4) | data formatting | bytes 786432 | tf_op jit(solution)/shard_map/transpose | solution.py:482

commit v12 on v5

--- a/solution.py
+++ b/solution.py
@@ -25,15 +25,16 @@
 SUBS = 8
 TALL = PITCH * SUBS
 
-OFF = (1, -1, 2, -2, 3, -3, 4, 0)
+OFF = (0, 1, -1, 2, -2, 3, -3, 4)
 SLOT = {off: slot for slot, off in enumerate(OFF)}
 OWN = SLOT[0]
-GROUPS = ((7,), (0, 1), (2, 3), (4, 5), (6,))
+GROUPS = ((0,), (1, 2), (3, 4), (5, 6), (7,))
 NEAR, CROSS, NEAR_EXT, CROSS_EXT = (pl.ds(2 * PIECE * i, 2 * PIECE) for i in range(4))
 PARTS = (NEAR, pl.ds(4 * PIECE, PIECE), CROSS, pl.ds(6 * PIECE, PIECE))
 HALF = 4 * PIECE
 BATCH = 8
 JOBS = 16
+CHIPS = 4
 
 
 def origin(direction, step):
@@ -44,7 +45,7 @@
     qkv_ref, taps_hbm, filt_hbm, skip_hbm, w_ref, out_ref,
     taps_ref, filt_ref, skip_ref,
     w_all, qkv_v, halo, ext_v, ub, qb, ut, qt, skt, hf, mats, y2,
-    ta, sa, qa, ra, qp, rp, fin,
+    ta, sa, qa, ra, qp, rp,
     load_sem, own_sem, halo_sem, tail_sem,
     xs, es, er, s2, r2, ys, yr, as1, ar1, as2, ar2, ps,
 ):
@@ -102,14 +103,23 @@
         hf[...] = filt_ref[...].astype(F32)
 
         def body(step, carry):
-            row = lax.broadcasted_iota(jnp.int32, (SPAN, SPAN), 0)
-            col = lax.broadcasted_iota(jnp.int32, (SPAN, SPAN), 1)
+            row = lax.broadcasted_iota(jnp.int32, (SUBS, SPAN), 0)
+            col = lax.broadcasted_iota(jnp.int32, (SUBS, SPAN), 1)
             for i in range(4):
                 g = step * 4 + i
-                taps = jnp.broadcast_to(hf[pl.ds(g, 1), :], (SPAN, SPAN))
-                turned = pltpu.roll(taps, 0, 1, stride=1, stride_axis=0)
-                mats[g, :SPAN] = jnp.where(row > col, turned, 0.0).astype(BF16)
-                mats[g, SPAN:] = jnp.where(row <= col, turned, 0.0).astype(BF16)
+                base = jnp.broadcast_to(hf[pl.ds(g, 1), :], (SUBS, SPAN))
+                for bit in (1, 2, 4):
+                    base = jnp.where((row & bit) != 0, pltpu.roll(base, bit, 1), base)
+                for pair in range(SPAN // (2 * SUBS)):
+                    above, below = [], []
+                    for k in (2 * pair, 2 * pair + 1):
+                        turned = pltpu.roll(base, SUBS * k, 1) if k else base
+                        under = row + SUBS * k > col
+                        above.append(jnp.where(under, turned, 0.0))
+                        below.append(jnp.where(under, 0.0, turned))
+                    at = 2 * SUBS * pair
+                    mats[g, at : at + 2 * SUBS] = jnp.concatenate(above, axis=0).astype(BF16)
+                    mats[g, SPAN + at : SPAN + at + 2 * SUBS] = jnp.concatenate(below, axis=0).astype(BF16)
             return carry
 
         lax.fori_loop(0, 16, body, 0)
@@ -202,7 +212,6 @@
     start_part(0)
     go(halo_copy)
     toeplitz()
-    near_arrives()
 
     def halo_arrives():
         halo_copy().wait_recv()
@@ -287,6 +296,12 @@
             for i, at in enumerate(spots):
                 for b in range(BLOCKS):
                     y2[0, at, SPAN * b : SPAN * (b + 1)] = found[BLOCKS * i + b]
+            happen(step, {
+                2: [(cross_ext_arrives,)],
+                3: [(part_arrives, 1, 2)],
+                4: [(part_arrives, 2, 1)],
+                5: [(part_arrives, 1, 3)],
+            })
             return carry
 
         lax.fori_loop(quarter * 2, quarter * 2 + 2, body, 0)
@@ -295,18 +310,22 @@
         at = pl.ds(pl.multiple_of(quarter * (WIDTH // 4), WIDTH // 4), WIDTH // 4)
         return remote(y2.at[0, at], y2.at[1, at], ys.at[quarter], yr.at[quarter], z_at(inner))
 
+    def pick(n, table):
+        found = -1
+        for at, value in table.items():
+            found = jnp.where(n == at, value, found)
+        return found
+
     def slot_of(job):
-        late = lax.div(job - 10, 2) + 4
-        return jnp.where(job >= 10, late, lax.rem(lax.rem(job, 5) + 7, RING))
+        return jnp.where(job < RING, job, pick(job - RING, {0: 0, 1: 3, 2: 4, 3: 7, 4: 1, 5: 5, 6: 6, 7: 2}))
 
     def tokens_of(job):
-        late = 1 - lax.rem(job, 2)
-        return jnp.where(job >= 10, late, jnp.where(job >= 5, 1, 0))
+        return lax.div(job, RING)
 
     def target_of(job):
         slot = slot_of(job)
-        off = (lax.div(slot, 2) + 1) * (1 - 2 * lax.rem(slot, 2))
-        return lax.rem(y + jnp.where(slot == OWN, 0, off) + RING, RING)
+        off = lax.div(slot + 1, 2) * (2 * lax.rem(slot, 2) - 1)
+        return lax.rem(y + off + RING, RING)
 
     def project(job, half):
         rows = w_all[slot_of(job), pl.ds(pl.multiple_of(half * HALF, HALF), HALF)]
@@ -353,8 +372,7 @@
         return remote(qp, rp, ps.at[0], ps.at[1], z_at(inner))
 
     ahead = lax.rem(c - y + RING, RING)
-    my_group = jnp.minimum(ahead, RING - ahead)
-    ready = jnp.where(my_group <= 1, 13, jnp.where(my_group == 2, 14, jnp.where(my_group == 3, 17, 18)))
+    ready = jnp.minimum(13 + pick(ahead, {0: 0, 2: 1, 6: 2, 4: 3, 1: 4, 3: 5, 5: 6, 7: 7}), 19)
 
     def finish():
         for half in range(2):
@@ -366,29 +384,33 @@
             swap_y(quarter).wait_recv()
 
     halo_arrives()
-    cross_arrives()
-
-    def feature_quarter(quarter, carry):
-        lax.fori_loop(quarter * 2, quarter * 2 + 2, lambda strip, carry: (features(strip), carry)[1], 0)
-        tail(quarter).start()
-        happen(quarter, {
-            0: [(part_arrives, 1, 0)],
-            1: [(cross_ext_arrives,), (part_arrives, 1, 1)],
-            2: [(part_arrives, 1, 2)],
-            3: [(part_arrives, 1, 3)],
-        })
+
+    def quarters(n, carry):
+        @pl.when(n < 4)
+        def feature_quarter():
+            def body(strip, carry):
+                features(strip)
+                happen(strip, {
+                    1: [(near_arrives,)],
+                    2: [(part_arrives, 1, 0)],
+                    4: [(cross_arrives,)],
+                    5: [(part_arrives, 1, 1)],
+                    7: [(part_arrives, 2, 0)],
+                })
+                return carry
+
+            lax.fori_loop(n * 2, n * 2 + 2, body, 0)
+            tail(n).start()
+
+        @pl.when(n >= 2)
+        def conv_quarter():
+            tail_arrives(n - 2)
+            conv(n - 2)
+            swap_y(n - 2).start()
+
         return carry
 
-    lax.fori_loop(0, 4, feature_quarter, 0)
-
-    def conv_quarter(quarter, carry):
-        tail_arrives(quarter)
-        conv(quarter)
-        swap_y(quarter).start()
-        happen(quarter, {2: [(part_arrives, 2, 0)], 3: [(part_arrives, 2, 1)]})
-        return carry
-
-    lax.fori_loop(0, 4, conv_quarter, 0)
+    lax.fori_loop(0, 6, quarters, 0)
     own.wait()
 
     def turn(n, carry):
@@ -401,18 +423,15 @@
             finish()
 
         happen(n, {
+            0: [(part_arrives, 2, 2)],
             1: [(settle, 1)],
-            2: [(part_arrives, 2, 2), (part_arrives, 2, 3)],
-            3: [(settle, 2)],
-            5: [(partner_y,), (part_arrives, 3, 0)],
-            6: [(part_arrives, 3, 1)],
-            7: [(part_arrives, 3, 2)],
-            8: [(part_arrives, 3, 3)],
-            10: [(settle, 3)],
-            11: [(part_arrives, 4, 0)],
-            12: [(part_arrives, 4, 1), (part_arrives, 4, 2)],
-            13: [(part_arrives, 4, 3)],
-            14: [(settle, 4)],
+            2: [(part_arrives, 2, 3), (part_arrives, 3, 0)],
+            3: [(settle, 2), (part_arrives, 3, 1)],
+            4: [(part_arrives, 3, 2)],
+            5: [(part_arrives, 3, 3), (part_arrives, 4, 0), (settle, 3)],
+            6: [(part_arrives, 4, 1), (part_arrives, 4, 2)],
+            7: [(part_arrives, 4, 3), (settle, 4)],
+            8: [(partner_y,)],
         })
 
         @pl.when(n < JOBS)
@@ -421,23 +440,19 @@
 
         return carry
 
-    lax.fori_loop(0, JOBS + 3, turn, 0)
+    lax.fori_loop(0, JOBS + 4, turn, 0)
 
     def place(z_from, rows):
         at = lax.rem(z + z_from + 2 * RING, RING) * (2 * PIECE)
-        fin[pl.ds(pl.multiple_of(at, 2 * PIECE), 2 * PIECE), :] = rows
+        out_ref[pl.ds(pl.multiple_of(at, 2 * PIECE), 2 * PIECE), :] = rows
 
     for half in range(2):
-        found = gathered(0, half)
+        found = gathered(0, half).astype(BF16)
         for i, z_from in enumerate(((0, outer + 4), (outer, 4))[half]):
             place(z_from, found[2 * PIECE * i : 2 * PIECE * (i + 1)])
     hand().wait_recv()
     for i, z_from in enumerate((inner, 2 * inner + 4, 2 * inner, inner + 4)):
-        place(z_from, rp[2 * PIECE * i : 2 * PIECE * (i + 1)].astype(F32))
-    for a in range(BLOCKS):
-        for n in range(4):
-            tile = fin[LANES * n : LANES * (n + 1), SPAN * a : SPAN * (a + 1)]
-            out_ref[SPAN * a : SPAN * (a + 1), LANES * n : LANES * (n + 1)] = tile.T.astype(BF16)
+        place(z_from, rp[2 * PIECE * i : 2 * PIECE * (i + 1)])
 
     for make, args in started:
         make(*args).wait_send()
@@ -463,14 +478,13 @@
 
 
 def local(qkv, feat_taps, long_filter, skip_gain, out_weight):
-    vmem = pl.BlockSpec(memory_space=pltpu.VMEM)
     anywhere = pl.BlockSpec(memory_space=pl.ANY)
     dma = pltpu.SemaphoreType.DMA
     return pl.pallas_call(
         kernel,
-        out_shape=jax.ShapeDtypeStruct((ROWS, 512), BF16),
+        out_shape=jax.ShapeDtypeStruct((512, ROWS), BF16),
         in_specs=[anywhere] * 5,
-        out_specs=vmem,
+        out_specs=pl.BlockSpec(memory_space=pltpu.VMEM),
         scratch_shapes=[
             pltpu.VMEM((3, FTAPS, WIDTH), F32),
             pltpu.VMEM((WIDTH // GROUP, SPAN), BF16),
@@ -493,7 +507,6 @@
             pltpu.VMEM((2, 4, 2, HALF, ROWS), BF16),
             pltpu.VMEM((2 * HALF, ROWS), BF16),
             pltpu.VMEM((2 * HALF, ROWS), BF16),
-            pltpu.VMEM((512, ROWS), F32),
             dma((6,)), dma, dma((2,)), dma((2, 4)),
             dma((2,)), dma((2, RING)), dma((2, RING)),
             dma((2, 4, 4)), dma((2, 4, 4)), dma((4,)), dma((4,)),
@@ -502,7 +515,7 @@
         compiler_params=pltpu.CompilerParams(
             collective_id=0, has_side_effects=True, vmem_limit_bytes=56 * 2**20
         ),
-    )(qkv, feat_taps, long_filter.T, skip_gain.reshape(1, WIDTH), out_weight.T)
+    )(qkv, feat_taps, long_filter.T, skip_gain.reshape(1, WIDTH), out_weight.T).T
 
 
 def solution(mesh):

time: 90.1 us -> 90.7 us (level)
  the two profiles are of different devices: /device:TPU:68 before, /device:TPU:7 now
where the time goes in v12:
time: 90.7 us; the launch traced here: 90.5 us
  Pallas kernels  88.5 us (98%)
  local copies, waits for them, and re-layouts  1.92 us (2%)
    pallas_call x1, Pallas kernels, local(): pl.pallas_call(kernel, out_shape=jax.ShapeDtypeStruct((512, ROWS), BF16),...  88.5 us
    transpose x1, local copies, waits for them, and re-layouts, local(): return pl.pallas_call(kernel, out_shape=jax.ShapeDtypeStruct((512, ROWS),...  1.92 us

profile of v12, /device:TPU:7, one launch (start us, length us, event | category | flops | bytes accessed | tf_op | source)
XLA Modules:
  0.0 90.5 jit_solution(13924409429943924568)
XLA Ops:
  0.0 88.5 %shard_map.55 = bf16[512,384]{1,0:T(8,128)(2,1)} custom-call(bf16[3,384,1024]{2,1,0:T(8,128)(2,1)} %qkv_ref.1, f32[3,7,1024]{2,1,0:T(8,128)} %taps_hbm.1, bf16[64,128]{1,0:T(8,128)(2,1)} %bitcast.6, f32[1,1024]{1,0:T(1,128)} %bitcast.7, bf16[64,1024]{1,0:T(8,128)(2,1)} %bitcast.5), custom_call_target="tpu_custom_call" | custom-call | tf_op jit(solution)/shard_map/pallas_call | solution.py:483
  88.6 1.9 %copy.6 = bf16[384,512]{1,0:T(8,128)(2,1)} copy(bf16[384,512]{0,1:T(8,128)(2,1)} %bitcast.4) | data formatting | bytes 786432 | tf_op jit(solution)/shard_map/transpose | solution.py:518

commit v13 on v11

--- a/solution.py
+++ b/solution.py
@@ -25,7 +25,7 @@
 OFF = (1, -1, 2, -2, 3, -3, 4, 0)
 SLOT = {off: slot for slot, off in enumerate(OFF)}
 PACKS = ((7, 8), (0, 2), (2, 4), (4, 6), (6, 7))
-FAR_UP = (0, 1, 4)
+FAR_UP = ((0, 4), (0,))
 OWN = SLOT[0]
 FAR = SLOT[4]
 PAIRS = 3
@@ -72,6 +72,12 @@
     def go(copy):
         copy.start()
         started.append(copy)
+
+    barrier = pltpu.get_barrier_semaphore()
+    greeted = [{"chan": lax.rem(c + d, 8)} for d in range(1, 8)]
+    greeted += [z_at(1), z_at(-1), y_at(1), y_at(-1), seq_at(1), seq_at(-1)]
+    for to in greeted:
+        pl.semaphore_signal(barrier, inc=1, device_id=to, device_id_type=MESH)
 
     loads = [
         pltpu.make_async_copy(qkv_ref.at[i], qkv_v.at[i], load_sem.at[i]) for i in (1, 2, 0)
@@ -90,11 +96,6 @@
     for copy in loads + own:
         copy.start()
 
-    barrier = pltpu.get_barrier_semaphore()
-    greeted = [{"chan": lax.rem(c + d, 8)} for d in range(1, 8)]
-    greeted += [z_at(1), z_at(-1), y_at(1), y_at(-1), seq_at(1), seq_at(-1)]
-    for to in greeted:
-        pl.semaphore_signal(barrier, inc=1, device_id=to, device_id_type=MESH)
     pl.semaphore_wait(barrier, len(greeted))
 
     def first(kind, direction, step):
@@ -124,10 +125,10 @@
         at = kind, lane, step - 1, pack
         return remote(src, dst, s2.at[at], r2.at[at], major_at[kind](direction))
 
-    def lanes_of(step, pack):
+    def lanes_of(kind, step, pack):
         if step < 4:
             return (1, -1)
-        return (1,) if pack in FAR_UP else (-1,)
+        return (1,) if pack in FAR_UP[kind] else (-1,)
 
     def first_arrives(step):
         for kind in range(2):
@@ -141,9 +142,9 @@
 
     def second_arrives(step, pack):
         for kind in range(2):
-            for direction in lanes_of(step, pack):
+            for direction in lanes_of(kind, step, pack):
                 second(kind, direction, step, pack).wait_recv()
-                if step < 4 and direction in lanes_of(step + 1, pack):
+                if step < 4 and direction in lanes_of(kind, step + 1, pack):
                     go(second(kind, direction, step + 1, pack))
 
     events = [(2.2 * k, first_arrives, (k,)) for k in range(1, 5)]
@@ -178,13 +179,13 @@
     halo_copy = remote(
         qkv_ref.at[:, ROWS - HALO : ROWS], halo, halo_sem.at[0], halo_sem.at[1], seq_at(1)
     )
-    go(halo_copy)
     for kind in range(2):
         for direction in (1, -1):
             go(first(kind, direction, 1))
     for kind in range(2):
         for direction in (1, -1):
             go(second(kind, direction, 1, 0))
+    go(halo_copy)
 
     def widen(strip):
         at = pl.ds(pl.multiple_of(strip * LANES, LANES), LANES)

time: 84.5 us -> 83.1 us (0.983)
  Pallas kernels: 82.4 us -> 81 us
    pallas_call x1, Pallas kernels: 82.4 us -> 81 us  [local(): pl.pallas_call(kernel, out_shape=jax.ShapeDtypeStruct((512, ROWS), BF16),...]
where the time goes in v13:
time: 83.1 us; the launch traced here: 82.9 us
  Pallas kernels  81 us (97%)
  local copies, waits for them, and re-layouts  1.92 us (2%)
    pallas_call x1, Pallas kernels, local(): pl.pallas_call(kernel, out_shape=jax.ShapeDtypeStruct((512, ROWS), BF16),...  81 us
    transpose x1, local copies, waits for them, and re-layouts, local(): return pl.pallas_call(kernel, out_shape=jax.ShapeDtypeStruct((512, ROWS),...  1.92 us

profile of v13, /device:TPU:4, one launch (start us, length us, event | category | flops | bytes accessed | tf_op | source)
XLA Modules:
  0.0 82.9 jit_solution(8854385655820346165)
XLA Ops:
  0.0 81.0 %shard_map.55 = bf16[512,384]{1,0:T(8,128)(2,1)} custom-call(bf16[3,384,1024]{2,1,0:T(8,128)(2,1)} %qkv_ref.1, f32[3,7,1024]{2,1,0:T(8,128)} %taps_hbm.1, bf16[64,128]{1,0:T(8,128)(2,1)} %bitcast.6, f32[1,1024]{1,0:T(1,128)} %bitcast.7, bf16[64,1024]{1,0:T(8,128)(2,1)} %bitcast.5), custom_call_target="tpu_custom_call" | custom-call | tf_op jit(solution)/shard_map/pallas_call | solution.py:450
  81.0 1.9 %copy.6 = bf16[384,512]{1,0:T(8,128)(2,1)} copy(bf16[384,512]{0,1:T(8,128)(2,1)} %bitcast.4) | data formatting | bytes 786432 | tf_op jit(solution)/shard_map/transpose | solution.py:483

commit v14 on v13

--- a/solution.py
+++ b/solution.py
@@ -149,7 +149,7 @@
 
     events = [(2.2 * k, first_arrives, (k,)) for k in range(1, 5)]
     events += [
-        (2.6 + 10.5 * (k - 1) + 2.4 * g, second_arrives, (k, g)) for k in range(1, 5) for g in range(5)
+        (2.6 + 10.5 * (k - 1) + 2.4 * g, second_arrives, (k, g)) for k in range(1, 4) for g in range(5)
     ]
     events.sort(key=lambda e: e[0])
     events = [(at, fn, args) for at, fn, args in events]
@@ -299,8 +299,8 @@
 
         delivered.append((to, copy))
 
-    STARTS = (0, 256, 768, 1280, 1792, 1920)
-    COUNTS = (256, 512, 512, 512, 128, 128)
+    STARTS = (0, 256, 768, 1280, 1792, 1856, 1920, 1984)
+    COUNTS = (256, 512, 512, 512, 64, 64, 64, 64)
 
     def b_rows(turn, half):
         return w_all[1, 2 * turn + half].reshape(RING * PIECE, WIDTH)
@@ -311,7 +311,7 @@
         if bundle < 4:
             low = 2 * (bundle - 1)
             return four(0, low, half) + four(0, low + 1, half) + [b_rows(bundle - 1, half)]
-        return [two(kind, FAR, bundle - 4, half) for kind in range(2)]
+        return [two(bundle % 2, FAR, bundle // 2 - 2, half)]
 
     def rows_of(bundle):
         return slice(STARTS[bundle], STARTS[bundle] + COUNTS[bundle])
@@ -359,9 +359,10 @@
                     qa.at[from_row : from_row + PIECE], rb.at[turn, x, p],
                     bs2.at[turn, m], br2.at[turn, x, p], target(m),
                 )
+        elif bundle % 2 == 0:
+            post_row(FAR, start, 2 * PIECE, bundle // 2 - 2)
         else:
-            post_row(FAR, start, 2 * PIECE, bundle - 4)
-            post_single(1, bundle - 4, start + 2 * PIECE)
+            post_single(1, bundle // 2 - 2, start)
 
     def own_wait():
         for copy in own:
@@ -420,16 +421,24 @@
         need(k)
         work(1.8, give, k)
         work(2.2, take, k)
-    while not {(4, g) for g in (0, 1, 2)} <= seen:
-        take_event()
-    give(4)
+    def farthest(kind, packs):
+        for pack in packs:
+            for direction in lanes_of(kind, 4, pack):
+                second(kind, direction, 4, pack).wait_recv()
+
+    for kind in range(2):
+        farthest(kind, (1, 2))
+        give(4 + kind)
     take(4)
-    need(4)
-    give(5)
+    take(5)
+    for kind in range(2):
+        farthest(kind, (0, 3, 4))
+        give(6 + kind)
     pair_sums(0)
+    take(6)
     pair_sums(1)
+    take(7)
     single_sums(0, OWN)
-    take(5)
     pair_sums(2)
     single_sums(1, FAR)
     row_sums()
@@ -474,7 +483,7 @@
             dma((6,)), dma((2,)), dma((2,)), dma((2,)),
             dma((2, 2, 4)), dma((2, 2, 4)),
             dma((2, 2, 4, 5)), dma((2, 2, 4, 5)),
-            dma((6,)), dma((6,)), dma((RING, 2)), dma((4, 2)),
+            dma((8,)), dma((8,)), dma((RING, 2)), dma((4, 2)),
             dma((PAIRS, RING)), dma((PAIRS, 4, 2)), dma((2, 2, 2)), dma((2, 4)),
         ],
         compiler_params=pltpu.CompilerParams(

time: 83.1 us -> 83.1 us (level)
  no operation moved by 1% of the time
where the time goes in v14:
time: 83.1 us; the launch traced here: 83 us
  Pallas kernels  81 us (97%)
  local copies, waits for them, and re-layouts  1.92 us (2%)
    pallas_call x1, Pallas kernels, local(): pl.pallas_call(kernel, out_shape=jax.ShapeDtypeStruct((512, ROWS), BF16),...  81 us
    transpose x1, local copies, waits for them, and re-layouts, local(): return pl.pallas_call(kernel, out_shape=jax.ShapeDtypeStruct((512, ROWS),...  1.92 us

profile of v14, /device:TPU:4, one launch (start us, length us, event | category | flops | bytes accessed | tf_op | source)
XLA Modules:
  0.0 83.0 jit_solution(467859814139688849)
XLA Ops:
  0.0 81.0 %shard_map.55 = bf16[512,384]{1,0:T(8,128)(2,1)} custom-call(bf16[3,384,1024]{2,1,0:T(8,128)(2,1)} %qkv_ref.1, f32[3,7,1024]{2,1,0:T(8,128)} %taps_hbm.1, bf16[64,128]{1,0:T(8,128)(2,1)} %bitcast.6, f32[1,1024]{1,0:T(1,128)} %bitcast.7, bf16[64,1024]{1,0:T(8,128)(2,1)} %bitcast.5), custom_call_target="tpu_custom_call" | custom-call | tf_op jit(solution)/shard_map/pallas_call | solution.py:459
  81.0 1.9 %copy.6 = bf16[384,512]{1,0:T(8,128)(2,1)} copy(bf16[384,512]{0,1:T(8,128)(2,1)} %bitcast.4) | data formatting | bytes 786432 | tf_op jit(solution)/shard_map/transpose | solution.py:492

commit v15 on v13

--- a/solution.py
+++ b/solution.py
@@ -147,7 +147,7 @@
                 if step < 4 and direction in lanes_of(kind, step + 1, pack):
                     go(second(kind, direction, step + 1, pack))
 
-    events = [(2.2 * k, first_arrives, (k,)) for k in range(1, 5)]
+    events = [(at, first_arrives, (k,)) for k, at in enumerate((0.9, 3.5, 5.0, 6.6), 1)]
     events += [
         (2.6 + 10.5 * (k - 1) + 2.4 * g, second_arrives, (k, g)) for k in range(1, 5) for g in range(5)
     ]
@@ -185,7 +185,6 @@
     for kind in range(2):
         for direction in (1, -1):
             go(second(kind, direction, 1, 0))
-    go(halo_copy)
 
     def widen(strip):
         at = pl.ds(pl.multiple_of(strip * LANES, LANES), LANES)
@@ -402,6 +401,8 @@
                 place(0, slot, found[PIECE * i : PIECE * (i + 1)])
 
     work(1.0, widen_all)
+    take_event()
+    go(halo_copy)
     for lo in (0, 4):
         work(1.4, features, BLOCKS - 1, (lo, lo + 4))
     work(0.1, send_tail)

time: 83.1 us -> 83 us (level)
  no operation moved by 1% of the time
where the time goes in v15:
time: 83 us; the launch traced here: 82.8 us
  Pallas kernels  80.9 us (97%)
  local copies, waits for them, and re-layouts  1.92 us (2%)
    pallas_call x1, Pallas kernels, local(): pl.pallas_call(kernel, out_shape=jax.ShapeDtypeStruct((512, ROWS), BF16),...  80.9 us
    transpose x1, local copies, waits for them, and re-layouts, local(): return pl.pallas_call(kernel, out_shape=jax.ShapeDtypeStruct((512, ROWS),...  1.92 us

profile of v15, /device:TPU:4, one launch (start us, length us, event | category | flops | bytes accessed | tf_op | source)
XLA Modules:
  0.0 82.8 jit_solution(9478119166353888316)
XLA Ops:
  0.0 80.9 %shard_map.55 = bf16[512,384]{1,0:T(8,128)(2,1)} custom-call(bf16[3,384,1024]{2,1,0:T(8,128)(2,1)} %qkv_ref.1, f32[3,7,1024]{2,1,0:T(8,128)} %taps_hbm.1, bf16[64,128]{1,0:T(8,128)(2,1)} %bitcast.6, f32[1,1024]{1,0:T(1,128)} %bitcast.7, bf16[64,1024]{1,0:T(8,128)(2,1)} %bitcast.5), custom_call_target="tpu_custom_call" | custom-call | tf_op jit(solution)/shard_map/pallas_call | solution.py:451
  80.9 1.9 %copy.6 = bf16[384,512]{1,0:T(8,128)(2,1)} copy(bf16[384,512]{0,1:T(8,128)(2,1)} %bitcast.4) | data formatting | bytes 786432 | tf_op jit(solution)/shard_map/transpose | solution.py:484
